TPU v7x, 512 devices: a whole 4x8x8 slice. The times are simulated.
512 devices in a mesh: seq: 128 (over z, x, y_hi), hap: 4 (over y_lo, core).
Axes of the slice: x: 4, y: 8 (y_hi: 4, y_lo: 2; y = y_hi * 2 + y_lo), z: 8, core: 2. Of those that a mesh axis runs over, the one named last changes fastest.
Arguments:
- tokens: bfloat16 [4, 16384, 512], P('hap', 'seq'), may hold values from -24 to 24
- cotangent: bfloat16 [4, 16384, 512], P('hap', 'seq'), may hold values from -6 to 6
- gaps: int32 [128, 2], P('seq'), may hold values from 0 to 128, as said below
- conv_taps: float32 [2, 3, 512], replicated, may hold values from -3.5 to 3.5
- norm_gains: float32 [2, 512], replicated, may hold values from 0.25 to 1.75
- projection: bfloat16 [2, 512, 1024], replicated, may hold values from -0.25 to 0.25
Outputs:
- tokens_grad: bfloat16 [4, 16384, 512], P('hap', 'seq')
- projection_grad: float32 [2, 512, 1024], P(None, 'seq')
- taps_grad: float32 [2, 3, 512], replicated
- gains_grad: float32 [2, 512], replicated
Inputs may be any that keep to these rules, and one draw needn't show every extreme that they name: `gaps`: each row holds a start and an end with start <= end; some run is wholly a gap and some has none; gap density varies from region to region.
All inputs are finite; a program needn't handle non-finite values.
Results may differ from a plain program's by a relative error of at most 0.0058.
Values may be sent and summed in bfloat16 or wider, within the bound.
No kernel may reach another device: no remote copies, remote signals or barrier semaphores. Data moves between devices by JAX's collectives and lax.ppermute only.
A program may use at most 64 MiB of HBM per device.

v0:
```python
import jax
import jax.numpy as jnp
from jax import lax
from jax.sharding import PartitionSpec as P

DILATION_BINS = 32
LAYERS = 2


EPS = 1e-06


def extended(x, sides, width):
    for axis, dim in sides:
        devices, length = (lax.axis_size(axis), x.shape[dim])
        up = [(i, (i + 1) % devices) for i in range(devices - 1)]
        down = [(j, i) for i, j in up]
        last = lax.slice_in_dim(x, length - width, length, axis=dim)
        initial = lax.slice_in_dim(x, 0, width, axis=dim)
        before = lax.ppermute(last, axis, up)
        after = lax.ppermute(initial, axis, down)
        x = jnp.concatenate([before, x, after], axis=dim)
    return x


def valid_of(gap_rows):
    offsets = jnp.arange(128, dtype=jnp.int32)[None, :]
    inside = (offsets >= gap_rows[:, 0:1]) & (offsets < gap_rows[:, 1:2])
    return jnp.where(inside, 0.0, 1.0).astype(jnp.float32).reshape(-1)


def norm_part(inputs, valid, gain):
    scaled = inputs.astype(jnp.float32)
    inv_rms = lax.rsqrt(jnp.mean(scaled * scaled, axis=-1, keepdims=True) + EPS)
    return (scaled, inv_rms, scaled * inv_rms * gain * valid[:, None])


def project(preactivation, weight):
    hidden = jax.nn.gelu(preactivation).astype(jnp.bfloat16)
    proj_out = jnp.dot(hidden, weight, preferred_element_type=jnp.float32)
    halfway = weight.shape[1] // 2
    return (hidden, proj_out[:, :halfway], jax.nn.sigmoid(proj_out[:, halfway:]))


def convolve(filter_weight, padded_tracks, receptive_extent):
    return (
        filter_weight[0] * padded_tracks[0:receptive_extent]
        + filter_weight[1] * padded_tracks[DILATION_BINS : DILATION_BINS + receptive_extent]
        + filter_weight[2] * padded_tracks[2 * DILATION_BINS : 2 * DILATION_BINS + receptive_extent]
    )


def back_layer(grad, stored, valid, filter_weight, gain, weight):
    scaled, inv_rms, normalized_tracks, padded_tracks, preactivation, hidden, first, gate = stored
    local_bin_count = grad.shape[0]
    branch = valid[:, None] * grad
    dproj = jnp.concatenate([branch * gate, branch * first * gate * (1.0 - gate)], 1).astype(
        jnp.bfloat16
    )
    dhidden = lax.dot_general(
        dproj, weight, (((1,), (1,)), ((), ())), preferred_element_type=jnp.float32
    )
    proj_term = lax.dot_general(
        hidden, dproj, (((0,), (0,)), ((), ())), preferred_element_type=jnp.float32
    )
    preactivation_gradient = jax.vjp(jax.nn.gelu, preactivation)[1](dhidden)[0]
    wide_preactivation_gradient = extended(preactivation_gradient, (("seq", 0),), DILATION_BINS)
    normalized_gradient = (
        filter_weight[0] * wide_preactivation_gradient[2 * DILATION_BINS :]
        + filter_weight[1] * preactivation_gradient
        + filter_weight[2] * wide_preactivation_gradient[:local_bin_count]
    )
    tap_term = jnp.stack(
        [
            jnp.sum(preactivation_gradient * padded_tracks[:local_bin_count], 0),
            jnp.sum(preactivation_gradient * normalized_tracks, 0),
            jnp.sum(preactivation_gradient * padded_tracks[2 * DILATION_BINS :], 0),
        ]
    )
    dq = normalized_gradient * valid[:, None]
    gain_term = jnp.sum(dq * scaled * inv_rms, 0)
    dt = dq * gain
    grad = grad + inv_rms * dt - scaled * inv_rms**3 * jnp.mean(dt * scaled, axis=-1, keepdims=True)
    return (grad, proj_term, tap_term, gain_term)


def shards(tokens, cotangent, gaps, conv_taps, norm_gains, projection):
    features = tokens[0]
    local_bin_count = features.shape[0]
    valid = valid_of(gaps)
    stored_all = []
    current = features
    for layer in range(LAYERS):
        scaled, inv_rms, normalized_tracks = norm_part(current, valid, norm_gains[layer])
        padded_tracks = extended(normalized_tracks, (("seq", 0),), DILATION_BINS)
        preactivation = convolve(conv_taps[layer], padded_tracks, local_bin_count)
        hidden, first, gate = project(preactivation, projection[layer])
        current = (scaled + valid[:, None] * first * gate).astype(jnp.bfloat16)
        stored_all.append(
            (scaled, inv_rms, normalized_tracks, padded_tracks, preactivation, hidden, first, gate)
        )
    grad = cotangent[0].astype(jnp.float32)
    proj_terms = [None] * LAYERS
    filter_tap_products = [None] * LAYERS
    gain_terms = [None] * LAYERS
    for layer in reversed(range(LAYERS)):
        grad, proj_term, filter_tap_products[layer], gain_terms[layer] = back_layer(
            grad, stored_all[layer], valid, conv_taps[layer], norm_gains[layer], projection[layer]
        )
        proj_terms[layer] = proj_term
    stacked = jnp.stack(proj_terms)
    shared = lax.psum_scatter(stacked, "seq", scatter_dimension=1, tiled=True)
    projection_grad = lax.psum(shared, "hap")
    taps_grad, gains_grad = lax.psum(
        (jnp.stack(filter_tap_products), jnp.stack(gain_terms)), ("seq", "hap")
    )
    return (grad.astype(jnp.bfloat16)[None], projection_grad, taps_grad, gains_grad)


def solution(mesh):
    return jax.shard_map(
        shards,
        mesh=mesh,
        in_specs=(P("hap", "seq", None), P("hap", "seq", None), P("seq", None), P(), P(), P()),
        out_specs=(P("hap", "seq", None), P(None, "seq", None), P(), P()),
        check_vma=False,
    )
```

profile of v0, /device:TPU:1, one launch (start us, length us, event | category | flops | bytes accessed | tf_op | source)
XLA Modules:
  0.0 1558.2 jit_solution(6021974988914970784)
XLA Ops:
  7.2 1.0 fusion.38
  8.3 1.3 fusion.81
  9.6 0.8 fusion.80
  10.4 1.3 multiply_multiply_fusion.4
  11.7 1.0 fusion.40
  12.7 1.4 collective-permute-start.1
  14.1 5.7 collective-permute-start
  19.8 0.8 fusion.79
  20.6 0.5 collective-permute-done
  21.1 1.6 fusion.6
  23.2 1.3 collective-permute-start.3
  24.5 6.7 collective-permute-start.2
  31.1 0.4 collective-permute-done.3
  31.6 0.9 collective-permute-done.2
  33.0 0.6 fusion.30
  33.6 6.4 collective-permute-start.5
  40.0 1.3 collective-permute-start.4
  41.3 0.5 convolution_bitcast_fusion
  41.8 5.9 collective-permute-done.4
  48.4 0.5 convolution_bitcast_fusion.1
  48.9 2.3 pad_maximum_fusion
  51.2 1.3 dynamic-slice
  53.1 0.6 fusion.24
  53.7 5.5 collective-permute-start.7
  59.3 1.3 collective-permute-start.6
  60.6 4.8 collective-permute-done.6
  65.7 126.8 %all-reduce.1 = (f32[2,3,512]{2,1,0:T(4,128)S(1)}, f32[2,512]{1,0:T(2,128)}) all-reduce(f32[2,3,512]{2,1,0:T(4,128)S(1)} %pad_maximum_fusion.15, f32[2,512]{1,0:T(2,128)S(1)} %pad_maximum_fusion.16), channel_id=1, replica_groups=mesh['seq'=128,'hap'=4] {'seq','hap'}, use_global_device_ids=true, to_apply=%region_12.13 | all-reduce | flops 4096 | bytes 32768 | tf_op jit(solution)/shard_map/psum | solution.py:114
  192.5 0.6 copy.11
  193.1 0.8 fusion.68
  193.9 1254.7 %all-reduce.4.cloned.1.call-done = f32[2,512,1024]{2,1,0:T(8,128)} async-done(((f32[2,512,1024]{2,1,0:T(8,128)}), f32[2,512,1024]{2,1,0:T(8,128)}) %all-reduce.4.cloned.1.call-update) | async-done | bytes 4194320
  1448.6 0.8 constant_dynamic-slice_fusion
  1449.4 101.9 %psum.21 = f32[2,4,1024]{2,1,0:T(4,128)} all-reduce(f32[2,4,1024]{2,1,0:T(4,128)S(1)} %constant_dynamic-slice_fusion), channel_id=1, replica_groups=mesh['seq'=128,'hap'=4] {'hap'}, use_global_device_ids=true, to_apply=%region_5.6 | all-reduce | flops 8192 | bytes 65536 | tf_op jit(solution)/shard_map/psum | solution.py:113
  (30 shorter events, 2.0 us)
Async XLA Ops:
  7.2 15.6 %copy-start = (bf16[1,128,512]{2,1,0:T(8,128)(2,1)S(1)}, bf16[1,128,512]{2,1,0:T(8,128)(2,1)}, u32[]{:S(2)}) copy-start(bf16[1,128,512]{2,1,0:T(8,128)(2,1)} %param.6) | copy-start | bytes 393220
  7.2 1441.4 %all-reduce.4.cloned.1.call-start = ((), (), s32[]{:S(2)}) async-start(), calls=%async_computation | async-start | bytes 8388608
  12.7 19.8 %copy-start.2 = (bf16[2,512,1024]{2,1,0:T(8,128)(2,1)S(1)}, bf16[2,512,1024]{2,1,0:T(8,128)(2,1)}, u32[]{:S(2)}) copy-start(bf16[2,512,1024]{2,1,0:T(8,128)(2,1)} %param.11) | copy-start | bytes 6291460
  12.7 7.9 collective-permute-start.1
  14.1 7.0 collective-permute-start
  22.8 10.1 copy-start.1
  23.2 8.4 collective-permute-start.3
  24.5 8.0 collective-permute-start.2
  33.6 8.2 collective-permute-start.5
  40.0 7.7 collective-permute-start.4
  53.7 6.9 collective-permute-start.7
  59.3 6.1 collective-permute-start.6
Sparse Core Ops, SparseCore 0:
  51.3 1397.2 all-reduce.3
where the time goes:
time: 1560 us
  waiting for transfers between devices  1270 us (81%)
  blocking collectives  229 us (15%)
  starting transfers between devices  29.6 us (2%)
    unnamed x2, waiting for transfers between devices  1250 us
    psum x1, blocking collectives, shards(): lax.psum((jnp.stack(filter_tap_products), jnp.stack(gain_terms)), ('seq',...  127 us
    psum x1, blocking collectives, shards(): projection_grad = lax.psum(shared, 'hap')  102 us
  transfers between devices with their start and end apart: 9, of which 6 were waited for; matrix products, arithmetic and copies ran while one was open for 0% of the time, Pallas kernels for 0%

commit v1 on v0

v1 whole, which is shorter than its diff:
```python
import jax
import jax.numpy as jnp
from jax import lax
from jax.experimental import pallas as pl
from jax.experimental.pallas import tpu as pltpu
from jax.sharding import Mesh
from jax.sharding import PartitionSpec as P

C = 512
DIL = 32
EPS = 1e-06
F32 = jnp.float32
BF16 = jnp.bfloat16
NEAR = ("zl", "xl", "yl")
FAR = ("zh", "xh", "yh")
SEQ = ("zh", "zl", "xh", "xl", "yh")
HAP = ("yl", "c")
G0 = 0.7978845608028654
G1 = 0.044715
PACK = 208
ACT = 144


def gelu_and_slope(x):
    x2 = x * x
    t = jnp.tanh(G0 * x * (1.0 + G1 * x2))
    cdf = 0.5 + 0.5 * t
    slope = cdf + (0.5 * G0) * x * (1.0 - t * t) * (1.0 + (3.0 * G1) * x2)
    return x * cdf, slope


def sigmoid(x):
    return 0.5 + 0.5 * jnp.tanh(0.5 * x)


def dot(a, b, dims):
    return lax.dot_general(a, b, (dims, ((), ())), preferred_element_type=F32)


def fold8(v):
    return jnp.sum(v.reshape(v.shape[0] // 8, 8, v.shape[1]), axis=0)


def hi_lo(v):
    hi = v.astype(BF16)
    lo = (v - hi.astype(F32)).astype(BF16)
    return hi, lo


def body(prev, nxt, tok, cot, own_gap, taps, gains, proj, out, keep, send,
         n0, i0, g0, h0, ab0, x1, n1, i1, g1, h1, po1, dp1, dh1, gr1, dp0, dh0, act):
    core = lax.axis_index("c")
    steps = lax.broadcasted_iota(jnp.int32, (DIL, 1), 0).astype(F32)

    gap_of = []
    for tile in (prev[192:208, :], own_gap[...], nxt[192:208, :]):
        tile = tile.astype(F32)
        gap_of.append((tile[0:1, 0:1], 128.0 - tile[1:2, 0:1]))

    def rows(base, count=DIL):
        ref, at = ((prev, base), (tok, base - 128), (nxt, base - 256))[base // 128]
        return ref[at:at + count, :].astype(F32)

    def cot_rows(base):
        if base < 128:
            return prev[128 + base - 64:128 + base - 32, :].astype(F32)
        if base < 256:
            return cot[base - 128:base - 96, :].astype(F32)
        return nxt[128 + base - 256:128 + base - 224, :].astype(F32)

    valid_of = []
    for chunk in range(12):
        start, end = gap_of[chunk // 4]
        at = steps + float(DIL * (chunk % 4))
        valid_of.append(jnp.where((at >= start) & (at < end), 0.0, 1.0))

    def norm(v, valid, gain):
        inv = lax.rsqrt(jnp.sum(v * v, axis=-1, keepdims=True) * (1.0 / C) + EPS)
        return inv, v * inv * gain * valid

    def tap(layer, k):
        return taps[layer, k:k + 1, :]

    def conv(ref, at, layer):
        return (tap(layer, 0) * ref[at - DIL:at, :] + tap(layer, 1) * ref[at:at + DIL, :]
                + tap(layer, 2) * ref[at + DIL:at + 2 * DIL, :])

    for c in range(12):
        inv, normed = norm(rows(c * DIL), valid_of[c], gains[0:1, :])
        i0[c * DIL:(c + 1) * DIL, :] = inv
        n0[c * DIL:(c + 1) * DIL, :] = normed
    for c in range(1, 11):
        hid, slope = gelu_and_slope(conv(n0, c * DIL, 0))
        h0[(c - 1) * DIL:c * DIL, :] = hid.astype(BF16)
        g0[(c - 1) * DIL:c * DIL, :] = slope
    ab0[...] = dot(h0[...], proj[0], ((1,), (0,)))
    for c in range(1, 11):
        at = slice((c - 1) * DIL, c * DIL)
        first = ab0[at, 0:C]
        gate = sigmoid(ab0[at, C:2 * C])
        both = first * gate
        nx = (rows(c * DIL) + valid_of[c] * both).astype(BF16).astype(F32)
        ab0[at, 0:C] = gate
        ab0[at, C:2 * C] = both * (1.0 - gate)
        inv, normed = norm(nx, valid_of[c], gains[1:2, :])
        x1[at, :] = nx
        i1[at, :] = inv
        n1[at, :] = normed
    for c in range(2, 10):
        hid, slope = gelu_and_slope(conv(n1, (c - 1) * DIL, 1))
        h1[(c - 2) * DIL:(c - 1) * DIL, :] = hid.astype(BF16)
        g1[(c - 2) * DIL:(c - 1) * DIL, :] = slope
    po1[...] = dot(h1[...], proj[1], ((1,), (0,)))
    for c in range(2, 10):
        at = slice((c - 2) * DIL, (c - 1) * DIL)
        first = po1[at, 0:C]
        gate = sigmoid(po1[at, C:2 * C])
        bg = valid_of[c] * cot_rows(c * DIL) * gate
        dp1[at, 0:C] = bg.astype(BF16)
        dp1[at, C:2 * C] = (bg * first * (1.0 - gate)).astype(BF16)
    dh1[...] = dot(dp1[...], proj[1], ((1,), (1,)))
    for c in range(8):
        at = slice(c * DIL, (c + 1) * DIL)
        dh1[at, :] = dh1[at, :] * g1[at, :]

    def back(dref, c_off, layer, c, sref_rows, inv, valid, gain):
        at = c_off
        dn = (tap(layer, 0) * dref[at + DIL:at + 2 * DIL, :] + tap(layer, 1) * dref[at:at + DIL, :]
              + tap(layer, 2) * dref[at - DIL:at, :])
        dq = dn * valid
        si = sref_rows * inv
        qs = dq * si
        dt = dq * gain
        m = jnp.sum(qs * gain, axis=-1, keepdims=True) * (1.0 / C)
        return inv * (dt - si * m), qs

    def small_rows(parts):
        return [jnp.sum(p, axis=0, keepdims=True) for p in parts]

    acc = [jnp.zeros((8, C), F32) for _ in range(4)]
    for c in range(3, 9):
        at1 = slice((c - 1) * DIL, c * DIL)
        delta, qs = back(dh1, (c - 2) * DIL, 1, c, x1[at1, :], i1[at1, :], valid_of[c], gains[1:2, :])
        grad = cot_rows(c * DIL) + delta
        branch = valid_of[c] * grad
        to = slice((c - 3) * DIL, (c - 2) * DIL)
        dp0[to, 0:C] = (branch * ab0[at1, 0:C]).astype(BF16)
        dp0[to, C:2 * C] = (branch * ab0[at1, C:2 * C]).astype(BF16)
        if 4 <= c < 8:
            gr1[(c - 4) * DIL:(c - 3) * DIL, :] = grad
            d = dh1[(c - 2) * DIL:(c - 1) * DIL, :]
            for k in range(3):
                acc[k] += fold8(d * n1[(c - 2 + k) * DIL:(c - 1 + k) * DIL, :])
            acc[3] += fold8(qs)

    def put(layer, hid, dpr, parts):
        act[layer, 0:128, 0:C] = hid
        act[layer, 0:128, C:3 * C] = dpr
        four = jnp.concatenate(small_rows(parts) + [jnp.zeros((12, C), F32)], axis=0)
        hi, lo = hi_lo(four)
        act[layer, 128:ACT, 0:C] = hi
        act[layer, 128:ACT, C:2 * C] = lo
        act[layer, 128:ACT, 2 * C:3 * C] = jnp.zeros((16, C), BF16)

    put(1, h1[64:192, :], dp1[64:192, :], acc)

    dh0[...] = dot(dp0[...], proj[0], ((1,), (1,)))
    for c in range(6):
        at = slice(c * DIL, (c + 1) * DIL)
        dh0[at, :] = dh0[at, :] * g0[(c + 2) * DIL:(c + 3) * DIL, :]
    acc = [jnp.zeros((8, C), F32) for _ in range(4)]
    for c in range(4, 8):
        delta, qs = back(dh0, (c - 3) * DIL, 0, c, rows(c * DIL), i0[c * DIL:(c + 1) * DIL, :],
                         valid_of[c], gains[0:1, :])
        at = slice((c - 4) * DIL, (c - 3) * DIL)
        out[at, :] = (gr1[at, :] + delta).astype(BF16)
        d = dh0[(c - 3) * DIL:(c - 2) * DIL, :]
        for k in range(3):
            acc[k] += fold8(d * n0[(c - 1 + k) * DIL:(c + k) * DIL, :])
        acc[3] += fold8(qs)
    put(0, h0[96:224, :], dp0[32:160, :], acc)
    keep[...] = act[core]
    send[...] = act[1 - core]


def terms(keep, recv, out):
    q = lax.broadcasted_iota(jnp.int32, (C, 1), 0)
    ch = (((q >> 4) & 3) << 7 | ((q >> 8) & 1) << 6 | ((q >> 3) & 1) << 5 | ((q >> 7) & 1) << 4
          | ((q >> 1) & 3) << 2 | ((q >> 6) & 1) << 1 | (q & 1))
    pick = (ch == lax.broadcasted_iota(jnp.int32, (C, C), 1)).astype(F32).astype(BF16)
    ha = dot(pick, keep[0:128, 0:C], ((1,), (1,))).astype(BF16)
    hb = dot(pick, recv[0:128, 0:C], ((1,), (1,))).astype(BF16)
    for j in range(8):
        cols = slice(C + j * 128, C + (j + 1) * 128)
        t = dot(ha, keep[0:128, cols], ((1,), (0,))) + dot(hb, recv[0:128, cols], ((1,), (0,)))
        out[:, j * 64:(j + 1) * 64, :] = t.astype(BF16).reshape(8, 64, 128)
    small = (keep[128:ACT, 0:C].astype(F32) + keep[128:ACT, C:2 * C].astype(F32)
             + recv[128:ACT, 0:C].astype(F32) + recv[128:ACT, C:2 * C].astype(F32))
    pad = jnp.zeros((12, 128), F32)
    for g in range(8):
        row, half = g // 2, (g % 2) * 256
        two = jnp.concatenate([small[row:row + 1, half + 128 * m:half + 128 * (m + 1)] for m in range(2)], axis=0)
        hi = two.astype(BF16).astype(F32)
        out[g, 512:528, :] = jnp.concatenate([hi, two - hi, pad], axis=0).astype(BF16)


def first_sum(recv, out):
    total = recv[0].astype(F32)
    for i in range(1, 8):
        total += recv[i].astype(F32)
    p = lax.broadcasted_iota(jnp.int32, (C, 1), 0)
    src = ((p >> 1) & 7) << 6 | (p >> 4) << 1 | (p & 1)
    pick = (src == lax.broadcasted_iota(jnp.int32, (C, C), 1)).astype(F32).astype(BF16)
    moved = dot(pick, total[0:512, :].astype(BF16), ((1,), (0,))).astype(BF16)
    out[:, 0:16, :] = moved.reshape(32, 16, 128)
    two = total[512:514, :] + total[514:516, :]
    hi = two.astype(BF16).astype(F32)
    tile = jnp.concatenate([hi, two - hi, jnp.zeros((12, 128), F32)], axis=0).astype(BF16)
    for d in range(32):
        out[d, 16:32, :] = tile


def second_sum(recv, out):
    total = recv[0].astype(F32)
    for i in range(1, 32):
        total += recv[i].astype(F32)
    two = total[16:18, :] + total[18:20, :]
    both = jnp.concatenate([total[0:16, :], two, jnp.zeros((6, 128), F32)], axis=0)
    for i in range(16):
        out[i] = both


def place(recv, proj, taps, gains):
    base = (lax.axis_index("zl") * 2 + lax.axis_index("xl")) * 4
    for c in range(2):
        for y in range(2):
            piece = recv[base + y * 2 + c]
            for j in range(8):
                proj[c, 2 * y:2 * y + 2, j * 128:(j + 1) * 128] = piece[2 * j:2 * j + 2, :]
        for g in range(8):
            two = recv[g * 2 + c, 16:24, :]
            for m in range(2):
                cols = slice((g % 2) * 256 + m * 128, (g % 2) * 256 + (m + 1) * 128)
                if g < 6:
                    taps[c, g // 2:g // 2 + 1, cols] = two[m:m + 1, :]
                else:
                    gains[c:c + 1, cols] = two[m:m + 1, :]


def call(kernel, outs, scratch=(), **kw):
    single = not isinstance(outs, (list, tuple))
    return pl.pallas_call(
        kernel,
        out_shape=outs,
        out_specs=pl.BlockSpec(memory_space=pltpu.VMEM) if single
        else [pl.BlockSpec(memory_space=pltpu.VMEM)] * len(outs),
        scratch_shapes=list(scratch),
        compiler_params=pltpu.CompilerParams(vmem_limit_bytes=48 * 1024 * 1024),
        **kw,
    )


def shards(tokens, cotangent, gaps, taps, gains, proj):
    tok, cot = tokens[0], cotangent[0]
    pair = jnp.stack([gaps[0, 0], 128 - gaps[0, 1]]).astype(BF16)
    own_gap = jnp.pad(jnp.broadcast_to(pair[:, None], (2, C)), ((0, 14), (0, 0)))
    n = 128
    up = jnp.concatenate([tok, cot[64:], own_gap], axis=0)
    down = jnp.concatenate([tok, cot[:64], own_gap], axis=0)
    prev = lax.ppermute(up, SEQ, [(i, i + 1) for i in range(n - 1)])
    nxt = lax.ppermute(down, SEQ, [(i + 1, i) for i in range(n - 1)])
    s = jax.ShapeDtypeStruct
    v = pltpu.VMEM
    tokens_grad, keep, send = call(
        body,
        [s((128, C), BF16), s((ACT, 3 * C), BF16), s((ACT, 3 * C), BF16)],
        [v((384, C), F32), v((384, 1), F32), v((320, C), F32), v((320, C), BF16), v((320, 2 * C), F32),
         v((320, C), F32), v((320, C), F32), v((320, 1), F32), v((256, C), F32), v((256, C), BF16),
         v((256, 2 * C), F32), v((256, 2 * C), BF16), v((256, C), F32), v((128, C), F32),
         v((192, 2 * C), BF16), v((192, C), F32), v((2, ACT, 3 * C), BF16)],
    )(prev, nxt, tok, cot, own_gap, taps, gains, proj)
    recv = lax.ppermute(send, "c", [(0, 1), (1, 0)])
    part = call(terms, s((8, 528, 128), BF16))(keep, recv)
    part = lax.all_to_all(part, NEAR, 0, 0, tiled=True)
    part = call(first_sum, s((32, 32, 128), BF16))(part)
    part = lax.all_to_all(part, FAR, 0, 0, tiled=True)
    part = call(second_sum, s((16, 24, 128), F32))(part)
    part = lax.all_to_all(part, NEAR + ("c",), 0, 0, tiled=True)
    projection_grad, taps_grad, gains_grad = call(
        place, [s((2, 4, 1024), F32), s((2, 3, C), F32), s((2, C), F32)]
    )(part)
    return tokens_grad[None], projection_grad, taps_grad, gains_grad


def solution(mesh):
    fine = Mesh(mesh.devices.reshape(4, 2, 2, 2, 4, 2, 2), ("zh", "zl", "xh", "xl", "yh", "yl", "c"))
    return jax.shard_map(
        shards,
        mesh=fine,
        in_specs=(P(HAP, SEQ, None), P(HAP, SEQ, None), P(SEQ, None), P(), P(), P()),
        out_specs=(P(HAP, SEQ, None), P(None, SEQ, None), P(), P()),
        check_vma=False,
    )
```

time: 1560 us -> 101 us (0.06)
  waiting for transfers between devices: 1270 us -> 4.26 us
  blocking collectives: 229 us -> 62.4 us
    unnamed x2 -> x0, waiting for transfers between devices: 1250 us -> none
    psum x2 -> x0, blocking collectives: 229 us -> none  [the longest x1 127 us: shards(): lax.psum((jnp.stack(filter_tap_products), jnp.stack(gain_terms)), ('seq',...]
    all_to_all x0 -> x3, blocking collectives: none -> 62.4 us  [the longest x1 25.1 us: shards(): part = lax.all_to_all(part, FAR, 0, 0, tiled=True)]
  transfers between devices with their start and end apart: 9 -> 3, of which waited for: 6 -> 2; matrix products, arithmetic and copies ran while one was open for 0% -> 1% of each run, Pallas kernels for 0% -> 0%
where the time goes in v1:
time: 101 us
  blocking collectives  62.4 us (62%)
  starting transfers between devices  19 us (19%)
  Pallas kernels  6.09 us (6%)
  local copies, waits for them, and re-layouts  5.84 us (6%)
  waiting for transfers between devices  4.26 us (4%)
  other arithmetic  1.7 us (2%)
  between operations  1.37 us (1%)
    all_to_all x1, blocking collectives, shards(): part = lax.all_to_all(part, FAR, 0, 0, tiled=True)  25.1 us
    all_to_all x1, blocking collectives, shards(): part = lax.all_to_all(part, NEAR, 0, 0, tiled=True)  24.8 us
    all_to_all x1, blocking collectives, shards(): part = lax.all_to_all(part, NEAR + ('c',), 0, 0, tiled=True)  12.6 us
    ppermute x1, starting transfers between devices, shards(): recv = lax.ppermute(send, 'c', [(0, 1), (1, 0)])  12 us
    ppermute x1, starting transfers between devices, shards(): prev = lax.ppermute(up, SEQ, [(i, i + 1) for i in range(n - 1)])  5.68 us
    pallas_call x1, Pallas kernels, shards(): call(body, [s((128, C), BF16), s((ACT, 3 * C), BF16), s((ACT, 3 * C), BF1...  3.87 us
    unnamed x10, local copies, waits for them, and re-layouts  3.61 us
    ppermute x1, waiting for transfers between devices, shards(): nxt = lax.ppermute(down, SEQ, [(i + 1, i) for i in range(n - 1)])  2.86 us
  transfers between devices with their start and end apart: 3, of which 2 were waited for; matrix products, arithmetic and copies ran while one was open for 1% of the time, Pallas kernels for 0%

profile of v1, /device:TPU:1, one launch (start us, length us, event | category | flops | bytes accessed | tf_op | source)
XLA Modules:
  0.0 100.6 jit_solution(11301150619614246333)
XLA Ops:
  0.6 0.0 copy-start.1
  0.6 0.0 copy-start.2
  0.7 1.3 %slice.22 = s32[1,1]{1,0:T(1,128)} slice(s32[1,2]{1,0:T(1,128)} %param.8), slice={[0:1], [1:2]} | slice | bytes 8 | tf_op jit(solution)/shard_map/slice | solution.py:265
  1.9 0.7 convert.9
  3.2 0.9 slice_bitcast_fusion
  4.1 0.1 fusion
  4.2 0.1 pad.7.own_gap
  4.3 0.9 pad_maximum_fusion
  5.3 1.3 %collective-permute-start.1 = (bf16[208,512]{1,0:T(8,128)(2,1)S(1)}, bf16[208,512]{1,0:T(8,128)(2,1)S(1)}, u32[]{:S(2)}, u32[]{:S(2)}) collective-permute-start(bf16[208,512]{1,0:T(8,128)(2,1)S(1)} %get-tuple-element.20), channel_id=1, source_target_pairs={{4,0},{8,4},{12,8},{16,12},{20,16},{24,20},{28,24},{32,28},{36,32}... | collective-permute-start | bytes 638984 | tf_op jit(solution)/shard_map/ppermute | solution.py:271
  6.6 5.7 %collective-permute-start = (bf16[208,512]{1,0:T(8,128)(2,1)S(1)}, bf16[208,512]{1,0:T(8,128)(2,1)S(1)}, u32[]{:S(2)}, u32[]{:S(2)}) collective-permute-start(bf16[208,512]{1,0:T(8,128)(2,1)S(1)} %get-tuple-element.21), channel_id=1, source_target_pairs={{0,4},{4,8},{8,12},{12,16},{16,20},{20,24},{24,28},{28,32},{32,36}... | collective-permute-start | bytes 638984 | tf_op jit(solution)/shard_map/ppermute | solution.py:270
  12.3 0.7 copy.10.taps
  13.0 2.9 %collective-permute-done.1.nxt = bf16[208,512]{1,0:T(8,128)(2,1)S(1)} collective-permute-done((bf16[208,512]{1,0:T(8,128)(2,1)S(1)}, bf16[208,512]{1,0:T(8,128)(2,1)S(1)}, u32[]{:S(2)}, u32[]{:S(2)}) %collective-permute-start.1) | collective-permute-done | bytes 213024 | tf_op jit(solution)/shard_map/ppermute | solution.py:271
  15.8 0.0 collective-permute-done.prev
  15.8 0.0 copy-done.1
  15.8 0.0 copy-done.2
  15.8 0.0 copy-start
  15.8 1.6 %copy-done = bf16[2,512,1024]{2,1,0:T(8,128)(2,1)S(1)} copy-done((bf16[2,512,1024]{2,1,0:T(8,128)(2,1)S(1)}, bf16[2,512,1024]{2,1,0:T(8,128)(2,1)}, u32[]{:S(2)}) %copy-start) | copy-done | bytes 2097176
  17.4 0.0 copy-start.3
  17.4 0.7 copy-done.3
  18.1 3.9 %shard_map.93 = (bf16[128,512]{1,0:T(8,128)(2,1)}, bf16[144,1536]{1,0:T(8,128)(2,1)S(1)}, bf16[144,1536]{1,0:T(8,128)(2,1)S(1)}) custom-call(bf16[208,512]{1,0:T(8,128)(2,1)S(1)} %collective-permute-done.prev, bf16[208,512]{1,0:T(8,128)(2,1)S(1)} %collective-permute-done.1.nxt, bf16[128,512]{1,0:T(8,128)(2,1)S(1)} %bitcast.12, ...), custom_call_target="tpu_custom_call" | custom-call | tf_op jit(solution)/shard_map/pallas_call | solution.py:274
  22.0 12.0 %collective-permute-start.2 = (bf16[144,1536]{1,0:T(8,128)(2,1)S(1)}, bf16[144,1536]{1,0:T(8,128)(2,1)S(1)}, u32[]{:S(2)}, u32[]{:S(2)}) collective-permute-start(bf16[144,1536]{1,0:T(8,128)(2,1)S(1)} %get-tuple-element.12), channel_id=1, source_target_pairs={{0,1},{1,0},{2,3},{3,2},{4,5},{5,4},{6,7},{7,6},{8,9},{9,8},{10,11... | collective-permute-start | bytes 1327112 | tf_op jit(solution)/shard_map/ppermute | solution.py:282
  34.0 1.4 %collective-permute-done.2.recv = bf16[144,1536]{1,0:T(8,128)(2,1)S(1)} collective-permute-done((bf16[144,1536]{1,0:T(8,128)(2,1)S(1)}, bf16[144,1536]{1,0:T(8,128)(2,1)S(1)}, u32[]{:S(2)}, u32[]{:S(2)}) %collective-permute-start.2) | collective-permute-done | bytes 442400 | tf_op jit(solution)/shard_map/ppermute | solution.py:282
  35.4 1.1 %shard_map.94 = bf16[8,528,128]{2,1,0:T(8,128)(2,1)S(1)} custom-call(bf16[144,1536]{1,0:T(8,128)(2,1)S(1)} %get-tuple-element.11.keep, bf16[144,1536]{1,0:T(8,128)(2,1)S(1)} %collective-permute-done.2.recv), custom_call_target="tpu_custom_call" | custom-call | tf_op jit(solution)/shard_map/pallas_call | solution.py:283
  36.5 24.8 %all_to_all.15.recv = bf16[8,528,128]{2,1,0:T(8,128)(2,1)S(1)} all-to-all(bf16[8,528,128]{2,1,0:T(8,128)(2,1)S(1)} %shard_map.94), channel_id=1, replica_groups=mesh['zh'=4,'zl'=2,'xh'=2,'xl'=2,'yh'=4,'yl'=2,'c'=2] {'zl','xl','yl'}, dimensions={0} | all-to-all | bytes 2162688 | tf_op jit(solution)/shard_map/all_to_all | solution.py:284
  61.3 0.4 shard_map.95
  61.7 25.1 %all_to_all.16.recv = bf16[32,32,128]{2,1,0:T(8,128)(2,1)S(1)} all-to-all(bf16[32,32,128]{2,1,0:T(8,128)(2,1)S(1)} %shard_map.95), channel_id=1, replica_groups=mesh['zh'=4,'zl'=2,'xh'=2,'xl'=2,'yh'=4,'yl'=2,'c'=2] {'zh','xh','yh'}, dimensions={0} | all-to-all | bytes 524288 | tf_op jit(solution)/shard_map/all_to_all | solution.py:286
  86.8 12.6 %all_to_all.17.recv = f32[16,24,128]{2,1,0:T(8,128)S(1)} all-to-all(f32[16,24,128]{2,1,0:T(8,128)S(1)} %shard_map.96), channel_id=1, replica_groups=mesh['zh'=4,'zl'=2,'xh'=2,'xl'=2,'yh'=4,'yl'=2,'c'=2] {'zl','xl','yl','c'}, dimensions={0} | all-to-all | bytes 393216 | tf_op jit(solution)/shard_map/all_to_all | solution.py:288
  99.4 0.6 shard_map.97
  100.0 0.6 copy.11
  (1 shorter events, 0.0 us)
Async XLA Ops:
  0.6 15.2 %copy-start.1 = (bf16[1,128,512]{2,1,0:T(8,128)(2,1)S(1)}, bf16[1,128,512]{2,1,0:T(8,128)(2,1)}, u32[]{:S(2)}) copy-start(bf16[1,128,512]{2,1,0:T(8,128)(2,1)} %param.7) | copy-start | bytes 393220
  0.6 15.2 %copy-start.2 = (bf16[1,128,512]{2,1,0:T(8,128)(2,1)S(1)}, bf16[1,128,512]{2,1,0:T(8,128)(2,1)}, u32[]{:S(2)}) copy-start(bf16[1,128,512]{2,1,0:T(8,128)(2,1)} %param.6) | copy-start | bytes 393220
  5.3 10.6 %collective-permute-start.1 = (bf16[208,512]{1,0:T(8,128)(2,1)S(1)}, bf16[208,512]{1,0:T(8,128)(2,1)S(1)}, u32[]{:S(2)}, u32[]{:S(2)}) collective-permute-start(bf16[208,512]{1,0:T(8,128)(2,1)S(1)} %get-tuple-element.20), channel_id=1, source_target_pairs={{4,0},{8,4},{12,8},{16,12},{20,16},{24,20},{28,24},{32,28},{36,32}... | collective-permute-start | bytes 638984 | tf_op jit(solution)/shard_map/ppermute | solution.py:271
  6.6 9.3 %collective-permute-start = (bf16[208,512]{1,0:T(8,128)(2,1)S(1)}, bf16[208,512]{1,0:T(8,128)(2,1)S(1)}, u32[]{:S(2)}, u32[]{:S(2)}) collective-permute-start(bf16[208,512]{1,0:T(8,128)(2,1)S(1)} %get-tuple-element.21), channel_id=1, source_target_pairs={{0,4},{4,8},{8,12},{12,16},{16,20},{20,24},{24,28},{28,32},{32,36}... | collective-permute-start | bytes 638984 | tf_op jit(solution)/shard_map/ppermute | solution.py:270
  15.8 1.6 %copy-start = (bf16[2,512,1024]{2,1,0:T(8,128)(2,1)S(1)}, bf16[2,512,1024]{2,1,0:T(8,128)(2,1)}, u32[]{:S(2)}) copy-start(bf16[2,512,1024]{2,1,0:T(8,128)(2,1)} %proj.1) | copy-start | bytes 6291460
  17.4 0.7 copy-start.3
  22.0 13.4 %collective-permute-start.2 = (bf16[144,1536]{1,0:T(8,128)(2,1)S(1)}, bf16[144,1536]{1,0:T(8,128)(2,1)S(1)}, u32[]{:S(2)}, u32[]{:S(2)}) collective-permute-start(bf16[144,1536]{1,0:T(8,128)(2,1)S(1)} %get-tuple-element.12), channel_id=1, source_target_pairs={{0,1},{1,0},{2,3},{3,2},{4,5},{5,4},{6,7},{7,6},{8,9},{9,8},{10,11... | collective-permute-start | bytes 1327112 | tf_op jit(solution)/shard_map/ppermute | solution.py:282

commit v2 on v1

--- a/solution.py
+++ b/solution.py
@@ -17,7 +17,7 @@
 HAP = ("yl", "c")
 G0 = 0.7978845608028654
 G1 = 0.044715
-PACK = 208
+MARK = 64.0
 ACT = 144
 
 
@@ -47,19 +47,33 @@
     return hi, lo
 
 
-def body(prev, nxt, tok, cot, own_gap, taps, gains, proj, out, keep, send,
+def pack(gaps, tok, cot, up, down):
+    at = lax.broadcasted_iota(jnp.int32, (128, 1), 0)
+    inside = (at >= gaps[0, 0]) & (at < gaps[0, 1])
+    marked = jnp.where(inside, MARK, tok[...].astype(F32)).astype(BF16)
+    up[0:128, :] = marked
+    down[0:128, :] = marked
+    up[128:192, :] = cot[64:128, :]
+    down[128:192, :] = cot[0:64, :]
+
+
+def warm(gaps, tok, cot, taps, gains, proj, valid, tok_out, cot_out, taps_out, gains_out, proj_out):
+    at = lax.broadcasted_iota(jnp.int32, (128, 1), 0)
+    valid[...] = jnp.where((at >= gaps[0, 0]) & (at < gaps[0, 1]), 0.0, 1.0)
+    for a, b in ((tok, tok_out), (cot, cot_out), (taps, taps_out), (gains, gains_out), (proj, proj_out)):
+        b[...] = a[...]
+
+
+def body(own_valid, prev, nxt, tok, cot, taps, gains, proj, out, keep, send,
          n0, i0, g0, h0, ab0, x1, n1, i1, g1, h1, po1, dp1, dh1, gr1, dp0, dh0, act):
     core = lax.axis_index("c")
-    steps = lax.broadcasted_iota(jnp.int32, (DIL, 1), 0).astype(F32)
-
-    gap_of = []
-    for tile in (prev[192:208, :], own_gap[...], nxt[192:208, :]):
-        tile = tile.astype(F32)
-        gap_of.append((tile[0:1, 0:1], 128.0 - tile[1:2, 0:1]))
-
-    def rows(base, count=DIL):
+    place_in_seq = sum(lax.axis_index(a) for a in SEQ)
+    inner = (place_in_seq > 0, None, place_in_seq < 9)
+
+    def rows(base):
         ref, at = ((prev, base), (tok, base - 128), (nxt, base - 256))[base // 128]
-        return ref[at:at + count, :].astype(F32)
+        v = ref[at:at + DIL, :].astype(F32)
+        return v if ref is tok else jnp.where(v[:, 0:1] < 0.5 * MARK, v, 0.0)
 
     def cot_rows(base):
         if base < 128:
@@ -70,16 +84,19 @@
 
     valid_of = []
     for chunk in range(12):
-        start, end = gap_of[chunk // 4]
-        at = steps + float(DIL * (chunk % 4))
-        valid_of.append(jnp.where((at >= start) & (at < end), 0.0, 1.0))
+        if 4 <= chunk < 8:
+            valid_of.append(own_valid[DIL * (chunk - 4):DIL * (chunk - 3), :])
+        else:
+            ref = prev if chunk < 4 else nxt
+            lead = ref[DIL * (chunk % 4):DIL * (chunk % 4) + DIL, 0:128].astype(F32)[:, 0:1]
+            valid_of.append(jnp.where(lead < 0.5 * MARK, jnp.where(inner[chunk // 4], 1.0, 0.0), 0.0))
 
     def norm(v, valid, gain):
         inv = lax.rsqrt(jnp.sum(v * v, axis=-1, keepdims=True) * (1.0 / C) + EPS)
         return inv, v * inv * gain * valid
 
     def tap(layer, k):
-        return taps[layer, k:k + 1, :]
+        return taps[k, layer:layer + 1, :]
 
     def conv(ref, at, layer):
         return (tap(layer, 0) * ref[at - DIL:at, :] + tap(layer, 1) * ref[at:at + DIL, :]
@@ -196,12 +213,10 @@
         out[:, j * 64:(j + 1) * 64, :] = t.astype(BF16).reshape(8, 64, 128)
     small = (keep[128:ACT, 0:C].astype(F32) + keep[128:ACT, C:2 * C].astype(F32)
              + recv[128:ACT, 0:C].astype(F32) + recv[128:ACT, C:2 * C].astype(F32))
-    pad = jnp.zeros((12, 128), F32)
+    tile = jnp.concatenate(
+        [small[r:r + 1, 128 * q:128 * (q + 1)] for r in range(4) for q in range(4)], axis=0).astype(BF16)
     for g in range(8):
-        row, half = g // 2, (g % 2) * 256
-        two = jnp.concatenate([small[row:row + 1, half + 128 * m:half + 128 * (m + 1)] for m in range(2)], axis=0)
-        hi = two.astype(BF16).astype(F32)
-        out[g, 512:528, :] = jnp.concatenate([hi, two - hi, pad], axis=0).astype(BF16)
+        out[g, 512:528, :] = tile
 
 
 def first_sum(recv, out):
@@ -213,9 +228,7 @@
     pick = (src == lax.broadcasted_iota(jnp.int32, (C, C), 1)).astype(F32).astype(BF16)
     moved = dot(pick, total[0:512, :].astype(BF16), ((1,), (0,))).astype(BF16)
     out[:, 0:16, :] = moved.reshape(32, 16, 128)
-    two = total[512:514, :] + total[514:516, :]
-    hi = two.astype(BF16).astype(F32)
-    tile = jnp.concatenate([hi, two - hi, jnp.zeros((12, 128), F32)], axis=0).astype(BF16)
+    tile = total[512:528, :].astype(BF16)
     for d in range(32):
         out[d, 16:32, :] = tile
 
@@ -224,72 +237,70 @@
     total = recv[0].astype(F32)
     for i in range(1, 32):
         total += recv[i].astype(F32)
-    two = total[16:18, :] + total[18:20, :]
-    both = jnp.concatenate([total[0:16, :], two, jnp.zeros((6, 128), F32)], axis=0)
-    for i in range(16):
-        out[i] = both
+    out[...] = total
 
 
 def place(recv, proj, taps, gains):
-    base = (lax.axis_index("zl") * 2 + lax.axis_index("xl")) * 4
     for c in range(2):
         for y in range(2):
-            piece = recv[base + y * 2 + c]
             for j in range(8):
-                proj[c, 2 * y:2 * y + 2, j * 128:(j + 1) * 128] = piece[2 * j:2 * j + 2, :]
-        for g in range(8):
-            two = recv[g * 2 + c, 16:24, :]
-            for m in range(2):
-                cols = slice((g % 2) * 256 + m * 128, (g % 2) * 256 + (m + 1) * 128)
-                if g < 6:
-                    taps[c, g // 2:g // 2 + 1, cols] = two[m:m + 1, :]
+                proj[c, 2 * y:2 * y + 2, j * 128:(j + 1) * 128] = recv[y * 2 + c, 2 * j:2 * j + 2, :]
+        for r in range(4):
+            for q in range(4):
+                row = recv[c, 16 + r * 4 + q:17 + r * 4 + q, :]
+                if r < 3:
+                    taps[r, c:c + 1, q * 128:(q + 1) * 128] = row
                 else:
-                    gains[c:c + 1, cols] = two[m:m + 1, :]
-
-
-def call(kernel, outs, scratch=(), **kw):
+                    gains[c:c + 1, q * 128:(q + 1) * 128] = row
+
+
+def call(kernel, ins, outs, scratch=(), mib=48):
     single = not isinstance(outs, (list, tuple))
+    vmem = pl.BlockSpec(memory_space=pltpu.VMEM)
     return pl.pallas_call(
         kernel,
         out_shape=outs,
-        out_specs=pl.BlockSpec(memory_space=pltpu.VMEM) if single
-        else [pl.BlockSpec(memory_space=pltpu.VMEM)] * len(outs),
+        in_specs=[pl.BlockSpec(memory_space={"v": pltpu.VMEM, "s": pltpu.SMEM, "a": pl.ANY}[m]) for m in ins],
+        out_specs=vmem if single else [vmem] * len(outs),
         scratch_shapes=list(scratch),
-        compiler_params=pltpu.CompilerParams(vmem_limit_bytes=48 * 1024 * 1024),
-        **kw,
+        compiler_params=pltpu.CompilerParams(vmem_limit_bytes=int(mib * 1024 * 1024)),
     )
 
 
 def shards(tokens, cotangent, gaps, taps, gains, proj):
     tok, cot = tokens[0], cotangent[0]
-    pair = jnp.stack([gaps[0, 0], 128 - gaps[0, 1]]).astype(BF16)
-    own_gap = jnp.pad(jnp.broadcast_to(pair[:, None], (2, C)), ((0, 14), (0, 0)))
     n = 128
-    up = jnp.concatenate([tok, cot[64:], own_gap], axis=0)
-    down = jnp.concatenate([tok, cot[:64], own_gap], axis=0)
+    s = jax.ShapeDtypeStruct
+    v = pltpu.VMEM
+    up, down = call(pack, "svv", [s((192, C), BF16), s((192, C), BF16)], mib=58)(gaps, tok, cot)
     prev = lax.ppermute(up, SEQ, [(i, i + 1) for i in range(n - 1)])
     nxt = lax.ppermute(down, SEQ, [(i + 1, i) for i in range(n - 1)])
-    s = jax.ShapeDtypeStruct
-    v = pltpu.VMEM
+    near_args = call(
+        warm,
+        "svvvvv",
+        [s((128, 1), F32), s((128, C), BF16), s((128, C), BF16), s((3, 2, C), F32), s((2, C), F32),
+         s((2, C, 2 * C), BF16)],
+    )(gaps, tok, cot, jnp.transpose(taps, (1, 0, 2)), gains, proj)
     tokens_grad, keep, send = call(
         body,
+        "vvvvvvvv",
         [s((128, C), BF16), s((ACT, 3 * C), BF16), s((ACT, 3 * C), BF16)],
         [v((384, C), F32), v((384, 1), F32), v((320, C), F32), v((320, C), BF16), v((320, 2 * C), F32),
          v((320, C), F32), v((320, C), F32), v((320, 1), F32), v((256, C), F32), v((256, C), BF16),
          v((256, 2 * C), F32), v((256, 2 * C), BF16), v((256, C), F32), v((128, C), F32),
          v((192, 2 * C), BF16), v((192, C), F32), v((2, ACT, 3 * C), BF16)],
-    )(prev, nxt, tok, cot, own_gap, taps, gains, proj)
+    )(near_args[0], prev, nxt, *near_args[1:])
     recv = lax.ppermute(send, "c", [(0, 1), (1, 0)])
-    part = call(terms, s((8, 528, 128), BF16))(keep, recv)
+    part = call(terms, "vv", s((8, 528, 128), BF16))(keep, recv)
     part = lax.all_to_all(part, NEAR, 0, 0, tiled=True)
-    part = call(first_sum, s((32, 32, 128), BF16))(part)
+    part = call(first_sum, "v", s((32, 32, 128), BF16))(part)
     part = lax.all_to_all(part, FAR, 0, 0, tiled=True)
-    part = call(second_sum, s((16, 24, 128), F32))(part)
-    part = lax.all_to_all(part, NEAR + ("c",), 0, 0, tiled=True)
+    part = call(second_sum, "v", s((32, 128), F32))(part)
+    part = lax.all_gather(part, HAP, axis=0)
     projection_grad, taps_grad, gains_grad = call(
-        place, [s((2, 4, 1024), F32), s((2, 3, C), F32), s((2, C), F32)]
+        place, "v", [s((2, 4, 1024), F32), s((3, 2, C), F32), s((2, C), F32)]
     )(part)
-    return tokens_grad[None], projection_grad, taps_grad, gains_grad
+    return tokens_grad[None], projection_grad, jnp.transpose(taps_grad, (1, 0, 2)), gains_grad
 
 
 def solution(mesh):

time: 101 us -> 92.8 us (0.919)
  starting transfers between devices: 19 us -> 8.84 us
  waiting for transfers between devices: 4.26 us -> 9.01 us
  blocking collectives: 62.4 us -> 59.8 us
  Pallas kernels: 6.09 us -> 8.64 us
  other arithmetic: 1.7 us -> 0 us
    all_to_all x1 -> x0, blocking collectives: 12.6 us -> none  [shards(): part = lax.all_to_all(part, NEAR + ('c',), 0, 0, tiled=True)]
    ppermute x1, starting transfers between devices: 12 us -> 2.5 us  [shards(): recv = lax.ppermute(send, 'c', [(0, 1), (1, 0)])]
    all_gather x0 -> x1, blocking collectives: none -> 8.88 us  [shards(): part = lax.all_gather(part, HAP, axis=0)]
    all_to_all x1, blocking collectives: 25.1 us -> 31.9 us  [shards(): part = lax.all_to_all(part, FAR, 0, 0, tiled=True)]
    all_to_all x1, blocking collectives: 24.8 us -> 19 us  [shards(): part = lax.all_to_all(part, NEAR, 0, 0, tiled=True)]
    ppermute x1, waiting for transfers between devices: 2.86 us -> 7.61 us  [shards(): nxt = lax.ppermute(down, SEQ, [(i + 1, i) for i in range(n - 1)])]
    pallas_call x5 -> x7, Pallas kernels: 6.09 us -> 8.64 us  [the longest x1 3.95 us: shards(): call(body, 'vvvvvvvv', [s((128, C), BF16), s((ACT, 3 * C), BF16), s((ACT,...]
    slice x2 -> x0, local copies, waits for them, and re-layouts: 2.16 us -> none  [the longest x1 1.28 us: shards(): pair = jnp.stack([gaps[0, 0], 128 - gaps[0, 1]]).astype(BF16)]
  transfers between devices with their start and end apart: 3 -> 3, of which waited for: 2 -> 2; matrix products, arithmetic and copies ran while one was open for 1% -> 0% of each run, Pallas kernels for 0% -> 1%
where the time goes in v2:
time: 92.8 us; the launch traced here: 92.4 us
  blocking collectives  59.8 us (64%)
  waiting for transfers between devices  9.01 us (10%)
  starting transfers between devices  8.84 us (10%)
  Pallas kernels  8.64 us (9%)
  local copies, waits for them, and re-layouts  5.44 us (6%)
    all_to_all x1, blocking collectives, shards(): part = lax.all_to_all(part, FAR, 0, 0, tiled=True)  31.9 us
    all_to_all x1, blocking collectives, shards(): part = lax.all_to_all(part, NEAR, 0, 0, tiled=True)  19 us
    all_gather x1, blocking collectives, shards(): part = lax.all_gather(part, HAP, axis=0)  8.88 us
    ppermute x1, waiting for transfers between devices, shards(): nxt = lax.ppermute(down, SEQ, [(i + 1, i) for i in range(n - 1)])  7.61 us
    unnamed x12, local copies, waits for them, and re-layouts  5.44 us
    ppermute x1, starting transfers between devices, shards(): prev = lax.ppermute(up, SEQ, [(i, i + 1) for i in range(n - 1)])  5.04 us
    pallas_call x1, Pallas kernels, shards(): call(body, 'vvvvvvvv', [s((128, C), BF16), s((ACT, 3 * C), BF16), s((ACT,...  3.95 us
    ppermute x1, starting transfers between devices, shards(): recv = lax.ppermute(send, 'c', [(0, 1), (1, 0)])  2.5 us
  transfers between devices with their start and end apart: 3, of which 2 were waited for; matrix products, arithmetic and copies ran while one was open for 0% of the time, Pallas kernels for 1%

profile of v2, /device:TPU:1, one launch (start us, length us, event | category | flops | bytes accessed | tf_op | source)
XLA Modules:
  0.0 92.4 jit_solution(12172132655605265709)
XLA Ops:
  0.6 1.8 %shard_map.94 = (bf16[192,512]{1,0:T(8,128)(2,1)}, bf16[192,512]{1,0:T(8,128)(2,1)}) custom-call(s32[1,2]{1,0:T(1,128)} %gaps.3, bf16[128,512]{1,0:T(8,128)(2,1)} %bitcast.6, bf16[128,512]{1,0:T(8,128)(2,1)} %bitcast.8), custom_call_target="tpu_custom_call" | custom-call | tf_op jit(solution)/shard_map/pallas_call | solution.py:275
  2.4 5.0 %collective-permute-start = (bf16[192,512]{1,0:T(8,128)(2,1)}, bf16[192,512]{1,0:T(8,128)(2,1)S(1)}, u32[]{:S(2)}, u32[]{:S(2)}) collective-permute-start(bf16[192,512]{1,0:T(8,128)(2,1)} %get-tuple-element.19), channel_id=1, source_target_pairs={{0,4},{4,8},{8,12},{12,16},{16,20},{20,24},{24,28},{28,32},{32,36}... | collective-permute-start | bytes 589832 | tf_op jit(solution)/shard_map/ppermute | solution.py:276
  7.4 1.3 %collective-permute-start.1 = (bf16[192,512]{1,0:T(8,128)(2,1)}, bf16[192,512]{1,0:T(8,128)(2,1)S(1)}, u32[]{:S(2)}, u32[]{:S(2)}) collective-permute-start(bf16[192,512]{1,0:T(8,128)(2,1)} %get-tuple-element.20), channel_id=1, source_target_pairs={{4,0},{8,4},{12,8},{16,12},{20,16},{24,20},{28,24},{32,28},{36,32}... | collective-permute-start | bytes 589832 | tf_op jit(solution)/shard_map/ppermute | solution.py:277
  8.7 0.0 copy-start
  8.7 1.6 %copy-done = bf16[2,512,1024]{2,1,0:T(8,128)(2,1)S(1)} copy-done((bf16[2,512,1024]{2,1,0:T(8,128)(2,1)S(1)}, bf16[2,512,1024]{2,1,0:T(8,128)(2,1)}, u32[]{:S(2)}) %copy-start) | copy-done | bytes 2097176
  10.3 0.0 copy-start.1
  10.3 0.9 copy-done.1
  11.2 0.0 copy-start.2
  11.2 0.9 copy-done.2
  12.1 0.0 copy-start.3
  12.1 0.7 copy-done.3
  12.8 0.0 copy-start.4
  12.9 0.7 copy-done.4
  13.5 0.0 copy-start.5
  13.5 0.7 copy-done.5
  14.2 0.7 shard_map.93
  14.9 0.0 collective-permute-done.prev
  14.9 7.6 %collective-permute-done.1.nxt = bf16[192,512]{1,0:T(8,128)(2,1)S(1)} collective-permute-done((bf16[192,512]{1,0:T(8,128)(2,1)}, bf16[192,512]{1,0:T(8,128)(2,1)S(1)}, u32[]{:S(2)}, u32[]{:S(2)}) %collective-permute-start.1) | collective-permute-done | bytes 196640 | tf_op jit(solution)/shard_map/ppermute | solution.py:277
  22.5 4.0 %shard_map.95 = (bf16[128,512]{1,0:T(8,128)(2,1)}, bf16[144,1536]{1,0:T(8,128)(2,1)S(1)}, bf16[144,1536]{1,0:T(8,128)(2,1)S(1)}) custom-call(f32[128,1]{1,0:T(8,128)S(1)} %get-tuple-element.18.own_valid, bf16[192,512]{1,0:T(8,128)(2,1)S(1)} %collective-permute-done.prev, bf16[192,512]{1,0:T(8,128)(2,1)S(1)} %collective-permute-done.1.nxt, ...), custom_call_target="tpu_custom_call" | custom-call | tf_op jit(solution)/shard_map/pallas_call | solution.py:284
  26.5 2.5 %collective-permute-start.2 = (bf16[144,1536]{1,0:T(8,128)(2,1)S(1)}, bf16[144,1536]{1,0:T(8,128)(2,1)S(1)}, u32[]{:S(2)}, u32[]{:S(2)}) collective-permute-start(bf16[144,1536]{1,0:T(8,128)(2,1)S(1)} %get-tuple-element.28), channel_id=1, source_target_pairs={{0,1},{1,0},{2,3},{3,2},{4,5},{5,4},{6,7},{7,6},{8,9},{9,8},{10,11... | collective-permute-start | bytes 1327112 | tf_op jit(solution)/shard_map/ppermute | solution.py:293
  29.0 1.4 %collective-permute-done.2.recv = bf16[144,1536]{1,0:T(8,128)(2,1)S(1)} collective-permute-done((bf16[144,1536]{1,0:T(8,128)(2,1)S(1)}, bf16[144,1536]{1,0:T(8,128)(2,1)S(1)}, u32[]{:S(2)}, u32[]{:S(2)}) %collective-permute-start.2) | collective-permute-done | bytes 442400 | tf_op jit(solution)/shard_map/ppermute | solution.py:293
  30.4 1.1 %shard_map.96 = bf16[8,528,128]{2,1,0:T(8,128)(2,1)S(1)} custom-call(bf16[144,1536]{1,0:T(8,128)(2,1)S(1)} %get-tuple-element.27.keep, bf16[144,1536]{1,0:T(8,128)(2,1)S(1)} %collective-permute-done.2.recv), custom_call_target="tpu_custom_call" | custom-call | tf_op jit(solution)/shard_map/pallas_call | solution.py:294
  31.5 19.0 %all_to_all.10.recv = bf16[8,528,128]{2,1,0:T(8,128)(2,1)S(1)} all-to-all(bf16[8,528,128]{2,1,0:T(8,128)(2,1)S(1)} %shard_map.96), channel_id=1, replica_groups=mesh['zh'=4,'zl'=2,'xh'=2,'xl'=2,'yh'=4,'yl'=2,'c'=2] {'zl','xl','yl'}, dimensions={0} | all-to-all | bytes 2162688 | tf_op jit(solution)/shard_map/all_to_all | solution.py:295
  50.5 0.4 shard_map.97
  50.9 31.9 %all_to_all.11.recv = bf16[32,32,128]{2,1,0:T(8,128)(2,1)S(1)} all-to-all(bf16[32,32,128]{2,1,0:T(8,128)(2,1)S(1)} %shard_map.97), channel_id=1, replica_groups=mesh['zh'=4,'zl'=2,'xh'=2,'xl'=2,'yh'=4,'yl'=2,'c'=2] {'zh','xh','yh'}, dimensions={0} | all-to-all | bytes 524288 | tf_op jit(solution)/shard_map/all_to_all | solution.py:297
  82.9 8.9 %all-gather = f32[128,128]{1,0:T(8,128)S(1)} all-gather(f32[32,128]{1,0:T(8,128)S(1)} %shard_map.98), channel_id=2, replica_groups=mesh['zh'=4,'zl'=2,'xh'=2,'xl'=2,'yh'=4,'yl'=2,'c'=2] {'yl','c'}, dimensions={0}, use_global_device_ids=true | all-gather | bytes 81920 | tf_op jit(solution)/shard_map/all_gather | solution.py:299
  91.7 0.6 shard_map.99
  (1 shorter events, 0.0 us)
Async XLA Ops:
  2.4 12.5 %collective-permute-start = (bf16[192,512]{1,0:T(8,128)(2,1)}, bf16[192,512]{1,0:T(8,128)(2,1)S(1)}, u32[]{:S(2)}, u32[]{:S(2)}) collective-permute-start(bf16[192,512]{1,0:T(8,128)(2,1)} %get-tuple-element.19), channel_id=1, source_target_pairs={{0,4},{4,8},{8,12},{12,16},{16,20},{20,24},{24,28},{28,32},{32,36}... | collective-permute-start | bytes 589832 | tf_op jit(solution)/shard_map/ppermute | solution.py:276
  7.4 15.1 %collective-permute-start.1 = (bf16[192,512]{1,0:T(8,128)(2,1)}, bf16[192,512]{1,0:T(8,128)(2,1)S(1)}, u32[]{:S(2)}, u32[]{:S(2)}) collective-permute-start(bf16[192,512]{1,0:T(8,128)(2,1)} %get-tuple-element.20), channel_id=1, source_target_pairs={{4,0},{8,4},{12,8},{16,12},{20,16},{24,20},{28,24},{32,28},{36,32}... | collective-permute-start | bytes 589832 | tf_op jit(solution)/shard_map/ppermute | solution.py:277
  8.7 1.6 %copy-start = (bf16[2,512,1024]{2,1,0:T(8,128)(2,1)S(1)}, bf16[2,512,1024]{2,1,0:T(8,128)(2,1)}, u32[]{:S(2)}) copy-start(bf16[2,512,1024]{2,1,0:T(8,128)(2,1)} %proj.1) | copy-start | bytes 6291460
  10.3 0.9 copy-start.1
  11.2 0.9 copy-start.2
  12.1 0.7 copy-start.3
  12.8 0.7 copy-start.4
  13.5 0.7 copy-start.5
  26.5 3.9 %collective-permute-start.2 = (bf16[144,1536]{1,0:T(8,128)(2,1)S(1)}, bf16[144,1536]{1,0:T(8,128)(2,1)S(1)}, u32[]{:S(2)}, u32[]{:S(2)}) collective-permute-start(bf16[144,1536]{1,0:T(8,128)(2,1)S(1)} %get-tuple-element.28), channel_id=1, source_target_pairs={{0,1},{1,0},{2,3},{3,2},{4,5},{5,4},{6,7},{7,6},{8,9},{9,8},{10,11... | collective-permute-start | bytes 1327112 | tf_op jit(solution)/shard_map/ppermute | solution.py:293

commit v3 on v2

--- a/solution.py
+++ b/solution.py
@@ -11,9 +11,9 @@
 EPS = 1e-06
 F32 = jnp.float32
 BF16 = jnp.bfloat16
-NEAR = ("zl", "xl", "yl")
-FAR = ("zh", "xh", "yh")
-SEQ = ("zh", "zl", "xh", "xl", "yh")
+NEAR = ("x", "yl")
+FAR = ("z", "yh")
+SEQ = ("z", "x", "yh")
 HAP = ("yl", "c")
 G0 = 0.7978845608028654
 G1 = 0.044715
@@ -68,7 +68,7 @@
          n0, i0, g0, h0, ab0, x1, n1, i1, g1, h1, po1, dp1, dh1, gr1, dp0, dh0, act):
     core = lax.axis_index("c")
     place_in_seq = sum(lax.axis_index(a) for a in SEQ)
-    inner = (place_in_seq > 0, None, place_in_seq < 9)
+    inner = (place_in_seq > 0, None, place_in_seq < 13)
 
     def rows(base):
         ref, at = ((prev, base), (tok, base - 128), (nxt, base - 256))[base // 128]
@@ -202,8 +202,7 @@
 
 def terms(keep, recv, out):
     q = lax.broadcasted_iota(jnp.int32, (C, 1), 0)
-    ch = (((q >> 4) & 3) << 7 | ((q >> 8) & 1) << 6 | ((q >> 3) & 1) << 5 | ((q >> 7) & 1) << 4
-          | ((q >> 1) & 3) << 2 | ((q >> 6) & 1) << 1 | (q & 1))
+    ch = ((q >> 3) & 7) << 6 | ((q >> 7) & 3) << 4 | ((q >> 1) & 3) << 2 | ((q >> 6) & 1) << 1 | (q & 1)
     pick = (ch == lax.broadcasted_iota(jnp.int32, (C, C), 1)).astype(F32).astype(BF16)
     ha = dot(pick, keep[0:128, 0:C], ((1,), (1,))).astype(BF16)
     hb = dot(pick, recv[0:128, 0:C], ((1,), (1,))).astype(BF16)
@@ -272,7 +271,8 @@
     n = 128
     s = jax.ShapeDtypeStruct
     v = pltpu.VMEM
-    up, down = call(pack, "svv", [s((192, C), BF16), s((192, C), BF16)], mib=58)(gaps, tok, cot)
+    far = [pltpu.with_memory_space_constraint(a, pltpu.HBM) for a in (gaps, tok, cot)]
+    up, down = call(pack, "svv", [s((192, C), BF16), s((192, C), BF16)], mib=48)(*far)
     prev = lax.ppermute(up, SEQ, [(i, i + 1) for i in range(n - 1)])
     nxt = lax.ppermute(down, SEQ, [(i + 1, i) for i in range(n - 1)])
     near_args = call(
@@ -304,7 +304,7 @@
 
 
 def solution(mesh):
-    fine = Mesh(mesh.devices.reshape(4, 2, 2, 2, 4, 2, 2), ("zh", "zl", "xh", "xl", "yh", "yl", "c"))
+    fine = Mesh(mesh.devices.reshape(8, 4, 4, 2, 2), ("z", "x", "yh", "yl", "c"))
     return jax.shard_map(
         shards,
         mesh=fine,

time: 92.8 us -> 87.7 us (0.945)
  blocking collectives: 59.8 us -> 55.7 us
    all_to_all x1, blocking collectives: 31.9 us -> 27.7 us  [shards(): part = lax.all_to_all(part, FAR, 0, 0, tiled=True)]
where the time goes in v3:
time: 87.7 us; the launch traced here: 87.3 us
  blocking collectives  55.7 us (64%)
  starting transfers between devices  8.86 us (10%)
  waiting for transfers between devices  8.8 us (10%)
  Pallas kernels  7.83 us (9%)
  local copies, waits for them, and re-layouts  5.44 us (6%)
    all_to_all x1, blocking collectives, shards(): part = lax.all_to_all(part, FAR, 0, 0, tiled=True)  27.7 us
    all_to_all x1, blocking collectives, shards(): part = lax.all_to_all(part, NEAR, 0, 0, tiled=True)  19.4 us
    all_gather x1, blocking collectives, shards(): part = lax.all_gather(part, HAP, axis=0)  8.54 us
    ppermute x1, waiting for transfers between devices, shards(): nxt = lax.ppermute(down, SEQ, [(i + 1, i) for i in range(n - 1)])  7.4 us
    unnamed x12, local copies, waits for them, and re-layouts  5.44 us
    ppermute x1, starting transfers between devices, shards(): prev = lax.ppermute(up, SEQ, [(i, i + 1) for i in range(n - 1)])  5.05 us
    pallas_call x1, Pallas kernels, shards(): call(body, 'vvvvvvvv', [s((128, C), BF16), s((ACT, 3 * C), BF16), s((ACT,...  3.95 us
    ppermute x1, starting transfers between devices, shards(): recv = lax.ppermute(send, 'c', [(0, 1), (1, 0)])  2.51 us
  transfers between devices with their start and end apart: 3, of which 2 were waited for; matrix products, arithmetic and copies ran while one was open for 0% of the time, Pallas kernels for 1%

profile of v3, /device:TPU:1, one launch (start us, length us, event | category | flops | bytes accessed | tf_op | source)
XLA Modules:
  0.0 87.3 jit_solution(8070548687040546564)
XLA Ops:
  0.6 1.0 %shard_map.94 = (bf16[192,512]{1,0:T(8,128)(2,1)S(1)}, bf16[192,512]{1,0:T(8,128)(2,1)S(1)}) custom-call(s32[1,2]{1,0:T(1,128)} %gaps.3, bf16[128,512]{1,0:T(8,128)(2,1)} %bitcast.6, bf16[128,512]{1,0:T(8,128)(2,1)} %bitcast.8), custom_call_target="tpu_custom_call" | custom-call | tf_op jit(solution)/shard_map/pallas_call | solution.py:275
  1.7 5.1 %collective-permute-start = (bf16[192,512]{1,0:T(8,128)(2,1)S(1)}, bf16[192,512]{1,0:T(8,128)(2,1)S(1)}, u32[]{:S(2)}, u32[]{:S(2)}) collective-permute-start(bf16[192,512]{1,0:T(8,128)(2,1)S(1)} %get-tuple-element.19), channel_id=1, source_target_pairs={{0,4},{4,8},{8,12},{12,16},{16,20},{20,24},{24,28},{28,32},{32,36}... | collective-permute-start | bytes 589832 | tf_op jit(solution)/shard_map/ppermute | solution.py:276
  6.7 1.3 %collective-permute-start.1 = (bf16[192,512]{1,0:T(8,128)(2,1)S(1)}, bf16[192,512]{1,0:T(8,128)(2,1)S(1)}, u32[]{:S(2)}, u32[]{:S(2)}) collective-permute-start(bf16[192,512]{1,0:T(8,128)(2,1)S(1)} %get-tuple-element.20), channel_id=1, source_target_pairs={{4,0},{8,4},{12,8},{16,12},{20,16},{24,20},{28,24},{32,28},{36,32}... | collective-permute-start | bytes 589832 | tf_op jit(solution)/shard_map/ppermute | solution.py:277
  8.0 0.0 copy-start
  8.0 1.6 %copy-done = bf16[2,512,1024]{2,1,0:T(8,128)(2,1)S(1)} copy-done((bf16[2,512,1024]{2,1,0:T(8,128)(2,1)S(1)}, bf16[2,512,1024]{2,1,0:T(8,128)(2,1)}, u32[]{:S(2)}) %copy-start) | copy-done | bytes 2097176
  9.6 0.0 copy-start.1
  9.6 0.9 %copy-done.1 = bf16[1,128,512]{2,1,0:T(8,128)(2,1)S(1)} copy-done((bf16[1,128,512]{2,1,0:T(8,128)(2,1)S(1)}, bf16[1,128,512]{2,1,0:T(8,128)(2,1)}, u32[]{:S(2)}) %copy-start.1) | copy-done | bytes 131096
  10.5 0.0 copy-start.2
  10.5 0.9 %copy-done.2 = bf16[1,128,512]{2,1,0:T(8,128)(2,1)S(1)} copy-done((bf16[1,128,512]{2,1,0:T(8,128)(2,1)S(1)}, bf16[1,128,512]{2,1,0:T(8,128)(2,1)}, u32[]{:S(2)}) %copy-start.2) | copy-done | bytes 131096
  11.4 0.0 copy-start.3
  11.4 0.7 copy-done.3
  12.1 0.0 copy-start.4
  12.1 0.7 copy-done.4
  12.8 0.0 copy-start.5
  12.8 0.7 copy-done.5
  13.5 0.7 shard_map.93
  14.2 0.0 collective-permute-done.prev
  14.2 7.4 %collective-permute-done.1.nxt = bf16[192,512]{1,0:T(8,128)(2,1)S(1)} collective-permute-done((bf16[192,512]{1,0:T(8,128)(2,1)S(1)}, bf16[192,512]{1,0:T(8,128)(2,1)S(1)}, u32[]{:S(2)}, u32[]{:S(2)}) %collective-permute-start.1) | collective-permute-done | bytes 196640 | tf_op jit(solution)/shard_map/ppermute | solution.py:277
  21.6 3.9 %shard_map.95 = (bf16[128,512]{1,0:T(8,128)(2,1)}, bf16[144,1536]{1,0:T(8,128)(2,1)S(1)}, bf16[144,1536]{1,0:T(8,128)(2,1)S(1)}) custom-call(f32[128,1]{1,0:T(8,128)S(1)} %get-tuple-element.18.own_valid, bf16[192,512]{1,0:T(8,128)(2,1)S(1)} %collective-permute-done.prev, bf16[192,512]{1,0:T(8,128)(2,1)S(1)} %collective-permute-done.1.nxt, ...), custom_call_target="tpu_custom_call" | custom-call | tf_op jit(solution)/shard_map/pallas_call | solution.py:284
  25.5 2.5 %collective-permute-start.2 = (bf16[144,1536]{1,0:T(8,128)(2,1)S(1)}, bf16[144,1536]{1,0:T(8,128)(2,1)S(1)}, u32[]{:S(2)}, u32[]{:S(2)}) collective-permute-start(bf16[144,1536]{1,0:T(8,128)(2,1)S(1)} %get-tuple-element.28), channel_id=1, source_target_pairs={{0,1},{1,0},{2,3},{3,2},{4,5},{5,4},{6,7},{7,6},{8,9},{9,8},{10,11... | collective-permute-start | bytes 1327112 | tf_op jit(solution)/shard_map/ppermute | solution.py:293
  28.1 1.4 %collective-permute-done.2.recv = bf16[144,1536]{1,0:T(8,128)(2,1)S(1)} collective-permute-done((bf16[144,1536]{1,0:T(8,128)(2,1)S(1)}, bf16[144,1536]{1,0:T(8,128)(2,1)S(1)}, u32[]{:S(2)}, u32[]{:S(2)}) %collective-permute-start.2) | collective-permute-done | bytes 442400 | tf_op jit(solution)/shard_map/ppermute | solution.py:293
  29.5 1.1 %shard_map.96 = bf16[8,528,128]{2,1,0:T(8,128)(2,1)S(1)} custom-call(bf16[144,1536]{1,0:T(8,128)(2,1)S(1)} %get-tuple-element.27.keep, bf16[144,1536]{1,0:T(8,128)(2,1)S(1)} %collective-permute-done.2.recv), custom_call_target="tpu_custom_call" | custom-call | tf_op jit(solution)/shard_map/pallas_call | solution.py:294
  30.5 19.4 %all_to_all.10.recv = bf16[8,528,128]{2,1,0:T(8,128)(2,1)S(1)} all-to-all(bf16[8,528,128]{2,1,0:T(8,128)(2,1)S(1)} %shard_map.96), channel_id=1, replica_groups=mesh['z'=8,'x'=4,'yh'=4,'yl'=2,'c'=2] {'x','yl'}, dimensions={0} | all-to-all | bytes 2162688 | tf_op jit(solution)/shard_map/all_to_all | solution.py:295
  49.9 0.4 shard_map.97
  50.4 27.7 %all_to_all.11.recv = bf16[32,32,128]{2,1,0:T(8,128)(2,1)S(1)} all-to-all(bf16[32,32,128]{2,1,0:T(8,128)(2,1)S(1)} %shard_map.97), channel_id=1, replica_groups=mesh['z'=8,'x'=4,'yh'=4,'yl'=2,'c'=2] {'z','yh'}, dimensions={0} | all-to-all | bytes 524288 | tf_op jit(solution)/shard_map/all_to_all | solution.py:297
  78.1 8.5 %all-gather = f32[128,128]{1,0:T(8,128)S(1)} all-gather(f32[32,128]{1,0:T(8,128)S(1)} %shard_map.98), channel_id=2, replica_groups=mesh['z'=8,'x'=4,'yh'=4,'yl'=2,'c'=2] {'yl','c'}, dimensions={0}, use_global_device_ids=true | all-gather | bytes 81920 | tf_op jit(solution)/shard_map/all_gather | solution.py:299
  86.7 0.6 shard_map.99
  (1 shorter events, 0.0 us)
Async XLA Ops:
  1.7 12.5 %collective-permute-start = (bf16[192,512]{1,0:T(8,128)(2,1)S(1)}, bf16[192,512]{1,0:T(8,128)(2,1)S(1)}, u32[]{:S(2)}, u32[]{:S(2)}) collective-permute-start(bf16[192,512]{1,0:T(8,128)(2,1)S(1)} %get-tuple-element.19), channel_id=1, source_target_pairs={{0,4},{4,8},{8,12},{12,16},{16,20},{20,24},{24,28},{28,32},{32,36}... | collective-permute-start | bytes 589832 | tf_op jit(solution)/shard_map/ppermute | solution.py:276
  6.7 14.9 %collective-permute-start.1 = (bf16[192,512]{1,0:T(8,128)(2,1)S(1)}, bf16[192,512]{1,0:T(8,128)(2,1)S(1)}, u32[]{:S(2)}, u32[]{:S(2)}) collective-permute-start(bf16[192,512]{1,0:T(8,128)(2,1)S(1)} %get-tuple-element.20), channel_id=1, source_target_pairs={{4,0},{8,4},{12,8},{16,12},{20,16},{24,20},{28,24},{32,28},{36,32}... | collective-permute-start | bytes 589832 | tf_op jit(solution)/shard_map/ppermute | solution.py:277
  8.0 1.6 %copy-start = (bf16[2,512,1024]{2,1,0:T(8,128)(2,1)S(1)}, bf16[2,512,1024]{2,1,0:T(8,128)(2,1)}, u32[]{:S(2)}) copy-start(bf16[2,512,1024]{2,1,0:T(8,128)(2,1)} %proj.1) | copy-start | bytes 6291460
  9.6 0.9 %copy-start.1 = (bf16[1,128,512]{2,1,0:T(8,128)(2,1)S(1)}, bf16[1,128,512]{2,1,0:T(8,128)(2,1)}, u32[]{:S(2)}) copy-start(bf16[1,128,512]{2,1,0:T(8,128)(2,1)} %param.6) | copy-start | bytes 393220
  10.5 0.9 %copy-start.2 = (bf16[1,128,512]{2,1,0:T(8,128)(2,1)S(1)}, bf16[1,128,512]{2,1,0:T(8,128)(2,1)}, u32[]{:S(2)}) copy-start(bf16[1,128,512]{2,1,0:T(8,128)(2,1)} %param.7) | copy-start | bytes 393220
  11.4 0.7 copy-start.3
  12.1 0.7 copy-start.4
  12.8 0.7 copy-start.5
  25.5 3.9 %collective-permute-start.2 = (bf16[144,1536]{1,0:T(8,128)(2,1)S(1)}, bf16[144,1536]{1,0:T(8,128)(2,1)S(1)}, u32[]{:S(2)}, u32[]{:S(2)}) collective-permute-start(bf16[144,1536]{1,0:T(8,128)(2,1)S(1)} %get-tuple-element.28), channel_id=1, source_target_pairs={{0,1},{1,0},{2,3},{3,2},{4,5},{5,4},{6,7},{7,6},{8,9},{9,8},{10,11... | collective-permute-start | bytes 1327112 | tf_op jit(solution)/shard_map/ppermute | solution.py:293

commit v4 on v3

--- a/solution.py
+++ b/solution.py
@@ -21,12 +21,13 @@
 ACT = 144
 
 
-def gelu_and_slope(x):
+def gelu_and_slope(x, with_slope=True):
     x2 = x * x
-    t = jnp.tanh(G0 * x * (1.0 + G1 * x2))
-    cdf = 0.5 + 0.5 * t
-    slope = cdf + (0.5 * G0) * x * (1.0 - t * t) * (1.0 + (3.0 * G1) * x2)
-    return x * cdf, slope
+    cdf = 0.5 + 0.5 * jnp.tanh(x * (G0 + (G0 * G1) * x2))
+    hid = x * cdf
+    if not with_slope:
+        return hid, None
+    return hid, cdf + hid * (1.0 - cdf) * (2.0 * G0 + (6.0 * G0 * G1) * x2)
 
 
 def sigmoid(x):
@@ -72,8 +73,7 @@
 
     def rows(base):
         ref, at = ((prev, base), (tok, base - 128), (nxt, base - 256))[base // 128]
-        v = ref[at:at + DIL, :].astype(F32)
-        return v if ref is tok else jnp.where(v[:, 0:1] < 0.5 * MARK, v, 0.0)
+        return ref[at:at + DIL, :].astype(F32)
 
     def cot_rows(base):
         if base < 128:
@@ -93,7 +93,7 @@
 
     def norm(v, valid, gain):
         inv = lax.rsqrt(jnp.sum(v * v, axis=-1, keepdims=True) * (1.0 / C) + EPS)
-        return inv, v * inv * gain * valid
+        return inv, v * (inv * valid) * gain
 
     def tap(layer, k):
         return taps[k, layer:layer + 1, :]
@@ -104,12 +104,14 @@
 
     for c in range(12):
         inv, normed = norm(rows(c * DIL), valid_of[c], gains[0:1, :])
-        i0[c * DIL:(c + 1) * DIL, :] = inv
+        if 4 <= c < 8:
+            i0[c * DIL:(c + 1) * DIL, :] = inv
         n0[c * DIL:(c + 1) * DIL, :] = normed
     for c in range(1, 11):
-        hid, slope = gelu_and_slope(conv(n0, c * DIL, 0))
+        hid, slope = gelu_and_slope(conv(n0, c * DIL, 0), 3 <= c < 9)
         h0[(c - 1) * DIL:c * DIL, :] = hid.astype(BF16)
-        g0[(c - 1) * DIL:c * DIL, :] = slope
+        if 3 <= c < 9:
+            g0[(c - 1) * DIL:c * DIL, :] = slope
     ab0[...] = dot(h0[...], proj[0], ((1,), (0,)))
     for c in range(1, 11):
         at = slice((c - 1) * DIL, c * DIL)
@@ -117,11 +119,12 @@
         gate = sigmoid(ab0[at, C:2 * C])
         both = first * gate
         nx = (rows(c * DIL) + valid_of[c] * both).astype(BF16).astype(F32)
-        ab0[at, 0:C] = gate
-        ab0[at, C:2 * C] = both * (1.0 - gate)
         inv, normed = norm(nx, valid_of[c], gains[1:2, :])
-        x1[at, :] = nx
-        i1[at, :] = inv
+        if 3 <= c < 9:
+            ab0[at, 0:C] = gate
+            ab0[at, C:2 * C] = both * (1.0 - gate)
+            x1[at, :] = nx
+            i1[at, :] = inv
         n1[at, :] = normed
     for c in range(2, 10):
         hid, slope = gelu_and_slope(conv(n1, (c - 1) * DIL, 1))
@@ -135,10 +138,7 @@
         bg = valid_of[c] * cot_rows(c * DIL) * gate
         dp1[at, 0:C] = bg.astype(BF16)
         dp1[at, C:2 * C] = (bg * first * (1.0 - gate)).astype(BF16)
-    dh1[...] = dot(dp1[...], proj[1], ((1,), (1,)))
-    for c in range(8):
-        at = slice(c * DIL, (c + 1) * DIL)
-        dh1[at, :] = dh1[at, :] * g1[at, :]
+    dh1[...] = dot(dp1[...], proj[1], ((1,), (1,))) * g1[...]
 
     def back(dref, c_off, layer, c, sref_rows, inv, valid, gain):
         at = c_off
@@ -181,10 +181,7 @@
 
     put(1, h1[64:192, :], dp1[64:192, :], acc)
 
-    dh0[...] = dot(dp0[...], proj[0], ((1,), (1,)))
-    for c in range(6):
-        at = slice(c * DIL, (c + 1) * DIL)
-        dh0[at, :] = dh0[at, :] * g0[(c + 2) * DIL:(c + 3) * DIL, :]
+    dh0[...] = dot(dp0[...], proj[0], ((1,), (1,))) * g0[64:256, :]
     acc = [jnp.zeros((8, C), F32) for _ in range(4)]
     for c in range(4, 8):
         delta, qs = back(dh0, (c - 3) * DIL, 0, c, rows(c * DIL), i0[c * DIL:(c + 1) * DIL, :],
@@ -200,15 +197,19 @@
     send[...] = act[1 - core]
 
 
-def terms(keep, recv, out):
+def own_terms(keep, pick, mine):
     q = lax.broadcasted_iota(jnp.int32, (C, 1), 0)
     ch = ((q >> 3) & 7) << 6 | ((q >> 7) & 3) << 4 | ((q >> 1) & 3) << 2 | ((q >> 6) & 1) << 1 | (q & 1)
-    pick = (ch == lax.broadcasted_iota(jnp.int32, (C, C), 1)).astype(F32).astype(BF16)
-    ha = dot(pick, keep[0:128, 0:C], ((1,), (1,))).astype(BF16)
-    hb = dot(pick, recv[0:128, 0:C], ((1,), (1,))).astype(BF16)
+    pick[...] = (ch == lax.broadcasted_iota(jnp.int32, (C, C), 1)).astype(F32).astype(BF16)
+    ha = dot(pick[...], keep[0:128, 0:C], ((1,), (1,))).astype(BF16)
+    mine[...] = dot(ha, keep[0:128, C:3 * C], ((1,), (0,)))
+
+
+def terms(keep, recv, pick, mine, out):
+    hb = dot(pick[...], recv[0:128, 0:C], ((1,), (1,))).astype(BF16)
     for j in range(8):
-        cols = slice(C + j * 128, C + (j + 1) * 128)
-        t = dot(ha, keep[0:128, cols], ((1,), (0,))) + dot(hb, recv[0:128, cols], ((1,), (0,)))
+        cols = slice(j * 128, (j + 1) * 128)
+        t = mine[:, cols] + dot(hb, recv[0:128, C + j * 128:C + (j + 1) * 128], ((1,), (0,)))
         out[:, j * 64:(j + 1) * 64, :] = t.astype(BF16).reshape(8, 64, 128)
     small = (keep[128:ACT, 0:C].astype(F32) + keep[128:ACT, C:2 * C].astype(F32)
              + recv[128:ACT, 0:C].astype(F32) + recv[128:ACT, C:2 * C].astype(F32))
@@ -266,22 +267,10 @@
     )
 
 
-def shards(tokens, cotangent, gaps, taps, gains, proj):
-    tok, cot = tokens[0], cotangent[0]
-    n = 128
+def main(*args):
     s = jax.ShapeDtypeStruct
     v = pltpu.VMEM
-    far = [pltpu.with_memory_space_constraint(a, pltpu.HBM) for a in (gaps, tok, cot)]
-    up, down = call(pack, "svv", [s((192, C), BF16), s((192, C), BF16)], mib=48)(*far)
-    prev = lax.ppermute(up, SEQ, [(i, i + 1) for i in range(n - 1)])
-    nxt = lax.ppermute(down, SEQ, [(i + 1, i) for i in range(n - 1)])
-    near_args = call(
-        warm,
-        "svvvvv",
-        [s((128, 1), F32), s((128, C), BF16), s((128, C), BF16), s((3, 2, C), F32), s((2, C), F32),
-         s((2, C, 2 * C), BF16)],
-    )(gaps, tok, cot, jnp.transpose(taps, (1, 0, 2)), gains, proj)
-    tokens_grad, keep, send = call(
+    return call(
         body,
         "vvvvvvvv",
         [s((128, C), BF16), s((ACT, 3 * C), BF16), s((ACT, 3 * C), BF16)],
@@ -289,9 +278,29 @@
          v((320, C), F32), v((320, C), F32), v((320, 1), F32), v((256, C), F32), v((256, C), BF16),
          v((256, 2 * C), F32), v((256, 2 * C), BF16), v((256, C), F32), v((128, C), F32),
          v((192, 2 * C), BF16), v((192, C), F32), v((2, ACT, 3 * C), BF16)],
-    )(near_args[0], prev, nxt, *near_args[1:])
+    )(*args)
+
+
+def shards(tokens, cotangent, gaps, taps, gains, proj):
+    tok, cot = tokens[0], cotangent[0]
+    n = 128
+    s = jax.ShapeDtypeStruct
+    far = [pltpu.with_memory_space_constraint(a, pltpu.HBM) for a in (gaps, tok, cot)]
+    up, down = call(pack, "svv", [s((192, C), BF16), s((192, C), BF16)], mib=48)(*far)
+    prev = lax.ppermute(up, SEQ, [(i, i + 1) for i in range(n - 1)])
+    nxt = lax.ppermute(down, SEQ, [(i + 1, i) for i in range(n - 1)])
+    here = [jnp.transpose(taps, (1, 0, 2)), gains, proj]
+    here = far + [pltpu.with_memory_space_constraint(a, pltpu.HBM) for a in here]
+    near_args = call(
+        warm,
+        "svvvvv",
+        [s((128, 1), F32), s((128, C), BF16), s((128, C), BF16), s((3, 2, C), F32), s((2, C), F32),
+         s((2, C, 2 * C), BF16)],
+    )(*here)
+    tokens_grad, keep, send = main(near_args[0], prev, nxt, *near_args[1:])
     recv = lax.ppermute(send, "c", [(0, 1), (1, 0)])
-    part = call(terms, "vv", s((8, 528, 128), BF16))(keep, recv)
+    pick, mine = call(own_terms, "v", [s((C, C), BF16), s((C, 2 * C), F32)])(keep)
+    part = call(terms, "vvvv", s((8, 528, 128), BF16))(keep, recv, pick, mine)
     part = lax.all_to_all(part, NEAR, 0, 0, tiled=True)
     part = call(first_sum, "v", s((32, 32, 128), BF16))(part)
     part = lax.all_to_all(part, FAR, 0, 0, tiled=True)

time: 87.7 us -> 87.4 us (level)
  local copies, waits for them, and re-layouts: 5.44 us -> 0 us
  waiting for transfers between devices: 8.8 us -> 12.1 us
  Pallas kernels: 7.83 us -> 9.74 us
    unnamed x12 -> x0, local copies, waits for them, and re-layouts: 5.44 us -> none
    ppermute x1, waiting for transfers between devices: 7.4 us -> 11.6 us  [shards(): nxt = lax.ppermute(down, SEQ, [(i + 1, i) for i in range(n - 1)])]
    pallas_call x1, Pallas kernels: 0.7 us -> 1.95 us  [shards(): call(warm, 'svvvvv', [s((128, 1), F32), s((128, C), BF16), s((128, C), BF...]
    ppermute x1, waiting for transfers between devices: 1.4 us -> 0.51 us  [shards(): recv = lax.ppermute(send, 'c', [(0, 1), (1, 0)])]
    pallas_call x2 -> x3, Pallas kernels: 5.01 us -> 5.67 us  [the longest x1 3.89 us: main(): call(body, 'vvvvvvvv', [s((128, C), BF16), s((ACT, 3 * C), BF16), s((ACT,...]
  transfers between devices with their start and end apart: 3 -> 3, of which waited for: 2 -> 2; matrix products, arithmetic and copies ran while one was open for 0% -> 0% of each run, Pallas kernels for 1% -> 3%
where the time goes in v4:
time: 87.4 us; the launch traced here: 87.1 us
  blocking collectives  55.7 us (64%)
  waiting for transfers between devices  12.1 us (14%)
  Pallas kernels  9.74 us (11%)
  starting transfers between devices  8.83 us (10%)
    all_to_all x1, blocking collectives, shards(): part = lax.all_to_all(part, FAR, 0, 0, tiled=True)  27.7 us
    all_to_all x1, blocking collectives, shards(): part = lax.all_to_all(part, NEAR, 0, 0, tiled=True)  19.4 us
    ppermute x1, waiting for transfers between devices, shards(): nxt = lax.ppermute(down, SEQ, [(i + 1, i) for i in range(n - 1)])  11.6 us
    all_gather x1, blocking collectives, shards(): part = lax.all_gather(part, HAP, axis=0)  8.53 us
    ppermute x1, starting transfers between devices, shards(): prev = lax.ppermute(up, SEQ, [(i, i + 1) for i in range(n - 1)])  5.05 us
    pallas_call x1, Pallas kernels, main(): call(body, 'vvvvvvvv', [s((128, C), BF16), s((ACT, 3 * C), BF16), s((ACT,...  3.89 us
    ppermute x1, starting transfers between devices, shards(): recv = lax.ppermute(send, 'c', [(0, 1), (1, 0)])  2.48 us
    pallas_call x1, Pallas kernels, shards(): call(warm, 'svvvvv', [s((128, 1), F32), s((128, C), BF16), s((128, C), BF...  1.95 us
  transfers between devices with their start and end apart: 3, of which 2 were waited for; matrix products, arithmetic and copies ran while one was open for 0% of the time, Pallas kernels for 3%

profile of v4, /device:TPU:1, one launch (start us, length us, event | category | flops | bytes accessed | tf_op | source)
XLA Modules:
  0.0 87.1 jit_solution(8639302904750942805)
XLA Ops:
  0.6 1.0 %shard_map.94 = (bf16[192,512]{1,0:T(8,128)(2,1)S(1)}, bf16[192,512]{1,0:T(8,128)(2,1)S(1)}) custom-call(s32[1,2]{1,0:T(1,128)} %gaps.3, bf16[128,512]{1,0:T(8,128)(2,1)} %bitcast.7, bf16[128,512]{1,0:T(8,128)(2,1)} %bitcast.9), custom_call_target="tpu_custom_call" | custom-call | tf_op jit(solution)/shard_map/pallas_call | solution.py:289
  1.7 5.1 %collective-permute-start = (bf16[192,512]{1,0:T(8,128)(2,1)S(1)}, bf16[192,512]{1,0:T(8,128)(2,1)S(1)}, u32[]{:S(2)}, u32[]{:S(2)}) collective-permute-start(bf16[192,512]{1,0:T(8,128)(2,1)S(1)} %get-tuple-element.21), channel_id=1, source_target_pairs={{0,4},{4,8},{8,12},{12,16},{16,20},{20,24},{24,28},{28,32},{32,36}... | collective-permute-start | bytes 589832 | tf_op jit(solution)/shard_map/ppermute | solution.py:290
  6.7 1.3 %collective-permute-start.1 = (bf16[192,512]{1,0:T(8,128)(2,1)S(1)}, bf16[192,512]{1,0:T(8,128)(2,1)S(1)}, u32[]{:S(2)}, u32[]{:S(2)}) collective-permute-start(bf16[192,512]{1,0:T(8,128)(2,1)S(1)} %get-tuple-element.22), channel_id=1, source_target_pairs={{4,0},{8,4},{12,8},{16,12},{20,16},{24,20},{28,24},{32,28},{36,32}... | collective-permute-start | bytes 589832 | tf_op jit(solution)/shard_map/ppermute | solution.py:291
  8.0 1.9 %shard_map.93 = (f32[128,1]{1,0:T(8,128)S(1)}, bf16[128,512]{1,0:T(8,128)(2,1)S(1)}, bf16[128,512]{1,0:T(8,128)(2,1)S(1)}, f32[3,2,512]{2,1,0:T(2,128)S(1)}, f32...) custom-call(s32[1,2]{1,0:T(1,128)} %gaps.3, bf16[128,512]{1,0:T(8,128)(2,1)} %bitcast.8, bf16[128,512]{1,0:T(8,128)(2,1)} %bitcast.10, ...), custom_call_target="tpu_custom_call" | custom-call | tf_op jit(solution)/shard_map/pallas_call | solution.py:294
  10.0 0.0 collective-permute-done.prev
  10.0 11.6 %collective-permute-done.1.nxt = bf16[192,512]{1,0:T(8,128)(2,1)S(1)} collective-permute-done((bf16[192,512]{1,0:T(8,128)(2,1)S(1)}, bf16[192,512]{1,0:T(8,128)(2,1)S(1)}, u32[]{:S(2)}, u32[]{:S(2)}) %collective-permute-start.1) | collective-permute-done | bytes 196640 | tf_op jit(solution)/shard_map/ppermute | solution.py:291
  21.6 3.9 %shard_map.95 = (bf16[128,512]{1,0:T(8,128)(2,1)}, bf16[144,1536]{1,0:T(8,128)(2,1)S(1)}, bf16[144,1536]{1,0:T(8,128)(2,1)S(1)}) custom-call(f32[128,1]{1,0:T(8,128)S(1)} %get-tuple-element.20.own_valid, bf16[192,512]{1,0:T(8,128)(2,1)S(1)} %collective-permute-done.prev, bf16[192,512]{1,0:T(8,128)(2,1)S(1)} %collective-permute-done.1.nxt, ...), custom_call_target="tpu_custom_call" | custom-call | tf_op jit(solution)/shard_map/pallas_call | solution.py:273
  25.5 2.5 %collective-permute-start.2 = (bf16[144,1536]{1,0:T(8,128)(2,1)S(1)}, bf16[144,1536]{1,0:T(8,128)(2,1)S(1)}, u32[]{:S(2)}, u32[]{:S(2)}) collective-permute-start(bf16[144,1536]{1,0:T(8,128)(2,1)S(1)} %get-tuple-element.30), channel_id=1, source_target_pairs={{0,1},{1,0},{2,3},{3,2},{4,5},{5,4},{6,7},{7,6},{8,9},{9,8},{10,11... | collective-permute-start | bytes 1327112 | tf_op jit(solution)/shard_map/ppermute | solution.py:301
  28.0 0.9 %shard_map.96 = (bf16[512,512]{1,0:T(8,128)(2,1)S(1)}, f32[512,1024]{1,0:T(8,128)S(1)}) custom-call(bf16[144,1536]{1,0:T(8,128)(2,1)S(1)} %get-tuple-element.29.keep), custom_call_target="tpu_custom_call" | custom-call | tf_op jit(solution)/shard_map/pallas_call | solution.py:302
  28.9 0.5 collective-permute-done.2.recv
  29.4 0.9 %shard_map.97 = bf16[8,528,128]{2,1,0:T(8,128)(2,1)S(1)} custom-call(bf16[144,1536]{1,0:T(8,128)(2,1)S(1)} %get-tuple-element.29.keep, bf16[144,1536]{1,0:T(8,128)(2,1)S(1)} %collective-permute-done.2.recv, bf16[512,512]{1,0:T(8,128)(2,1)S(1)} %get-tuple-element.31.pick, f32[512,1024]{1,0:T(8,128)S(1)} %get-tuple-element.32.mine), custom_call_target="tpu_custom_call" | custom-call | tf_op jit(solution)/shard_map/pallas_call | solution.py:303
  30.3 19.4 %all_to_all.10.recv = bf16[8,528,128]{2,1,0:T(8,128)(2,1)S(1)} all-to-all(bf16[8,528,128]{2,1,0:T(8,128)(2,1)S(1)} %shard_map.97), channel_id=1, replica_groups=mesh['z'=8,'x'=4,'yh'=4,'yl'=2,'c'=2] {'x','yl'}, dimensions={0} | all-to-all | bytes 2162688 | tf_op jit(solution)/shard_map/all_to_all | solution.py:304
  49.7 0.4 shard_map.98
  50.1 27.7 %all_to_all.11.recv = bf16[32,32,128]{2,1,0:T(8,128)(2,1)S(1)} all-to-all(bf16[32,32,128]{2,1,0:T(8,128)(2,1)S(1)} %shard_map.98), channel_id=1, replica_groups=mesh['z'=8,'x'=4,'yh'=4,'yl'=2,'c'=2] {'z','yh'}, dimensions={0} | all-to-all | bytes 524288 | tf_op jit(solution)/shard_map/all_to_all | solution.py:306
  77.9 8.5 %all-gather = f32[128,128]{1,0:T(8,128)S(1)} all-gather(f32[32,128]{1,0:T(8,128)S(1)} %shard_map.99), channel_id=2, replica_groups=mesh['z'=8,'x'=4,'yh'=4,'yl'=2,'c'=2] {'yl','c'}, dimensions={0}, use_global_device_ids=true | all-gather | bytes 81920 | tf_op jit(solution)/shard_map/all_gather | solution.py:308
  86.4 0.6 shard_map.100
  (1 shorter events, 0.0 us)
Async XLA Ops:
  1.7 8.3 %collective-permute-start = (bf16[192,512]{1,0:T(8,128)(2,1)S(1)}, bf16[192,512]{1,0:T(8,128)(2,1)S(1)}, u32[]{:S(2)}, u32[]{:S(2)}) collective-permute-start(bf16[192,512]{1,0:T(8,128)(2,1)S(1)} %get-tuple-element.21), channel_id=1, source_target_pairs={{0,4},{4,8},{8,12},{12,16},{16,20},{20,24},{24,28},{28,32},{32,36}... | collective-permute-start | bytes 589832 | tf_op jit(solution)/shard_map/ppermute | solution.py:290
  6.7 14.9 %collective-permute-start.1 = (bf16[192,512]{1,0:T(8,128)(2,1)S(1)}, bf16[192,512]{1,0:T(8,128)(2,1)S(1)}, u32[]{:S(2)}, u32[]{:S(2)}) collective-permute-start(bf16[192,512]{1,0:T(8,128)(2,1)S(1)} %get-tuple-element.22), channel_id=1, source_target_pairs={{4,0},{8,4},{12,8},{16,12},{20,16},{24,20},{28,24},{32,28},{36,32}... | collective-permute-start | bytes 589832 | tf_op jit(solution)/shard_map/ppermute | solution.py:291
  25.5 3.9 %collective-permute-start.2 = (bf16[144,1536]{1,0:T(8,128)(2,1)S(1)}, bf16[144,1536]{1,0:T(8,128)(2,1)S(1)}, u32[]{:S(2)}, u32[]{:S(2)}) collective-permute-start(bf16[144,1536]{1,0:T(8,128)(2,1)S(1)} %get-tuple-element.30), channel_id=1, source_target_pairs={{0,1},{1,0},{2,3},{3,2},{4,5},{5,4},{6,7},{7,6},{8,9},{9,8},{10,11... | collective-permute-start | bytes 1327112 | tf_op jit(solution)/shard_map/ppermute | solution.py:301

commit v5 on v4

--- a/solution.py
+++ b/solution.py
@@ -11,9 +11,9 @@
 EPS = 1e-06
 F32 = jnp.float32
 BF16 = jnp.bfloat16
-NEAR = ("x", "yl")
-FAR = ("z", "yh")
-SEQ = ("z", "x", "yh")
+NEAR = ("zl", "x", "yl")
+FAR = ("zh", "yh")
+SEQ = ("zh", "zl", "x", "yh")
 HAP = ("yl", "c")
 G0 = 0.7978845608028654
 G1 = 0.044715
@@ -69,7 +69,7 @@
          n0, i0, g0, h0, ab0, x1, n1, i1, g1, h1, po1, dp1, dh1, gr1, dp0, dh0, act):
     core = lax.axis_index("c")
     place_in_seq = sum(lax.axis_index(a) for a in SEQ)
-    inner = (place_in_seq > 0, None, place_in_seq < 13)
+    inner = (place_in_seq > 0, None, place_in_seq < 10)
 
     def rows(base):
         ref, at = ((prev, base), (tok, base - 128), (nxt, base - 256))[base // 128]
@@ -199,7 +199,8 @@
 
 def own_terms(keep, pick, mine):
     q = lax.broadcasted_iota(jnp.int32, (C, 1), 0)
-    ch = ((q >> 3) & 7) << 6 | ((q >> 7) & 3) << 4 | ((q >> 1) & 3) << 2 | ((q >> 6) & 1) << 1 | (q & 1)
+    ch = (((q >> 3) & 3) << 7 | ((q >> 8) & 1) << 6 | ((q >> 6) & 3) << 4 | ((q >> 1) & 3) << 2
+          | ((q >> 5) & 1) << 1 | (q & 1))
     pick[...] = (ch == lax.broadcasted_iota(jnp.int32, (C, C), 1)).astype(F32).astype(BF16)
     ha = dot(pick[...], keep[0:128, 0:C], ((1,), (1,))).astype(BF16)
     mine[...] = dot(ha, keep[0:128, C:3 * C], ((1,), (0,)))
@@ -210,32 +211,32 @@
     for j in range(8):
         cols = slice(j * 128, (j + 1) * 128)
         t = mine[:, cols] + dot(hb, recv[0:128, C + j * 128:C + (j + 1) * 128], ((1,), (0,)))
-        out[:, j * 64:(j + 1) * 64, :] = t.astype(BF16).reshape(8, 64, 128)
+        out[:, j * 32:(j + 1) * 32, :] = t.astype(BF16).reshape(16, 32, 128)
     small = (keep[128:ACT, 0:C].astype(F32) + keep[128:ACT, C:2 * C].astype(F32)
              + recv[128:ACT, 0:C].astype(F32) + recv[128:ACT, C:2 * C].astype(F32))
     tile = jnp.concatenate(
         [small[r:r + 1, 128 * q:128 * (q + 1)] for r in range(4) for q in range(4)], axis=0).astype(BF16)
-    for g in range(8):
-        out[g, 512:528, :] = tile
+    for g in range(16):
+        out[g, 256:272, :] = tile
 
 
 def first_sum(recv, out):
     total = recv[0].astype(F32)
-    for i in range(1, 8):
+    for i in range(1, 16):
         total += recv[i].astype(F32)
-    p = lax.broadcasted_iota(jnp.int32, (C, 1), 0)
-    src = ((p >> 1) & 7) << 6 | (p >> 4) << 1 | (p & 1)
-    pick = (src == lax.broadcasted_iota(jnp.int32, (C, C), 1)).astype(F32).astype(BF16)
-    moved = dot(pick, total[0:512, :].astype(BF16), ((1,), (0,))).astype(BF16)
-    out[:, 0:16, :] = moved.reshape(32, 16, 128)
-    tile = total[512:528, :].astype(BF16)
-    for d in range(32):
+    p = lax.broadcasted_iota(jnp.int32, (256, 1), 0)
+    src = ((p >> 1) & 7) << 5 | (p >> 4) << 1 | (p & 1)
+    pick = (src == lax.broadcasted_iota(jnp.int32, (256, 256), 1)).astype(F32).astype(BF16)
+    moved = dot(pick, total[0:256, :].astype(BF16), ((1,), (0,))).astype(BF16)
+    out[:, 0:16, :] = moved.reshape(16, 16, 128)
+    tile = total[256:272, :].astype(BF16)
+    for d in range(16):
         out[d, 16:32, :] = tile
 
 
 def second_sum(recv, out):
     total = recv[0].astype(F32)
-    for i in range(1, 32):
+    for i in range(1, 16):
         total += recv[i].astype(F32)
     out[...] = total
 
@@ -300,9 +301,9 @@
     tokens_grad, keep, send = main(near_args[0], prev, nxt, *near_args[1:])
     recv = lax.ppermute(send, "c", [(0, 1), (1, 0)])
     pick, mine = call(own_terms, "v", [s((C, C), BF16), s((C, 2 * C), F32)])(keep)
-    part = call(terms, "vvvv", s((8, 528, 128), BF16))(keep, recv, pick, mine)
+    part = call(terms, "vvvv", s((16, 272, 128), BF16))(keep, recv, pick, mine)
     part = lax.all_to_all(part, NEAR, 0, 0, tiled=True)
-    part = call(first_sum, "v", s((32, 32, 128), BF16))(part)
+    part = call(first_sum, "v", s((16, 32, 128), BF16))(part)
     part = lax.all_to_all(part, FAR, 0, 0, tiled=True)
     part = call(second_sum, "v", s((32, 128), F32))(part)
     part = lax.all_gather(part, HAP, axis=0)
@@ -313,7 +314,7 @@
 
 
 def solution(mesh):
-    fine = Mesh(mesh.devices.reshape(8, 4, 4, 2, 2), ("z", "x", "yh", "yl", "c"))
+    fine = Mesh(mesh.devices.reshape(4, 2, 4, 4, 2, 2), ("zh", "zl", "x", "yh", "yl", "c"))
     return jax.shard_map(
         shards,
         mesh=fine,

time: 87.4 us -> 87.8 us (level)
    all_to_all x1, blocking collectives: 19.4 us -> 21.9 us  [shards(): part = lax.all_to_all(part, NEAR, 0, 0, tiled=True)]
    all_to_all x1, blocking collectives: 27.7 us -> 25.8 us  [shards(): part = lax.all_to_all(part, FAR, 0, 0, tiled=True)]
where the time goes in v5:
time: 87.8 us; the launch traced here: 87.5 us
  blocking collectives  56.3 us (64%)
  waiting for transfers between devices  12.1 us (14%)
  Pallas kernels  9.62 us (11%)
  starting transfers between devices  8.84 us (10%)
    all_to_all x1, blocking collectives, shards(): part = lax.all_to_all(part, FAR, 0, 0, tiled=True)  25.8 us
    all_to_all x1, blocking collectives, shards(): part = lax.all_to_all(part, NEAR, 0, 0, tiled=True)  21.9 us
    ppermute x1, waiting for transfers between devices, shards(): nxt = lax.ppermute(down, SEQ, [(i + 1, i) for i in range(n - 1)])  11.6 us
    all_gather x1, blocking collectives, shards(): part = lax.all_gather(part, HAP, axis=0)  8.53 us
    ppermute x1, starting transfers between devices, shards(): prev = lax.ppermute(up, SEQ, [(i, i + 1) for i in range(n - 1)])  5.05 us
    pallas_call x1, Pallas kernels, main(): call(body, 'vvvvvvvv', [s((128, C), BF16), s((ACT, 3 * C), BF16), s((ACT,...  3.87 us
    ppermute x1, starting transfers between devices, shards(): recv = lax.ppermute(send, 'c', [(0, 1), (1, 0)])  2.5 us
    pallas_call x1, Pallas kernels, shards(): call(warm, 'svvvvv', [s((128, 1), F32), s((128, C), BF16), s((128, C), BF...  1.95 us
  transfers between devices with their start and end apart: 3, of which 2 were waited for; matrix products, arithmetic and copies ran while one was open for 0% of the time, Pallas kernels for 3%

profile of v5, /device:TPU:1, one launch (start us, length us, event | category | flops | bytes accessed | tf_op | source)
XLA Modules:
  0.0 87.5 jit_solution(7306327977740764351)
XLA Ops:
  0.6 1.0 %shard_map.94 = (bf16[192,512]{1,0:T(8,128)(2,1)S(1)}, bf16[192,512]{1,0:T(8,128)(2,1)S(1)}) custom-call(s32[1,2]{1,0:T(1,128)} %gaps.3, bf16[128,512]{1,0:T(8,128)(2,1)} %bitcast.7, bf16[128,512]{1,0:T(8,128)(2,1)} %bitcast.9), custom_call_target="tpu_custom_call" | custom-call | tf_op jit(solution)/shard_map/pallas_call | solution.py:290
  1.7 5.1 %collective-permute-start = (bf16[192,512]{1,0:T(8,128)(2,1)S(1)}, bf16[192,512]{1,0:T(8,128)(2,1)S(1)}, u32[]{:S(2)}, u32[]{:S(2)}) collective-permute-start(bf16[192,512]{1,0:T(8,128)(2,1)S(1)} %get-tuple-element.21), channel_id=1, source_target_pairs={{0,4},{4,8},{8,12},{12,16},{16,20},{20,24},{24,28},{28,32},{32,36}... | collective-permute-start | bytes 589832 | tf_op jit(solution)/shard_map/ppermute | solution.py:291
  6.7 1.3 %collective-permute-start.1 = (bf16[192,512]{1,0:T(8,128)(2,1)S(1)}, bf16[192,512]{1,0:T(8,128)(2,1)S(1)}, u32[]{:S(2)}, u32[]{:S(2)}) collective-permute-start(bf16[192,512]{1,0:T(8,128)(2,1)S(1)} %get-tuple-element.22), channel_id=1, source_target_pairs={{4,0},{8,4},{12,8},{16,12},{20,16},{24,20},{28,24},{32,28},{36,32}... | collective-permute-start | bytes 589832 | tf_op jit(solution)/shard_map/ppermute | solution.py:292
  8.0 1.9 %shard_map.93 = (f32[128,1]{1,0:T(8,128)S(1)}, bf16[128,512]{1,0:T(8,128)(2,1)S(1)}, bf16[128,512]{1,0:T(8,128)(2,1)S(1)}, f32[3,2,512]{2,1,0:T(2,128)S(1)}, f32...) custom-call(s32[1,2]{1,0:T(1,128)} %gaps.3, bf16[128,512]{1,0:T(8,128)(2,1)} %bitcast.8, bf16[128,512]{1,0:T(8,128)(2,1)} %bitcast.10, ...), custom_call_target="tpu_custom_call" | custom-call | tf_op jit(solution)/shard_map/pallas_call | solution.py:295
  10.0 0.0 collective-permute-done.prev
  10.0 11.6 %collective-permute-done.1.nxt = bf16[192,512]{1,0:T(8,128)(2,1)S(1)} collective-permute-done((bf16[192,512]{1,0:T(8,128)(2,1)S(1)}, bf16[192,512]{1,0:T(8,128)(2,1)S(1)}, u32[]{:S(2)}, u32[]{:S(2)}) %collective-permute-start.1) | collective-permute-done | bytes 196640 | tf_op jit(solution)/shard_map/ppermute | solution.py:292
  21.6 3.9 %shard_map.95 = (bf16[128,512]{1,0:T(8,128)(2,1)}, bf16[144,1536]{1,0:T(8,128)(2,1)S(1)}, bf16[144,1536]{1,0:T(8,128)(2,1)S(1)}) custom-call(f32[128,1]{1,0:T(8,128)S(1)} %get-tuple-element.20.own_valid, bf16[192,512]{1,0:T(8,128)(2,1)S(1)} %collective-permute-done.prev, bf16[192,512]{1,0:T(8,128)(2,1)S(1)} %collective-permute-done.1.nxt, ...), custom_call_target="tpu_custom_call" | custom-call | tf_op jit(solution)/shard_map/pallas_call | solution.py:274
  25.5 2.5 %collective-permute-start.2 = (bf16[144,1536]{1,0:T(8,128)(2,1)S(1)}, bf16[144,1536]{1,0:T(8,128)(2,1)S(1)}, u32[]{:S(2)}, u32[]{:S(2)}) collective-permute-start(bf16[144,1536]{1,0:T(8,128)(2,1)S(1)} %get-tuple-element.30), channel_id=1, source_target_pairs={{0,1},{1,0},{2,3},{3,2},{4,5},{5,4},{6,7},{7,6},{8,9},{9,8},{10,11... | collective-permute-start | bytes 1327112 | tf_op jit(solution)/shard_map/ppermute | solution.py:302
  28.0 0.9 %shard_map.96 = (bf16[512,512]{1,0:T(8,128)(2,1)S(1)}, f32[512,1024]{1,0:T(8,128)S(1)}) custom-call(bf16[144,1536]{1,0:T(8,128)(2,1)S(1)} %get-tuple-element.29.keep), custom_call_target="tpu_custom_call" | custom-call | tf_op jit(solution)/shard_map/pallas_call | solution.py:303
  28.9 0.5 collective-permute-done.2.recv
  29.4 0.9 %shard_map.97 = bf16[16,272,128]{2,1,0:T(8,128)(2,1)S(1)} custom-call(bf16[144,1536]{1,0:T(8,128)(2,1)S(1)} %get-tuple-element.29.keep, bf16[144,1536]{1,0:T(8,128)(2,1)S(1)} %collective-permute-done.2.recv, bf16[512,512]{1,0:T(8,128)(2,1)S(1)} %get-tuple-element.31.pick, f32[512,1024]{1,0:T(8,128)S(1)} %get-tuple-element.32.mine), custom_call_target="tpu_custom_call" | custom-call | tf_op jit(solution)/shard_map/pallas_call | solution.py:304
  30.3 21.9 %all_to_all.10.recv = bf16[16,272,128]{2,1,0:T(8,128)(2,1)S(1)} all-to-all(bf16[16,272,128]{2,1,0:T(8,128)(2,1)S(1)} %shard_map.97), channel_id=1, replica_groups=mesh['zh'=4,'zl'=2,'x'=4,'yh'=4,'yl'=2,'c'=2] {'zl','x','yl'}, dimensions={0} | all-to-all | bytes 2228224 | tf_op jit(solution)/shard_map/all_to_all | solution.py:305
  52.2 0.3 shard_map.98
  52.5 25.8 %all_to_all.11.recv = bf16[16,32,128]{2,1,0:T(8,128)(2,1)S(1)} all-to-all(bf16[16,32,128]{2,1,0:T(8,128)(2,1)S(1)} %shard_map.98), channel_id=1, replica_groups=mesh['zh'=4,'zl'=2,'x'=4,'yh'=4,'yl'=2,'c'=2] {'zh','yh'}, dimensions={0} | all-to-all | bytes 262144 | tf_op jit(solution)/shard_map/all_to_all | solution.py:307
  78.4 8.5 %all-gather = f32[128,128]{1,0:T(8,128)S(1)} all-gather(f32[32,128]{1,0:T(8,128)S(1)} %shard_map.99), channel_id=2, replica_groups=mesh['zh'=4,'zl'=2,'x'=4,'yh'=4,'yl'=2,'c'=2] {'yl','c'}, dimensions={0}, use_global_device_ids=true | all-gather | bytes 81920 | tf_op jit(solution)/shard_map/all_gather | solution.py:309
  86.9 0.6 shard_map.100
  (1 shorter events, 0.0 us)
Async XLA Ops:
  1.7 8.3 %collective-permute-start = (bf16[192,512]{1,0:T(8,128)(2,1)S(1)}, bf16[192,512]{1,0:T(8,128)(2,1)S(1)}, u32[]{:S(2)}, u32[]{:S(2)}) collective-permute-start(bf16[192,512]{1,0:T(8,128)(2,1)S(1)} %get-tuple-element.21), channel_id=1, source_target_pairs={{0,4},{4,8},{8,12},{12,16},{16,20},{20,24},{24,28},{28,32},{32,36}... | collective-permute-start | bytes 589832 | tf_op jit(solution)/shard_map/ppermute | solution.py:291
  6.7 14.9 %collective-permute-start.1 = (bf16[192,512]{1,0:T(8,128)(2,1)S(1)}, bf16[192,512]{1,0:T(8,128)(2,1)S(1)}, u32[]{:S(2)}, u32[]{:S(2)}) collective-permute-start(bf16[192,512]{1,0:T(8,128)(2,1)S(1)} %get-tuple-element.22), channel_id=1, source_target_pairs={{4,0},{8,4},{12,8},{16,12},{20,16},{24,20},{28,24},{32,28},{36,32}... | collective-permute-start | bytes 589832 | tf_op jit(solution)/shard_map/ppermute | solution.py:292
  25.5 3.9 %collective-permute-start.2 = (bf16[144,1536]{1,0:T(8,128)(2,1)S(1)}, bf16[144,1536]{1,0:T(8,128)(2,1)S(1)}, u32[]{:S(2)}, u32[]{:S(2)}) collective-permute-start(bf16[144,1536]{1,0:T(8,128)(2,1)S(1)} %get-tuple-element.30), channel_id=1, source_target_pairs={{0,1},{1,0},{2,3},{3,2},{4,5},{5,4},{6,7},{7,6},{8,9},{9,8},{10,11... | collective-permute-start | bytes 1327112 | tf_op jit(solution)/shard_map/ppermute | solution.py:302

commit v6 on v4

--- a/solution.py
+++ b/solution.py
@@ -11,8 +11,7 @@
 EPS = 1e-06
 F32 = jnp.float32
 BF16 = jnp.bfloat16
-NEAR = ("x", "yl")
-FAR = ("z", "yh")
+ALL = ("z", "x", "yh", "yl", "c")
 SEQ = ("z", "x", "yh")
 HAP = ("yl", "c")
 G0 = 0.7978845608028654
@@ -197,9 +196,24 @@
     send[...] = act[1 - core]
 
 
+def device(near, far, core):
+    z = ((far >> 3) * 2 + (near >> 2) + core) % 8
+    x = ((far >> 2) % 2 * 2 + (near >> 1) % 2 + core) % 4
+    y = (far % 4 * 2 + near % 2 + core) % 8
+    return ((z * 4 + x) * 8 + y) * 2 + core
+
+
+NEAR = [[device(n, f, c) for n in range(8)] for c in range(2) for f in range(32)]
+FAR = [[device(n, f, c) for f in range(32)] for c in range(2) for n in range(8)]
+
+
 def own_terms(keep, pick, mine):
+    core = lax.axis_index("c")
     q = lax.broadcasted_iota(jnp.int32, (C, 1), 0)
-    ch = ((q >> 3) & 7) << 6 | ((q >> 7) & 3) << 4 | ((q >> 1) & 3) << 2 | ((q >> 6) & 1) << 1 | (q & 1)
+    z = ((((q >> 5) & 1) << 2 | ((q >> 4) & 1) << 1 | ((q >> 8) & 1)) + core) & 7
+    x = ((((q >> 3) & 1) << 1 | ((q >> 7) & 1)) + core) & 3
+    y = ((((q >> 1) & 3) << 1 | ((q >> 6) & 1)) + core) & 7
+    ch = z << 6 | x << 4 | y << 1 | (q & 1)
     pick[...] = (ch == lax.broadcasted_iota(jnp.int32, (C, C), 1)).astype(F32).astype(BF16)
     ha = dot(pick[...], keep[0:128, 0:C], ((1,), (1,))).astype(BF16)
     mine[...] = dot(ha, keep[0:128, C:3 * C], ((1,), (0,)))
@@ -301,9 +315,9 @@
     recv = lax.ppermute(send, "c", [(0, 1), (1, 0)])
     pick, mine = call(own_terms, "v", [s((C, C), BF16), s((C, 2 * C), F32)])(keep)
     part = call(terms, "vvvv", s((8, 528, 128), BF16))(keep, recv, pick, mine)
-    part = lax.all_to_all(part, NEAR, 0, 0, tiled=True)
+    part = lax.all_to_all(part, ALL, 0, 0, axis_index_groups=NEAR, tiled=True)
     part = call(first_sum, "v", s((32, 32, 128), BF16))(part)
-    part = lax.all_to_all(part, FAR, 0, 0, tiled=True)
+    part = lax.all_to_all(part, ALL, 0, 0, axis_index_groups=FAR, tiled=True)
     part = call(second_sum, "v", s((32, 128), F32))(part)
     part = lax.all_gather(part, HAP, axis=0)
     projection_grad, taps_grad, gains_grad = call(

time: 87.4 us -> 86.4 us (0.989)
  blocking collectives: 55.7 us -> 54.8 us
    all_to_all x2, blocking collectives: 47.1 us -> 44 us  [the longest x1 22.3 us: shards(): part = lax.all_to_all(part, ALL, 0, 0, axis_index_groups=FAR, tiled=True)]
    all_gather x1, blocking collectives: 8.53 us -> 10.8 us  [shards(): part = lax.all_gather(part, HAP, axis=0)]
where the time goes in v6:
time: 86.4 us; the launch traced here: 86.1 us
  blocking collectives  54.8 us (63%)
  waiting for transfers between devices  12 us (14%)
  Pallas kernels  9.89 us (11%)
  starting transfers between devices  8.83 us (10%)
    all_to_all x1, blocking collectives, shards(): part = lax.all_to_all(part, ALL, 0, 0, axis_index_groups=FAR, tiled=True)  22.3 us
    all_to_all x1, blocking collectives, shards(): part = lax.all_to_all(part, ALL, 0, 0, axis_index_groups=NEAR, tiled=True)  21.7 us
    ppermute x1, waiting for transfers between devices, shards(): nxt = lax.ppermute(down, SEQ, [(i + 1, i) for i in range(n - 1)])  11.6 us
    all_gather x1, blocking collectives, shards(): part = lax.all_gather(part, HAP, axis=0)  10.8 us
    ppermute x1, starting transfers between devices, shards(): prev = lax.ppermute(up, SEQ, [(i, i + 1) for i in range(n - 1)])  5.05 us
    pallas_call x1, Pallas kernels, main(): call(body, 'vvvvvvvv', [s((128, C), BF16), s((ACT, 3 * C), BF16), s((ACT,...  3.89 us
    ppermute x1, starting transfers between devices, shards(): recv = lax.ppermute(send, 'c', [(0, 1), (1, 0)])  2.48 us
    pallas_call x1, Pallas kernels, shards(): call(warm, 'svvvvv', [s((128, 1), F32), s((128, C), BF16), s((128, C), BF...  1.95 us
  transfers between devices with their start and end apart: 3, of which 2 were waited for; matrix products, arithmetic and copies ran while one was open for 0% of the time, Pallas kernels for 3%

profile of v6, /device:TPU:1, one launch (start us, length us, event | category | flops | bytes accessed | tf_op | source)
XLA Modules:
  0.0 86.1 jit_solution(10406988706716306209)
XLA Ops:
  0.6 1.0 %shard_map.94 = (bf16[192,512]{1,0:T(8,128)(2,1)S(1)}, bf16[192,512]{1,0:T(8,128)(2,1)S(1)}) custom-call(s32[1,2]{1,0:T(1,128)} %gaps.3, bf16[128,512]{1,0:T(8,128)(2,1)} %bitcast.7, bf16[128,512]{1,0:T(8,128)(2,1)} %bitcast.9), custom_call_target="tpu_custom_call" | custom-call | tf_op jit(solution)/shard_map/pallas_call | solution.py:303
  1.7 5.1 %collective-permute-start = (bf16[192,512]{1,0:T(8,128)(2,1)S(1)}, bf16[192,512]{1,0:T(8,128)(2,1)S(1)}, u32[]{:S(2)}, u32[]{:S(2)}) collective-permute-start(bf16[192,512]{1,0:T(8,128)(2,1)S(1)} %get-tuple-element.21), channel_id=1, source_target_pairs={{0,4},{4,8},{8,12},{12,16},{16,20},{20,24},{24,28},{28,32},{32,36}... | collective-permute-start | bytes 589832 | tf_op jit(solution)/shard_map/ppermute | solution.py:304
  6.7 1.3 %collective-permute-start.1 = (bf16[192,512]{1,0:T(8,128)(2,1)S(1)}, bf16[192,512]{1,0:T(8,128)(2,1)S(1)}, u32[]{:S(2)}, u32[]{:S(2)}) collective-permute-start(bf16[192,512]{1,0:T(8,128)(2,1)S(1)} %get-tuple-element.22), channel_id=1, source_target_pairs={{4,0},{8,4},{12,8},{16,12},{20,16},{24,20},{28,24},{32,28},{36,32}... | collective-permute-start | bytes 589832 | tf_op jit(solution)/shard_map/ppermute | solution.py:305
  8.0 1.9 %shard_map.93 = (f32[128,1]{1,0:T(8,128)S(1)}, bf16[128,512]{1,0:T(8,128)(2,1)S(1)}, bf16[128,512]{1,0:T(8,128)(2,1)S(1)}, f32[3,2,512]{2,1,0:T(2,128)S(1)}, f32...) custom-call(s32[1,2]{1,0:T(1,128)} %gaps.3, bf16[128,512]{1,0:T(8,128)(2,1)} %bitcast.8, bf16[128,512]{1,0:T(8,128)(2,1)} %bitcast.10, ...), custom_call_target="tpu_custom_call" | custom-call | tf_op jit(solution)/shard_map/pallas_call | solution.py:308
  10.0 0.0 collective-permute-done.prev
  10.0 11.6 %collective-permute-done.1.nxt = bf16[192,512]{1,0:T(8,128)(2,1)S(1)} collective-permute-done((bf16[192,512]{1,0:T(8,128)(2,1)S(1)}, bf16[192,512]{1,0:T(8,128)(2,1)S(1)}, u32[]{:S(2)}, u32[]{:S(2)}) %collective-permute-start.1) | collective-permute-done | bytes 196640 | tf_op jit(solution)/shard_map/ppermute | solution.py:305
  21.6 3.9 %shard_map.95 = (bf16[128,512]{1,0:T(8,128)(2,1)}, bf16[144,1536]{1,0:T(8,128)(2,1)S(1)}, bf16[144,1536]{1,0:T(8,128)(2,1)S(1)}) custom-call(f32[128,1]{1,0:T(8,128)S(1)} %get-tuple-element.20.own_valid, bf16[192,512]{1,0:T(8,128)(2,1)S(1)} %collective-permute-done.prev, bf16[192,512]{1,0:T(8,128)(2,1)S(1)} %collective-permute-done.1.nxt, ...), custom_call_target="tpu_custom_call" | custom-call | tf_op jit(solution)/shard_map/pallas_call | solution.py:287
  25.5 2.5 %collective-permute-start.2 = (bf16[144,1536]{1,0:T(8,128)(2,1)S(1)}, bf16[144,1536]{1,0:T(8,128)(2,1)S(1)}, u32[]{:S(2)}, u32[]{:S(2)}) collective-permute-start(bf16[144,1536]{1,0:T(8,128)(2,1)S(1)} %get-tuple-element.30), channel_id=1, source_target_pairs={{0,1},{1,0},{2,3},{3,2},{4,5},{5,4},{6,7},{7,6},{8,9},{9,8},{10,11... | collective-permute-start | bytes 1327112 | tf_op jit(solution)/shard_map/ppermute | solution.py:315
  28.0 1.0 %shard_map.96 = (bf16[512,512]{1,0:T(8,128)(2,1)S(1)}, f32[512,1024]{1,0:T(8,128)S(1)}) custom-call(bf16[144,1536]{1,0:T(8,128)(2,1)S(1)} %get-tuple-element.29.keep), custom_call_target="tpu_custom_call" | custom-call | tf_op jit(solution)/shard_map/pallas_call | solution.py:316
  29.0 0.4 collective-permute-done.2.recv
  29.4 0.9 %shard_map.97 = bf16[8,528,128]{2,1,0:T(8,128)(2,1)S(1)} custom-call(bf16[144,1536]{1,0:T(8,128)(2,1)S(1)} %get-tuple-element.29.keep, bf16[144,1536]{1,0:T(8,128)(2,1)S(1)} %collective-permute-done.2.recv, bf16[512,512]{1,0:T(8,128)(2,1)S(1)} %get-tuple-element.31.pick, f32[512,1024]{1,0:T(8,128)S(1)} %get-tuple-element.32.mine), custom_call_target="tpu_custom_call" | custom-call | tf_op jit(solution)/shard_map/pallas_call | solution.py:317
  30.3 21.7 %all_to_all.10.recv = bf16[8,528,128]{2,1,0:T(8,128)(2,1)S(1)} all-to-all(bf16[8,528,128]{2,1,0:T(8,128)(2,1)S(1)} %shard_map.97), channel_id=1, replica_groups={{0,2,16,18,64,66,80,82},{4,6,20,22,68,70,84,86},{8,10,24,26,72,74,88,90..., dimensions={0} | all-to-all | bytes 2162688 | tf_op jit(solution)/shard_map/all_to_all | solution.py:318
  51.9 0.4 shard_map.98
  52.4 22.3 %all_to_all.11.recv = bf16[32,32,128]{2,1,0:T(8,128)(2,1)S(1)} all-to-all(bf16[32,32,128]{2,1,0:T(8,128)(2,1)S(1)} %shard_map.98), channel_id=1, replica_groups={{0,4,8,12,32,36,40,44,128,132,136,140,160,164,168,172,256,260,264,268,2..., dimensions={0} | all-to-all | bytes 524288 | tf_op jit(solution)/shard_map/all_to_all | solution.py:320
  74.7 10.8 %all-gather = f32[128,128]{1,0:T(8,128)S(1)} all-gather(f32[32,128]{1,0:T(8,128)S(1)} %shard_map.99), channel_id=2, replica_groups=mesh['z'=8,'x'=4,'yh'=4,'yl'=2,'c'=2] {'yl','c'}, dimensions={0}, use_global_device_ids=true | all-gather | bytes 81920 | tf_op jit(solution)/shard_map/all_gather | solution.py:322
  85.5 0.6 shard_map.100
  (1 shorter events, 0.0 us)
Async XLA Ops:
  1.7 8.3 %collective-permute-start = (bf16[192,512]{1,0:T(8,128)(2,1)S(1)}, bf16[192,512]{1,0:T(8,128)(2,1)S(1)}, u32[]{:S(2)}, u32[]{:S(2)}) collective-permute-start(bf16[192,512]{1,0:T(8,128)(2,1)S(1)} %get-tuple-element.21), channel_id=1, source_target_pairs={{0,4},{4,8},{8,12},{12,16},{16,20},{20,24},{24,28},{28,32},{32,36}... | collective-permute-start | bytes 589832 | tf_op jit(solution)/shard_map/ppermute | solution.py:304
  6.7 14.9 %collective-permute-start.1 = (bf16[192,512]{1,0:T(8,128)(2,1)S(1)}, bf16[192,512]{1,0:T(8,128)(2,1)S(1)}, u32[]{:S(2)}, u32[]{:S(2)}) collective-permute-start(bf16[192,512]{1,0:T(8,128)(2,1)S(1)} %get-tuple-element.22), channel_id=1, source_target_pairs={{4,0},{8,4},{12,8},{16,12},{20,16},{24,20},{28,24},{32,28},{36,32}... | collective-permute-start | bytes 589832 | tf_op jit(solution)/shard_map/ppermute | solution.py:305
  25.5 3.9 %collective-permute-start.2 = (bf16[144,1536]{1,0:T(8,128)(2,1)S(1)}, bf16[144,1536]{1,0:T(8,128)(2,1)S(1)}, u32[]{:S(2)}, u32[]{:S(2)}) collective-permute-start(bf16[144,1536]{1,0:T(8,128)(2,1)S(1)} %get-tuple-element.30), channel_id=1, source_target_pairs={{0,1},{1,0},{2,3},{3,2},{4,5},{5,4},{6,7},{7,6},{8,9},{9,8},{10,11... | collective-permute-start | bytes 1327112 | tf_op jit(solution)/shard_map/ppermute | solution.py:315

commit v7 on v6

--- a/solution.py
+++ b/solution.py
@@ -240,11 +240,10 @@
     p = lax.broadcasted_iota(jnp.int32, (C, 1), 0)
     src = ((p >> 1) & 7) << 6 | (p >> 4) << 1 | (p & 1)
     pick = (src == lax.broadcasted_iota(jnp.int32, (C, C), 1)).astype(F32).astype(BF16)
-    moved = dot(pick, total[0:512, :].astype(BF16), ((1,), (0,))).astype(BF16)
-    out[:, 0:16, :] = moved.reshape(32, 16, 128)
-    tile = total[512:528, :].astype(BF16)
+    moved = dot(pick, total[0:512, :].astype(BF16), ((1,), (0,)))
+    half = jnp.where(lax.axis_index("yl") == 0, total[512:520, :], total[520:528, :])
     for d in range(32):
-        out[d, 16:32, :] = tile
+        out[d] = jnp.concatenate([moved[16 * d:16 * d + 16, :], half], axis=0).astype(BF16)
 
 
 def second_sum(recv, out):
@@ -261,7 +260,8 @@
                 proj[c, 2 * y:2 * y + 2, j * 128:(j + 1) * 128] = recv[y * 2 + c, 2 * j:2 * j + 2, :]
         for r in range(4):
             for q in range(4):
-                row = recv[c, 16 + r * 4 + q:17 + r * 4 + q, :]
+                at = 16 + (r % 2) * 4 + q
+                row = recv[(r // 2) * 2 + c, at:at + 1, :]
                 if r < 3:
                     taps[r, c:c + 1, q * 128:(q + 1) * 128] = row
                 else:
@@ -316,9 +316,9 @@
     pick, mine = call(own_terms, "v", [s((C, C), BF16), s((C, 2 * C), F32)])(keep)
     part = call(terms, "vvvv", s((8, 528, 128), BF16))(keep, recv, pick, mine)
     part = lax.all_to_all(part, ALL, 0, 0, axis_index_groups=NEAR, tiled=True)
-    part = call(first_sum, "v", s((32, 32, 128), BF16))(part)
+    part = call(first_sum, "v", s((32, 24, 128), BF16))(part)
     part = lax.all_to_all(part, ALL, 0, 0, axis_index_groups=FAR, tiled=True)
-    part = call(second_sum, "v", s((32, 128), F32))(part)
+    part = call(second_sum, "v", s((24, 128), F32))(part)
     part = lax.all_gather(part, HAP, axis=0)
     projection_grad, taps_grad, gains_grad = call(
         place, "v", [s((2, 4, 1024), F32), s((3, 2, C), F32), s((2, C), F32)]

time: 86.4 us -> 86 us (level)
    all_to_all x1, blocking collectives: 22.3 us -> 21.2 us  [shards(): part = lax.all_to_all(part, ALL, 0, 0, axis_index_groups=FAR, tiled=True)]
where the time goes in v7:
time: 86 us; the launch traced here: 85.7 us
  blocking collectives  54.4 us (63%)
  waiting for transfers between devices  12 us (14%)
  Pallas kernels  9.89 us (12%)
  starting transfers between devices  8.83 us (10%)
    all_to_all x1, blocking collectives, shards(): part = lax.all_to_all(part, ALL, 0, 0, axis_index_groups=NEAR, tiled=True)  21.7 us
    all_to_all x1, blocking collectives, shards(): part = lax.all_to_all(part, ALL, 0, 0, axis_index_groups=FAR, tiled=True)  21.2 us
    ppermute x1, waiting for transfers between devices, shards(): nxt = lax.ppermute(down, SEQ, [(i + 1, i) for i in range(n - 1)])  11.6 us
    all_gather x1, blocking collectives, shards(): part = lax.all_gather(part, HAP, axis=0)  11.5 us
    ppermute x1, starting transfers between devices, shards(): prev = lax.ppermute(up, SEQ, [(i, i + 1) for i in range(n - 1)])  5.05 us
    pallas_call x1, Pallas kernels, main(): call(body, 'vvvvvvvv', [s((128, C), BF16), s((ACT, 3 * C), BF16), s((ACT,...  3.89 us
    ppermute x1, starting transfers between devices, shards(): recv = lax.ppermute(send, 'c', [(0, 1), (1, 0)])  2.48 us
    pallas_call x1, Pallas kernels, shards(): call(warm, 'svvvvv', [s((128, 1), F32), s((128, C), BF16), s((128, C), BF...  1.95 us
  transfers between devices with their start and end apart: 3, of which 2 were waited for; matrix products, arithmetic and copies ran while one was open for 0% of the time, Pallas kernels for 3%

profile of v7, /device:TPU:1, one launch (start us, length us, event | category | flops | bytes accessed | tf_op | source)
XLA Modules:
  0.0 85.7 jit_solution(10379193938401474031)
XLA Ops:
  0.6 1.0 %shard_map.94 = (bf16[192,512]{1,0:T(8,128)(2,1)S(1)}, bf16[192,512]{1,0:T(8,128)(2,1)S(1)}) custom-call(s32[1,2]{1,0:T(1,128)} %gaps.3, bf16[128,512]{1,0:T(8,128)(2,1)} %bitcast.7, bf16[128,512]{1,0:T(8,128)(2,1)} %bitcast.9), custom_call_target="tpu_custom_call" | custom-call | tf_op jit(solution)/shard_map/pallas_call | solution.py:303
  1.7 5.1 %collective-permute-start = (bf16[192,512]{1,0:T(8,128)(2,1)S(1)}, bf16[192,512]{1,0:T(8,128)(2,1)S(1)}, u32[]{:S(2)}, u32[]{:S(2)}) collective-permute-start(bf16[192,512]{1,0:T(8,128)(2,1)S(1)} %get-tuple-element.21), channel_id=1, source_target_pairs={{0,4},{4,8},{8,12},{12,16},{16,20},{20,24},{24,28},{28,32},{32,36}... | collective-permute-start | bytes 589832 | tf_op jit(solution)/shard_map/ppermute | solution.py:304
  6.7 1.3 %collective-permute-start.1 = (bf16[192,512]{1,0:T(8,128)(2,1)S(1)}, bf16[192,512]{1,0:T(8,128)(2,1)S(1)}, u32[]{:S(2)}, u32[]{:S(2)}) collective-permute-start(bf16[192,512]{1,0:T(8,128)(2,1)S(1)} %get-tuple-element.22), channel_id=1, source_target_pairs={{4,0},{8,4},{12,8},{16,12},{20,16},{24,20},{28,24},{32,28},{36,32}... | collective-permute-start | bytes 589832 | tf_op jit(solution)/shard_map/ppermute | solution.py:305
  8.0 1.9 %shard_map.93 = (f32[128,1]{1,0:T(8,128)S(1)}, bf16[128,512]{1,0:T(8,128)(2,1)S(1)}, bf16[128,512]{1,0:T(8,128)(2,1)S(1)}, f32[3,2,512]{2,1,0:T(2,128)S(1)}, f32...) custom-call(s32[1,2]{1,0:T(1,128)} %gaps.3, bf16[128,512]{1,0:T(8,128)(2,1)} %bitcast.8, bf16[128,512]{1,0:T(8,128)(2,1)} %bitcast.10, ...), custom_call_target="tpu_custom_call" | custom-call | tf_op jit(solution)/shard_map/pallas_call | solution.py:308
  10.0 0.0 collective-permute-done.prev
  10.0 11.6 %collective-permute-done.1.nxt = bf16[192,512]{1,0:T(8,128)(2,1)S(1)} collective-permute-done((bf16[192,512]{1,0:T(8,128)(2,1)S(1)}, bf16[192,512]{1,0:T(8,128)(2,1)S(1)}, u32[]{:S(2)}, u32[]{:S(2)}) %collective-permute-start.1) | collective-permute-done | bytes 196640 | tf_op jit(solution)/shard_map/ppermute | solution.py:305
  21.6 3.9 %shard_map.95 = (bf16[128,512]{1,0:T(8,128)(2,1)}, bf16[144,1536]{1,0:T(8,128)(2,1)S(1)}, bf16[144,1536]{1,0:T(8,128)(2,1)S(1)}) custom-call(f32[128,1]{1,0:T(8,128)S(1)} %get-tuple-element.20.own_valid, bf16[192,512]{1,0:T(8,128)(2,1)S(1)} %collective-permute-done.prev, bf16[192,512]{1,0:T(8,128)(2,1)S(1)} %collective-permute-done.1.nxt, ...), custom_call_target="tpu_custom_call" | custom-call | tf_op jit(solution)/shard_map/pallas_call | solution.py:287
  25.5 2.5 %collective-permute-start.2 = (bf16[144,1536]{1,0:T(8,128)(2,1)S(1)}, bf16[144,1536]{1,0:T(8,128)(2,1)S(1)}, u32[]{:S(2)}, u32[]{:S(2)}) collective-permute-start(bf16[144,1536]{1,0:T(8,128)(2,1)S(1)} %get-tuple-element.30), channel_id=1, source_target_pairs={{0,1},{1,0},{2,3},{3,2},{4,5},{5,4},{6,7},{7,6},{8,9},{9,8},{10,11... | collective-permute-start | bytes 1327112 | tf_op jit(solution)/shard_map/ppermute | solution.py:315
  28.0 1.0 %shard_map.96 = (bf16[512,512]{1,0:T(8,128)(2,1)S(1)}, f32[512,1024]{1,0:T(8,128)S(1)}) custom-call(bf16[144,1536]{1,0:T(8,128)(2,1)S(1)} %get-tuple-element.29.keep), custom_call_target="tpu_custom_call" | custom-call | tf_op jit(solution)/shard_map/pallas_call | solution.py:316
  29.0 0.4 collective-permute-done.2.recv
  29.4 0.9 %shard_map.97 = bf16[8,528,128]{2,1,0:T(8,128)(2,1)S(1)} custom-call(bf16[144,1536]{1,0:T(8,128)(2,1)S(1)} %get-tuple-element.29.keep, bf16[144,1536]{1,0:T(8,128)(2,1)S(1)} %collective-permute-done.2.recv, bf16[512,512]{1,0:T(8,128)(2,1)S(1)} %get-tuple-element.31.pick, f32[512,1024]{1,0:T(8,128)S(1)} %get-tuple-element.32.mine), custom_call_target="tpu_custom_call" | custom-call | tf_op jit(solution)/shard_map/pallas_call | solution.py:317
  30.3 21.7 %all_to_all.10.recv = bf16[8,528,128]{2,1,0:T(8,128)(2,1)S(1)} all-to-all(bf16[8,528,128]{2,1,0:T(8,128)(2,1)S(1)} %shard_map.97), channel_id=1, replica_groups={{0,2,16,18,64,66,80,82},{4,6,20,22,68,70,84,86},{8,10,24,26,72,74,88,90..., dimensions={0} | all-to-all | bytes 2162688 | tf_op jit(solution)/shard_map/all_to_all | solution.py:318
  51.9 0.4 shard_map.98
  52.4 21.2 %all_to_all.11.recv = bf16[32,24,128]{2,1,0:T(8,128)(2,1)S(1)} all-to-all(bf16[32,24,128]{2,1,0:T(8,128)(2,1)S(1)} %shard_map.98), channel_id=1, replica_groups={{0,4,8,12,32,36,40,44,128,132,136,140,160,164,168,172,256,260,264,268,2..., dimensions={0} | all-to-all | bytes 393216 | tf_op jit(solution)/shard_map/all_to_all | solution.py:320
  73.6 11.5 %all-gather = f32[96,128]{1,0:T(8,128)S(1)} all-gather(f32[24,128]{1,0:T(8,128)S(1)} %shard_map.99), channel_id=2, replica_groups=mesh['z'=8,'x'=4,'yh'=4,'yl'=2,'c'=2] {'yl','c'}, dimensions={0}, use_global_device_ids=true | all-gather | bytes 61440 | tf_op jit(solution)/shard_map/all_gather | solution.py:322
  85.1 0.6 shard_map.100
  (1 shorter events, 0.0 us)
Async XLA Ops:
  1.7 8.3 %collective-permute-start = (bf16[192,512]{1,0:T(8,128)(2,1)S(1)}, bf16[192,512]{1,0:T(8,128)(2,1)S(1)}, u32[]{:S(2)}, u32[]{:S(2)}) collective-permute-start(bf16[192,512]{1,0:T(8,128)(2,1)S(1)} %get-tuple-element.21), channel_id=1, source_target_pairs={{0,4},{4,8},{8,12},{12,16},{16,20},{20,24},{24,28},{28,32},{32,36}... | collective-permute-start | bytes 589832 | tf_op jit(solution)/shard_map/ppermute | solution.py:304
  6.7 14.9 %collective-permute-start.1 = (bf16[192,512]{1,0:T(8,128)(2,1)S(1)}, bf16[192,512]{1,0:T(8,128)(2,1)S(1)}, u32[]{:S(2)}, u32[]{:S(2)}) collective-permute-start(bf16[192,512]{1,0:T(8,128)(2,1)S(1)} %get-tuple-element.22), channel_id=1, source_target_pairs={{4,0},{8,4},{12,8},{16,12},{20,16},{24,20},{28,24},{32,28},{36,32}... | collective-permute-start | bytes 589832 | tf_op jit(solution)/shard_map/ppermute | solution.py:305
  25.5 3.9 %collective-permute-start.2 = (bf16[144,1536]{1,0:T(8,128)(2,1)S(1)}, bf16[144,1536]{1,0:T(8,128)(2,1)S(1)}, u32[]{:S(2)}, u32[]{:S(2)}) collective-permute-start(bf16[144,1536]{1,0:T(8,128)(2,1)S(1)} %get-tuple-element.30), channel_id=1, source_target_pairs={{0,1},{1,0},{2,3},{3,2},{4,5},{5,4},{6,7},{7,6},{8,9},{9,8},{10,11... | collective-permute-start | bytes 1327112 | tf_op jit(solution)/shard_map/ppermute | solution.py:315

commit v8 on v7

--- a/solution.py
+++ b/solution.py
@@ -11,8 +11,9 @@
 EPS = 1e-06
 F32 = jnp.float32
 BF16 = jnp.bfloat16
-ALL = ("z", "x", "yh", "yl", "c")
-SEQ = ("z", "x", "yh")
+ALL = ("z", "xh", "xl", "yh", "yl", "c")
+LAST = ("xh", "yl", "c")
+SEQ = ("z", "xh", "xl", "yh")
 HAP = ("yl", "c")
 G0 = 0.7978845608028654
 G1 = 0.044715
@@ -68,7 +69,7 @@
          n0, i0, g0, h0, ab0, x1, n1, i1, g1, h1, po1, dp1, dh1, gr1, dp0, dh0, act):
     core = lax.axis_index("c")
     place_in_seq = sum(lax.axis_index(a) for a in SEQ)
-    inner = (place_in_seq > 0, None, place_in_seq < 13)
+    inner = (place_in_seq > 0, None, place_in_seq < 12)
 
     def rows(base):
         ref, at = ((prev, base), (tok, base - 128), (nxt, base - 256))[base // 128]
@@ -204,7 +205,7 @@
 
 
 NEAR = [[device(n, f, c) for n in range(8)] for c in range(2) for f in range(32)]
-FAR = [[device(n, f, c) for f in range(32)] for c in range(2) for n in range(8)]
+FAR = [[device(n, (g >> 2) << 3 | x << 2 | g % 4, c) for g in range(16)] for c in range(2) for n in range(8) for x in range(2)]
 
 
 def own_terms(keep, pick, mine):
@@ -238,30 +239,34 @@
     for i in range(1, 8):
         total += recv[i].astype(F32)
     p = lax.broadcasted_iota(jnp.int32, (C, 1), 0)
-    src = ((p >> 1) & 7) << 6 | (p >> 4) << 1 | (p & 1)
+    src = ((p >> 1) & 7) << 6 | ((p >> 7) & 3) << 4 | ((p >> 4) & 1) << 3 | ((p >> 5) & 3) << 1 | (p & 1)
     pick = (src == lax.broadcasted_iota(jnp.int32, (C, C), 1)).astype(F32).astype(BF16)
     moved = dot(pick, total[0:512, :].astype(BF16), ((1,), (0,)))
     half = jnp.where(lax.axis_index("yl") == 0, total[512:520, :], total[520:528, :])
-    for d in range(32):
-        out[d] = jnp.concatenate([moved[16 * d:16 * d + 16, :], half], axis=0).astype(BF16)
+    for d in range(16):
+        out[d] = jnp.concatenate([moved[32 * d:32 * d + 32, :], half], axis=0).astype(BF16)
 
 
 def second_sum(recv, out):
     total = recv[0].astype(F32)
-    for i in range(1, 32):
+    for i in range(1, 16):
         total += recv[i].astype(F32)
-    out[...] = total
+    swap = (lax.axis_index("c") == 1) & (lax.axis_index("xl") == 0)
+    a, b = total[0:16, :], total[16:32, :]
+    for i in range(8):
+        piece = jnp.where(swap, b, a) if i < 4 else jnp.where(swap, a, b)
+        out[i] = jnp.concatenate([piece, total[32:40, :]], axis=0)
 
 
 def place(recv, proj, taps, gains):
     for c in range(2):
         for y in range(2):
             for j in range(8):
-                proj[c, 2 * y:2 * y + 2, j * 128:(j + 1) * 128] = recv[y * 2 + c, 2 * j:2 * j + 2, :]
+                proj[c, 2 * y:2 * y + 2, j * 128:(j + 1) * 128] = recv[y * 2 + c, 2 * j:2 * j + 2, :] + recv[4 + y * 2 + c, 2 * j:2 * j + 2, :]
         for r in range(4):
             for q in range(4):
                 at = 16 + (r % 2) * 4 + q
-                row = recv[(r // 2) * 2 + c, at:at + 1, :]
+                row = recv[(r // 2) * 2 + c, at:at + 1, :] + recv[4 + (r // 2) * 2 + c, at:at + 1, :]
                 if r < 3:
                     taps[r, c:c + 1, q * 128:(q + 1) * 128] = row
                 else:
@@ -316,10 +321,10 @@
     pick, mine = call(own_terms, "v", [s((C, C), BF16), s((C, 2 * C), F32)])(keep)
     part = call(terms, "vvvv", s((8, 528, 128), BF16))(keep, recv, pick, mine)
     part = lax.all_to_all(part, ALL, 0, 0, axis_index_groups=NEAR, tiled=True)
-    part = call(first_sum, "v", s((32, 24, 128), BF16))(part)
+    part = call(first_sum, "v", s((16, 40, 128), BF16))(part)
     part = lax.all_to_all(part, ALL, 0, 0, axis_index_groups=FAR, tiled=True)
-    part = call(second_sum, "v", s((24, 128), F32))(part)
-    part = lax.all_gather(part, HAP, axis=0)
+    part = call(second_sum, "v", s((8, 24, 128), F32))(part)
+    part = lax.all_to_all(part, LAST, 0, 0, tiled=True)
     projection_grad, taps_grad, gains_grad = call(
         place, "v", [s((2, 4, 1024), F32), s((3, 2, C), F32), s((2, C), F32)]
     )(part)
@@ -327,7 +332,7 @@
 
 
 def solution(mesh):
-    fine = Mesh(mesh.devices.reshape(8, 4, 4, 2, 2), ("z", "x", "yh", "yl", "c"))
+    fine = Mesh(mesh.devices.reshape(8, 2, 2, 4, 2, 2), ALL)
     return jax.shard_map(
         shards,
         mesh=fine,

time: 86 us -> 85 us (0.988)
  blocking collectives: 54.4 us -> 53.3 us
    all_to_all x0 -> x1, blocking collectives: none -> 11.8 us  [shards(): part = lax.all_to_all(part, LAST, 0, 0, tiled=True)]
    all_gather x1 -> x0, blocking collectives: 11.5 us -> none  [shards(): part = lax.all_gather(part, HAP, axis=0)]
    all_to_all x1, blocking collectives: 21.2 us -> 19.8 us  [shards(): part = lax.all_to_all(part, ALL, 0, 0, axis_index_groups=FAR, tiled=True)]
  transfers between devices with their start and end apart: 3 -> 3, of which waited for: 2 -> 2; matrix products, arithmetic and copies ran while one was open for 0% -> 0% of each run, Pallas kernels for 3% -> 4%
where the time goes in v8:
time: 85 us; the launch traced here: 84.7 us
  blocking collectives  53.3 us (63%)
  waiting for transfers between devices  12 us (14%)
  Pallas kernels  9.91 us (12%)
  starting transfers between devices  8.84 us (10%)
    all_to_all x1, blocking collectives, shards(): part = lax.all_to_all(part, ALL, 0, 0, axis_index_groups=NEAR, tiled=True)  21.7 us
    all_to_all x1, blocking collectives, shards(): part = lax.all_to_all(part, ALL, 0, 0, axis_index_groups=FAR, tiled=True)  19.8 us
    all_to_all x1, blocking collectives, shards(): part = lax.all_to_all(part, LAST, 0, 0, tiled=True)  11.8 us
    ppermute x1, waiting for transfers between devices, shards(): nxt = lax.ppermute(down, SEQ, [(i + 1, i) for i in range(n - 1)])  11.6 us
    ppermute x1, starting transfers between devices, shards(): prev = lax.ppermute(up, SEQ, [(i, i + 1) for i in range(n - 1)])  5.05 us
    pallas_call x1, Pallas kernels, main(): call(body, 'vvvvvvvv', [s((128, C), BF16), s((ACT, 3 * C), BF16), s((ACT,...  3.87 us
    ppermute x1, starting transfers between devices, shards(): recv = lax.ppermute(send, 'c', [(0, 1), (1, 0)])  2.5 us
    pallas_call x1, Pallas kernels, shards(): call(warm, 'svvvvv', [s((128, 1), F32), s((128, C), BF16), s((128, C), BF...  1.95 us
  transfers between devices with their start and end apart: 3, of which 2 were waited for; matrix products, arithmetic and copies ran while one was open for 0% of the time, Pallas kernels for 4%

profile of v8, /device:TPU:1, one launch (start us, length us, event | category | flops | bytes accessed | tf_op | source)
XLA Modules:
  0.0 84.7 jit_solution(5446446310526640957)
XLA Ops:
  0.6 1.0 %shard_map.94 = (bf16[192,512]{1,0:T(8,128)(2,1)S(1)}, bf16[192,512]{1,0:T(8,128)(2,1)S(1)}) custom-call(s32[1,2]{1,0:T(1,128)} %gaps.3, bf16[128,512]{1,0:T(8,128)(2,1)} %bitcast.5, bf16[128,512]{1,0:T(8,128)(2,1)} %bitcast.7), custom_call_target="tpu_custom_call" | custom-call | tf_op jit(solution)/shard_map/pallas_call | solution.py:308
  1.7 5.1 %collective-permute-start = (bf16[192,512]{1,0:T(8,128)(2,1)S(1)}, bf16[192,512]{1,0:T(8,128)(2,1)S(1)}, u32[]{:S(2)}, u32[]{:S(2)}) collective-permute-start(bf16[192,512]{1,0:T(8,128)(2,1)S(1)} %get-tuple-element.21), channel_id=1, source_target_pairs={{0,4},{4,8},{8,12},{12,16},{16,20},{20,24},{24,28},{28,32},{32,36}... | collective-permute-start | bytes 589832 | tf_op jit(solution)/shard_map/ppermute | solution.py:309
  6.7 1.3 %collective-permute-start.1 = (bf16[192,512]{1,0:T(8,128)(2,1)S(1)}, bf16[192,512]{1,0:T(8,128)(2,1)S(1)}, u32[]{:S(2)}, u32[]{:S(2)}) collective-permute-start(bf16[192,512]{1,0:T(8,128)(2,1)S(1)} %get-tuple-element.22), channel_id=1, source_target_pairs={{4,0},{8,4},{12,8},{16,12},{20,16},{24,20},{28,24},{32,28},{36,32}... | collective-permute-start | bytes 589832 | tf_op jit(solution)/shard_map/ppermute | solution.py:310
  8.0 1.9 %shard_map.93 = (f32[128,1]{1,0:T(8,128)S(1)}, bf16[128,512]{1,0:T(8,128)(2,1)S(1)}, bf16[128,512]{1,0:T(8,128)(2,1)S(1)}, f32[3,2,512]{2,1,0:T(2,128)S(1)}, f32...) custom-call(s32[1,2]{1,0:T(1,128)} %gaps.3, bf16[128,512]{1,0:T(8,128)(2,1)} %bitcast.6, bf16[128,512]{1,0:T(8,128)(2,1)} %bitcast.8, ...), custom_call_target="tpu_custom_call" | custom-call | tf_op jit(solution)/shard_map/pallas_call | solution.py:313
  10.0 0.0 collective-permute-done.prev
  10.0 11.6 %collective-permute-done.1.nxt = bf16[192,512]{1,0:T(8,128)(2,1)S(1)} collective-permute-done((bf16[192,512]{1,0:T(8,128)(2,1)S(1)}, bf16[192,512]{1,0:T(8,128)(2,1)S(1)}, u32[]{:S(2)}, u32[]{:S(2)}) %collective-permute-start.1) | collective-permute-done | bytes 196640 | tf_op jit(solution)/shard_map/ppermute | solution.py:310
  21.6 3.9 %shard_map.95 = (bf16[128,512]{1,0:T(8,128)(2,1)}, bf16[144,1536]{1,0:T(8,128)(2,1)S(1)}, bf16[144,1536]{1,0:T(8,128)(2,1)S(1)}) custom-call(f32[128,1]{1,0:T(8,128)S(1)} %get-tuple-element.20.own_valid, bf16[192,512]{1,0:T(8,128)(2,1)S(1)} %collective-permute-done.prev, bf16[192,512]{1,0:T(8,128)(2,1)S(1)} %collective-permute-done.1.nxt, ...), custom_call_target="tpu_custom_call" | custom-call | tf_op jit(solution)/shard_map/pallas_call | solution.py:292
  25.5 2.5 %collective-permute-start.2 = (bf16[144,1536]{1,0:T(8,128)(2,1)S(1)}, bf16[144,1536]{1,0:T(8,128)(2,1)S(1)}, u32[]{:S(2)}, u32[]{:S(2)}) collective-permute-start(bf16[144,1536]{1,0:T(8,128)(2,1)S(1)} %get-tuple-element.30), channel_id=1, source_target_pairs={{0,1},{1,0},{2,3},{3,2},{4,5},{5,4},{6,7},{7,6},{8,9},{9,8},{10,11... | collective-permute-start | bytes 1327112 | tf_op jit(solution)/shard_map/ppermute | solution.py:320
  28.0 1.0 %shard_map.96 = (bf16[512,512]{1,0:T(8,128)(2,1)S(1)}, f32[512,1024]{1,0:T(8,128)S(1)}) custom-call(bf16[144,1536]{1,0:T(8,128)(2,1)S(1)} %get-tuple-element.29.keep), custom_call_target="tpu_custom_call" | custom-call | tf_op jit(solution)/shard_map/pallas_call | solution.py:321
  29.0 0.4 collective-permute-done.2.recv
  29.4 0.9 %shard_map.97 = bf16[8,528,128]{2,1,0:T(8,128)(2,1)S(1)} custom-call(bf16[144,1536]{1,0:T(8,128)(2,1)S(1)} %get-tuple-element.29.keep, bf16[144,1536]{1,0:T(8,128)(2,1)S(1)} %collective-permute-done.2.recv, bf16[512,512]{1,0:T(8,128)(2,1)S(1)} %get-tuple-element.31.pick, f32[512,1024]{1,0:T(8,128)S(1)} %get-tuple-element.32.mine), custom_call_target="tpu_custom_call" | custom-call | tf_op jit(solution)/shard_map/pallas_call | solution.py:322
  30.3 21.7 %all_to_all.15.recv = bf16[8,528,128]{2,1,0:T(8,128)(2,1)S(1)} all-to-all(bf16[8,528,128]{2,1,0:T(8,128)(2,1)S(1)} %shard_map.97), channel_id=1, replica_groups={{0,2,16,18,64,66,80,82},{4,6,20,22,68,70,84,86},{8,10,24,26,72,74,88,90..., dimensions={0} | all-to-all | bytes 2162688 | tf_op jit(solution)/shard_map/all_to_all | solution.py:323
  51.9 0.5 shard_map.98
  52.4 19.8 %all_to_all.16.recv = bf16[16,40,128]{2,1,0:T(8,128)(2,1)S(1)} all-to-all(bf16[16,40,128]{2,1,0:T(8,128)(2,1)S(1)} %shard_map.98), channel_id=1, replica_groups={{0,4,8,12,128,132,136,140,256,260,264,268,384,388,392,396},{32,36,40,44..., dimensions={0} | all-to-all | bytes 327680 | tf_op jit(solution)/shard_map/all_to_all | solution.py:325
  72.2 11.8 %all_to_all.17.recv = f32[8,24,128]{2,1,0:T(8,128)S(1)} all-to-all(f32[8,24,128]{2,1,0:T(8,128)S(1)} %shard_map.99), channel_id=1, replica_groups=mesh['z'=8,'xh'=2,'xl'=2,'yh'=4,'yl'=2,'c'=2] {'xh','yl','c'}, dimensions={0} | all-to-all | bytes 196608 | tf_op jit(solution)/shard_map/all_to_all | solution.py:327
  84.0 0.7 shard_map.100
  (1 shorter events, 0.0 us)
Async XLA Ops:
  1.7 8.3 %collective-permute-start = (bf16[192,512]{1,0:T(8,128)(2,1)S(1)}, bf16[192,512]{1,0:T(8,128)(2,1)S(1)}, u32[]{:S(2)}, u32[]{:S(2)}) collective-permute-start(bf16[192,512]{1,0:T(8,128)(2,1)S(1)} %get-tuple-element.21), channel_id=1, source_target_pairs={{0,4},{4,8},{8,12},{12,16},{16,20},{20,24},{24,28},{28,32},{32,36}... | collective-permute-start | bytes 589832 | tf_op jit(solution)/shard_map/ppermute | solution.py:309
  6.7 14.9 %collective-permute-start.1 = (bf16[192,512]{1,0:T(8,128)(2,1)S(1)}, bf16[192,512]{1,0:T(8,128)(2,1)S(1)}, u32[]{:S(2)}, u32[]{:S(2)}) collective-permute-start(bf16[192,512]{1,0:T(8,128)(2,1)S(1)} %get-tuple-element.22), channel_id=1, source_target_pairs={{4,0},{8,4},{12,8},{16,12},{20,16},{24,20},{28,24},{32,28},{36,32}... | collective-permute-start | bytes 589832 | tf_op jit(solution)/shard_map/ppermute | solution.py:310
  25.5 3.9 %collective-permute-start.2 = (bf16[144,1536]{1,0:T(8,128)(2,1)S(1)}, bf16[144,1536]{1,0:T(8,128)(2,1)S(1)}, u32[]{:S(2)}, u32[]{:S(2)}) collective-permute-start(bf16[144,1536]{1,0:T(8,128)(2,1)S(1)} %get-tuple-element.30), channel_id=1, source_target_pairs={{0,1},{1,0},{2,3},{3,2},{4,5},{5,4},{6,7},{7,6},{8,9},{9,8},{10,11... | collective-permute-start | bytes 1327112 | tf_op jit(solution)/shard_map/ppermute | solution.py:320

commit v9 on v8

--- a/solution.py
+++ b/solution.py
@@ -48,7 +48,7 @@
     return hi, lo
 
 
-def pack(gaps, tok, cot, up, down):
+def pack(gaps, tok, cot, down, up):
     at = lax.broadcasted_iota(jnp.int32, (128, 1), 0)
     inside = (at >= gaps[0, 0]) & (at < gaps[0, 1])
     marked = jnp.where(inside, MARK, tok[...].astype(F32)).astype(BF16)
@@ -65,7 +65,7 @@
         b[...] = a[...]
 
 
-def body(own_valid, prev, nxt, tok, cot, taps, gains, proj, out, keep, send,
+def body(own_valid, nxt, prev, tok, cot, taps, gains, proj, out, keep, send,
          n0, i0, g0, h0, ab0, x1, n1, i1, g1, h1, po1, dp1, dh1, gr1, dp0, dh0, act):
     core = lax.axis_index("c")
     place_in_seq = sum(lax.axis_index(a) for a in SEQ)
@@ -305,9 +305,9 @@
     n = 128
     s = jax.ShapeDtypeStruct
     far = [pltpu.with_memory_space_constraint(a, pltpu.HBM) for a in (gaps, tok, cot)]
-    up, down = call(pack, "svv", [s((192, C), BF16), s((192, C), BF16)], mib=48)(*far)
+    down, up = call(pack, "svv", [s((192, C), BF16), s((192, C), BF16)], mib=48)(*far)
+    nxt = lax.ppermute(down, SEQ, [(i + 1, i) for i in range(n - 1)])
     prev = lax.ppermute(up, SEQ, [(i, i + 1) for i in range(n - 1)])
-    nxt = lax.ppermute(down, SEQ, [(i + 1, i) for i in range(n - 1)])
     here = [jnp.transpose(taps, (1, 0, 2)), gains, proj]
     here = far + [pltpu.with_memory_space_constraint(a, pltpu.HBM) for a in here]
     near_args = call(
@@ -316,7 +316,7 @@
         [s((128, 1), F32), s((128, C), BF16), s((128, C), BF16), s((3, 2, C), F32), s((2, C), F32),
          s((2, C, 2 * C), BF16)],
     )(*here)
-    tokens_grad, keep, send = main(near_args[0], prev, nxt, *near_args[1:])
+    tokens_grad, keep, send = main(near_args[0], nxt, prev, *near_args[1:])
     recv = lax.ppermute(send, "c", [(0, 1), (1, 0)])
     pick, mine = call(own_terms, "v", [s((C, C), BF16), s((C, 2 * C), F32)])(keep)
     part = call(terms, "vvvv", s((8, 528, 128), BF16))(keep, recv, pick, mine)

time: 85 us -> 85.1 us (level)
  waiting for transfers between devices: 12 us -> 1.79 us
  starting transfers between devices: 8.84 us -> 18.6 us
    ppermute x1, waiting for transfers between devices: 11.6 us -> 1.43 us  [shards(): nxt = lax.ppermute(down, SEQ, [(i + 1, i) for i in range(n - 1)])]
    ppermute x1, starting transfers between devices: 2.5 us -> 11.6 us  [shards(): recv = lax.ppermute(send, 'c', [(0, 1), (1, 0)])]
    all_to_all x1, blocking collectives: 21.7 us -> 27.6 us  [shards(): part = lax.all_to_all(part, ALL, 0, 0, axis_index_groups=NEAR, tiled=True)]
    all_to_all x1, blocking collectives: 19.8 us -> 15.3 us  [shards(): part = lax.all_to_all(part, ALL, 0, 0, axis_index_groups=FAR, tiled=True)]
    all_to_all x1, blocking collectives: 11.8 us -> 10.5 us  [shards(): part = lax.all_to_all(part, LAST, 0, 0, tiled=True)]
where the time goes in v9:
time: 85.1 us; the launch traced here: 84.4 us
  blocking collectives  53.4 us (63%)
  starting transfers between devices  18.6 us (22%)
  Pallas kernels  9.93 us (12%)
  waiting for transfers between devices  1.79 us (2%)
    all_to_all x1, blocking collectives, shards(): part = lax.all_to_all(part, ALL, 0, 0, axis_index_groups=NEAR, tiled=True)  27.6 us
    all_to_all x1, blocking collectives, shards(): part = lax.all_to_all(part, ALL, 0, 0, axis_index_groups=FAR, tiled=True)  15.3 us
    ppermute x1, starting transfers between devices, shards(): recv = lax.ppermute(send, 'c', [(0, 1), (1, 0)])  11.6 us
    all_to_all x1, blocking collectives, shards(): part = lax.all_to_all(part, LAST, 0, 0, tiled=True)  10.5 us
    ppermute x1, starting transfers between devices, shards(): prev = lax.ppermute(up, SEQ, [(i, i + 1) for i in range(n - 1)])  5.68 us
    pallas_call x1, Pallas kernels, main(): call(body, 'vvvvvvvv', [s((128, C), BF16), s((ACT, 3 * C), BF16), s((ACT,...  3.89 us
    pallas_call x1, Pallas kernels, shards(): call(warm, 'svvvvv', [s((128, 1), F32), s((128, C), BF16), s((128, C), BF...  1.95 us
  transfers between devices with their start and end apart: 3, of which 2 were waited for; matrix products, arithmetic and copies ran while one was open for 0% of the time, Pallas kernels for 4%

profile of v9, /device:TPU:1, one launch (start us, length us, event | category | flops | bytes accessed | tf_op | source)
XLA Modules:
  0.0 84.4 jit_solution(3900632811475459826)
XLA Ops:
  0.6 1.0 %shard_map.94 = (bf16[192,512]{1,0:T(8,128)(2,1)S(1)}, bf16[192,512]{1,0:T(8,128)(2,1)S(1)}) custom-call(s32[1,2]{1,0:T(1,128)} %gaps.3, bf16[128,512]{1,0:T(8,128)(2,1)} %bitcast.5, bf16[128,512]{1,0:T(8,128)(2,1)} %bitcast.7), custom_call_target="tpu_custom_call" | custom-call | tf_op jit(solution)/shard_map/pallas_call | solution.py:308
  1.7 1.3 %collective-permute-start = (bf16[192,512]{1,0:T(8,128)(2,1)S(1)}, bf16[192,512]{1,0:T(8,128)(2,1)S(1)}, u32[]{:S(2)}, u32[]{:S(2)}) collective-permute-start(bf16[192,512]{1,0:T(8,128)(2,1)S(1)} %get-tuple-element.21), channel_id=1, source_target_pairs={{4,0},{8,4},{12,8},{16,12},{20,16},{24,20},{28,24},{32,28},{36,32}... | collective-permute-start | bytes 589832 | tf_op jit(solution)/shard_map/ppermute | solution.py:309
  3.0 5.7 %collective-permute-start.1 = (bf16[192,512]{1,0:T(8,128)(2,1)S(1)}, bf16[192,512]{1,0:T(8,128)(2,1)S(1)}, u32[]{:S(2)}, u32[]{:S(2)}) collective-permute-start(bf16[192,512]{1,0:T(8,128)(2,1)S(1)} %get-tuple-element.22), channel_id=1, source_target_pairs={{0,4},{4,8},{8,12},{12,16},{16,20},{20,24},{24,28},{28,32},{32,36}... | collective-permute-start | bytes 589832 | tf_op jit(solution)/shard_map/ppermute | solution.py:310
  8.6 1.9 %shard_map.93 = (f32[128,1]{1,0:T(8,128)S(1)}, bf16[128,512]{1,0:T(8,128)(2,1)S(1)}, bf16[128,512]{1,0:T(8,128)(2,1)S(1)}, f32[3,2,512]{2,1,0:T(2,128)S(1)}, f32...) custom-call(s32[1,2]{1,0:T(1,128)} %gaps.3, bf16[128,512]{1,0:T(8,128)(2,1)} %bitcast.6, bf16[128,512]{1,0:T(8,128)(2,1)} %bitcast.8, ...), custom_call_target="tpu_custom_call" | custom-call | tf_op jit(solution)/shard_map/pallas_call | solution.py:313
  10.6 1.4 %collective-permute-done.nxt = bf16[192,512]{1,0:T(8,128)(2,1)S(1)} collective-permute-done((bf16[192,512]{1,0:T(8,128)(2,1)S(1)}, bf16[192,512]{1,0:T(8,128)(2,1)S(1)}, u32[]{:S(2)}, u32[]{:S(2)}) %collective-permute-start) | collective-permute-done | bytes 196640 | tf_op jit(solution)/shard_map/ppermute | solution.py:309
  12.0 0.0 collective-permute-done.1.prev
  12.0 3.9 %shard_map.95 = (bf16[128,512]{1,0:T(8,128)(2,1)}, bf16[144,1536]{1,0:T(8,128)(2,1)S(1)}, bf16[144,1536]{1,0:T(8,128)(2,1)S(1)}) custom-call(f32[128,1]{1,0:T(8,128)S(1)} %get-tuple-element.20.own_valid, bf16[192,512]{1,0:T(8,128)(2,1)S(1)} %collective-permute-done.nxt, bf16[192,512]{1,0:T(8,128)(2,1)S(1)} %collective-permute-done.1.prev, ...), custom_call_target="tpu_custom_call" | custom-call | tf_op jit(solution)/shard_map/pallas_call | solution.py:292
  15.9 11.6 %collective-permute-start.2 = (bf16[144,1536]{1,0:T(8,128)(2,1)S(1)}, bf16[144,1536]{1,0:T(8,128)(2,1)S(1)}, u32[]{:S(2)}, u32[]{:S(2)}) collective-permute-start(bf16[144,1536]{1,0:T(8,128)(2,1)S(1)} %get-tuple-element.30), channel_id=1, source_target_pairs={{0,1},{1,0},{2,3},{3,2},{4,5},{5,4},{6,7},{7,6},{8,9},{9,8},{10,11... | collective-permute-start | bytes 1327112 | tf_op jit(solution)/shard_map/ppermute | solution.py:320
  27.5 1.0 %shard_map.96 = (bf16[512,512]{1,0:T(8,128)(2,1)S(1)}, f32[512,1024]{1,0:T(8,128)S(1)}) custom-call(bf16[144,1536]{1,0:T(8,128)(2,1)S(1)} %get-tuple-element.29.keep), custom_call_target="tpu_custom_call" | custom-call | tf_op jit(solution)/shard_map/pallas_call | solution.py:321
  28.6 0.4 collective-permute-done.2.recv
  28.9 0.9 %shard_map.97 = bf16[8,528,128]{2,1,0:T(8,128)(2,1)S(1)} custom-call(bf16[144,1536]{1,0:T(8,128)(2,1)S(1)} %get-tuple-element.29.keep, bf16[144,1536]{1,0:T(8,128)(2,1)S(1)} %collective-permute-done.2.recv, bf16[512,512]{1,0:T(8,128)(2,1)S(1)} %get-tuple-element.31.pick, f32[512,1024]{1,0:T(8,128)S(1)} %get-tuple-element.32.mine), custom_call_target="tpu_custom_call" | custom-call | tf_op jit(solution)/shard_map/pallas_call | solution.py:322
  29.8 27.6 %all_to_all.15.recv = bf16[8,528,128]{2,1,0:T(8,128)(2,1)S(1)} all-to-all(bf16[8,528,128]{2,1,0:T(8,128)(2,1)S(1)} %shard_map.97), channel_id=1, replica_groups={{0,2,16,18,64,66,80,82},{4,6,20,22,68,70,84,86},{8,10,24,26,72,74,88,90..., dimensions={0} | all-to-all | bytes 2162688 | tf_op jit(solution)/shard_map/all_to_all | solution.py:323
  57.4 0.5 shard_map.98
  57.9 15.3 %all_to_all.16.recv = bf16[16,40,128]{2,1,0:T(8,128)(2,1)S(1)} all-to-all(bf16[16,40,128]{2,1,0:T(8,128)(2,1)S(1)} %shard_map.98), channel_id=1, replica_groups={{0,4,8,12,128,132,136,140,256,260,264,268,384,388,392,396},{32,36,40,44..., dimensions={0} | all-to-all | bytes 327680 | tf_op jit(solution)/shard_map/all_to_all | solution.py:325
  73.2 10.5 %all_to_all.17.recv = f32[8,24,128]{2,1,0:T(8,128)S(1)} all-to-all(f32[8,24,128]{2,1,0:T(8,128)S(1)} %shard_map.99), channel_id=1, replica_groups=mesh['z'=8,'xh'=2,'xl'=2,'yh'=4,'yl'=2,'c'=2] {'xh','yl','c'}, dimensions={0} | all-to-all | bytes 196608 | tf_op jit(solution)/shard_map/all_to_all | solution.py:327
  83.7 0.7 shard_map.100
  (1 shorter events, 0.0 us)
Async XLA Ops:
  1.7 10.4 %collective-permute-start = (bf16[192,512]{1,0:T(8,128)(2,1)S(1)}, bf16[192,512]{1,0:T(8,128)(2,1)S(1)}, u32[]{:S(2)}, u32[]{:S(2)}) collective-permute-start(bf16[192,512]{1,0:T(8,128)(2,1)S(1)} %get-tuple-element.21), channel_id=1, source_target_pairs={{4,0},{8,4},{12,8},{16,12},{20,16},{24,20},{28,24},{32,28},{36,32}... | collective-permute-start | bytes 589832 | tf_op jit(solution)/shard_map/ppermute | solution.py:309
  3.0 9.1 %collective-permute-start.1 = (bf16[192,512]{1,0:T(8,128)(2,1)S(1)}, bf16[192,512]{1,0:T(8,128)(2,1)S(1)}, u32[]{:S(2)}, u32[]{:S(2)}) collective-permute-start(bf16[192,512]{1,0:T(8,128)(2,1)S(1)} %get-tuple-element.22), channel_id=1, source_target_pairs={{0,4},{4,8},{8,12},{12,16},{16,20},{20,24},{24,28},{28,32},{32,36}... | collective-permute-start | bytes 589832 | tf_op jit(solution)/shard_map/ppermute | solution.py:310
  15.9 13.0 %collective-permute-start.2 = (bf16[144,1536]{1,0:T(8,128)(2,1)S(1)}, bf16[144,1536]{1,0:T(8,128)(2,1)S(1)}, u32[]{:S(2)}, u32[]{:S(2)}) collective-permute-start(bf16[144,1536]{1,0:T(8,128)(2,1)S(1)} %get-tuple-element.30), channel_id=1, source_target_pairs={{0,1},{1,0},{2,3},{3,2},{4,5},{5,4},{6,7},{7,6},{8,9},{9,8},{10,11... | collective-permute-start | bytes 1327112 | tf_op jit(solution)/shard_map/ppermute | solution.py:320

commit v10 on v8

--- a/solution.py
+++ b/solution.py
@@ -198,9 +198,9 @@
 
 
 def device(near, far, core):
-    z = ((far >> 3) * 2 + (near >> 2) + core) % 8
-    x = ((far >> 2) % 2 * 2 + (near >> 1) % 2 + core) % 4
-    y = (far % 4 * 2 + near % 2 + core) % 8
+    z = ((far >> 3) * 2 + (near >> 2)) * (1 - 2 * core) % 8
+    x = ((far >> 2) % 2 * 2 + (near >> 1) % 2) * (1 - 2 * core) % 4
+    y = (far % 4 * 2 + near % 2) * (1 - 2 * core) % 8
     return ((z * 4 + x) * 8 + y) * 2 + core
 
 
@@ -209,11 +209,11 @@
 
 
 def own_terms(keep, pick, mine):
-    core = lax.axis_index("c")
+    turn = 1 - 2 * lax.axis_index("c")
     q = lax.broadcasted_iota(jnp.int32, (C, 1), 0)
-    z = ((((q >> 5) & 1) << 2 | ((q >> 4) & 1) << 1 | ((q >> 8) & 1)) + core) & 7
-    x = ((((q >> 3) & 1) << 1 | ((q >> 7) & 1)) + core) & 3
-    y = ((((q >> 1) & 3) << 1 | ((q >> 6) & 1)) + core) & 7
+    z = ((((q >> 5) & 1) << 2 | ((q >> 4) & 1) << 1 | ((q >> 8) & 1)) * turn) & 7
+    x = ((((q >> 3) & 1) << 1 | ((q >> 7) & 1)) * turn) & 3
+    y = ((((q >> 1) & 3) << 1 | ((q >> 6) & 1)) * turn) & 7
     ch = z << 6 | x << 4 | y << 1 | (q & 1)
     pick[...] = (ch == lax.broadcasted_iota(jnp.int32, (C, C), 1)).astype(F32).astype(BF16)
     ha = dot(pick[...], keep[0:128, 0:C], ((1,), (1,))).astype(BF16)
@@ -251,7 +251,7 @@
     total = recv[0].astype(F32)
     for i in range(1, 16):
         total += recv[i].astype(F32)
-    swap = (lax.axis_index("c") == 1) & (lax.axis_index("xl") == 0)
+    swap = (lax.axis_index("c") == 1) & (lax.axis_index("xl") == 1)
     a, b = total[0:16, :], total[16:32, :]
     for i in range(8):
         piece = jnp.where(swap, b, a) if i < 4 else jnp.where(swap, a, b)

time: 85 us -> 85.4 us (level)
    all_to_all x1, blocking collectives: 11.8 us -> 7.38 us  [shards(): part = lax.all_to_all(part, LAST, 0, 0, tiled=True)]
    all_to_all x1, blocking collectives: 21.7 us -> 25.9 us  [shards(): part = lax.all_to_all(part, ALL, 0, 0, axis_index_groups=NEAR, tiled=True)]
where the time goes in v10:
time: 85.4 us; the launch traced here: 85.1 us
  blocking collectives  53.7 us (63%)
  waiting for transfers between devices  12 us (14%)
  Pallas kernels  9.91 us (12%)
  starting transfers between devices  8.84 us (10%)
    all_to_all x1, blocking collectives, shards(): part = lax.all_to_all(part, ALL, 0, 0, axis_index_groups=NEAR, tiled=True)  25.9 us
    all_to_all x1, blocking collectives, shards(): part = lax.all_to_all(part, ALL, 0, 0, axis_index_groups=FAR, tiled=True)  20.4 us
    ppermute x1, waiting for transfers between devices, shards(): nxt = lax.ppermute(down, SEQ, [(i + 1, i) for i in range(n - 1)])  11.6 us
    all_to_all x1, blocking collectives, shards(): part = lax.all_to_all(part, LAST, 0, 0, tiled=True)  7.38 us
    ppermute x1, starting transfers between devices, shards(): prev = lax.ppermute(up, SEQ, [(i, i + 1) for i in range(n - 1)])  5.05 us
    pallas_call x1, Pallas kernels, main(): call(body, 'vvvvvvvv', [s((128, C), BF16), s((ACT, 3 * C), BF16), s((ACT,...  3.87 us
    ppermute x1, starting transfers between devices, shards(): recv = lax.ppermute(send, 'c', [(0, 1), (1, 0)])  2.5 us
    pallas_call x1, Pallas kernels, shards(): call(warm, 'svvvvv', [s((128, 1), F32), s((128, C), BF16), s((128, C), BF...  1.95 us
  transfers between devices with their start and end apart: 3, of which 2 were waited for; matrix products, arithmetic and copies ran while one was open for 0% of the time, Pallas kernels for 4%

profile of v10, /device:TPU:1, one launch (start us, length us, event | category | flops | bytes accessed | tf_op | source)
XLA Modules:
  0.0 85.1 jit_solution(11039566177506171562)
XLA Ops:
  0.6 1.0 %shard_map.94 = (bf16[192,512]{1,0:T(8,128)(2,1)S(1)}, bf16[192,512]{1,0:T(8,128)(2,1)S(1)}) custom-call(s32[1,2]{1,0:T(1,128)} %gaps.3, bf16[128,512]{1,0:T(8,128)(2,1)} %bitcast.5, bf16[128,512]{1,0:T(8,128)(2,1)} %bitcast.7), custom_call_target="tpu_custom_call" | custom-call | tf_op jit(solution)/shard_map/pallas_call | solution.py:308
  1.7 5.1 %collective-permute-start = (bf16[192,512]{1,0:T(8,128)(2,1)S(1)}, bf16[192,512]{1,0:T(8,128)(2,1)S(1)}, u32[]{:S(2)}, u32[]{:S(2)}) collective-permute-start(bf16[192,512]{1,0:T(8,128)(2,1)S(1)} %get-tuple-element.21), channel_id=1, source_target_pairs={{0,4},{4,8},{8,12},{12,16},{16,20},{20,24},{24,28},{28,32},{32,36}... | collective-permute-start | bytes 589832 | tf_op jit(solution)/shard_map/ppermute | solution.py:309
  6.7 1.3 %collective-permute-start.1 = (bf16[192,512]{1,0:T(8,128)(2,1)S(1)}, bf16[192,512]{1,0:T(8,128)(2,1)S(1)}, u32[]{:S(2)}, u32[]{:S(2)}) collective-permute-start(bf16[192,512]{1,0:T(8,128)(2,1)S(1)} %get-tuple-element.22), channel_id=1, source_target_pairs={{4,0},{8,4},{12,8},{16,12},{20,16},{24,20},{28,24},{32,28},{36,32}... | collective-permute-start | bytes 589832 | tf_op jit(solution)/shard_map/ppermute | solution.py:310
  8.0 1.9 %shard_map.93 = (f32[128,1]{1,0:T(8,128)S(1)}, bf16[128,512]{1,0:T(8,128)(2,1)S(1)}, bf16[128,512]{1,0:T(8,128)(2,1)S(1)}, f32[3,2,512]{2,1,0:T(2,128)S(1)}, f32...) custom-call(s32[1,2]{1,0:T(1,128)} %gaps.3, bf16[128,512]{1,0:T(8,128)(2,1)} %bitcast.6, bf16[128,512]{1,0:T(8,128)(2,1)} %bitcast.8, ...), custom_call_target="tpu_custom_call" | custom-call | tf_op jit(solution)/shard_map/pallas_call | solution.py:313
  10.0 0.0 collective-permute-done.prev
  10.0 11.6 %collective-permute-done.1.nxt = bf16[192,512]{1,0:T(8,128)(2,1)S(1)} collective-permute-done((bf16[192,512]{1,0:T(8,128)(2,1)S(1)}, bf16[192,512]{1,0:T(8,128)(2,1)S(1)}, u32[]{:S(2)}, u32[]{:S(2)}) %collective-permute-start.1) | collective-permute-done | bytes 196640 | tf_op jit(solution)/shard_map/ppermute | solution.py:310
  21.6 3.9 %shard_map.95 = (bf16[128,512]{1,0:T(8,128)(2,1)}, bf16[144,1536]{1,0:T(8,128)(2,1)S(1)}, bf16[144,1536]{1,0:T(8,128)(2,1)S(1)}) custom-call(f32[128,1]{1,0:T(8,128)S(1)} %get-tuple-element.20.own_valid, bf16[192,512]{1,0:T(8,128)(2,1)S(1)} %collective-permute-done.prev, bf16[192,512]{1,0:T(8,128)(2,1)S(1)} %collective-permute-done.1.nxt, ...), custom_call_target="tpu_custom_call" | custom-call | tf_op jit(solution)/shard_map/pallas_call | solution.py:292
  25.5 2.5 %collective-permute-start.2 = (bf16[144,1536]{1,0:T(8,128)(2,1)S(1)}, bf16[144,1536]{1,0:T(8,128)(2,1)S(1)}, u32[]{:S(2)}, u32[]{:S(2)}) collective-permute-start(bf16[144,1536]{1,0:T(8,128)(2,1)S(1)} %get-tuple-element.30), channel_id=1, source_target_pairs={{0,1},{1,0},{2,3},{3,2},{4,5},{5,4},{6,7},{7,6},{8,9},{9,8},{10,11... | collective-permute-start | bytes 1327112 | tf_op jit(solution)/shard_map/ppermute | solution.py:320
  28.0 1.0 %shard_map.96 = (bf16[512,512]{1,0:T(8,128)(2,1)S(1)}, f32[512,1024]{1,0:T(8,128)S(1)}) custom-call(bf16[144,1536]{1,0:T(8,128)(2,1)S(1)} %get-tuple-element.29.keep), custom_call_target="tpu_custom_call" | custom-call | tf_op jit(solution)/shard_map/pallas_call | solution.py:321
  29.0 0.4 collective-permute-done.2.recv
  29.4 0.9 %shard_map.97 = bf16[8,528,128]{2,1,0:T(8,128)(2,1)S(1)} custom-call(bf16[144,1536]{1,0:T(8,128)(2,1)S(1)} %get-tuple-element.29.keep, bf16[144,1536]{1,0:T(8,128)(2,1)S(1)} %collective-permute-done.2.recv, bf16[512,512]{1,0:T(8,128)(2,1)S(1)} %get-tuple-element.31.pick, f32[512,1024]{1,0:T(8,128)S(1)} %get-tuple-element.32.mine), custom_call_target="tpu_custom_call" | custom-call | tf_op jit(solution)/shard_map/pallas_call | solution.py:322
  30.3 25.9 %all_to_all.15.recv = bf16[8,528,128]{2,1,0:T(8,128)(2,1)S(1)} all-to-all(bf16[8,528,128]{2,1,0:T(8,128)(2,1)S(1)} %shard_map.97), channel_id=1, replica_groups={{0,2,16,18,64,66,80,82},{4,6,20,22,68,70,84,86},{8,10,24,26,72,74,88,90..., dimensions={0} | all-to-all | bytes 2162688 | tf_op jit(solution)/shard_map/all_to_all | solution.py:323
  56.1 0.5 shard_map.98
  56.6 20.4 %all_to_all.16.recv = bf16[16,40,128]{2,1,0:T(8,128)(2,1)S(1)} all-to-all(bf16[16,40,128]{2,1,0:T(8,128)(2,1)S(1)} %shard_map.98), channel_id=1, replica_groups={{0,4,8,12,128,132,136,140,256,260,264,268,384,388,392,396},{32,36,40,44..., dimensions={0} | all-to-all | bytes 327680 | tf_op jit(solution)/shard_map/all_to_all | solution.py:325
  77.0 7.4 %all_to_all.17.recv = f32[8,24,128]{2,1,0:T(8,128)S(1)} all-to-all(f32[8,24,128]{2,1,0:T(8,128)S(1)} %shard_map.99), channel_id=1, replica_groups=mesh['z'=8,'xh'=2,'xl'=2,'yh'=4,'yl'=2,'c'=2] {'xh','yl','c'}, dimensions={0} | all-to-all | bytes 196608 | tf_op jit(solution)/shard_map/all_to_all | solution.py:327
  84.4 0.7 shard_map.100
  (1 shorter events, 0.0 us)
Async XLA Ops:
  1.7 8.3 %collective-permute-start = (bf16[192,512]{1,0:T(8,128)(2,1)S(1)}, bf16[192,512]{1,0:T(8,128)(2,1)S(1)}, u32[]{:S(2)}, u32[]{:S(2)}) collective-permute-start(bf16[192,512]{1,0:T(8,128)(2,1)S(1)} %get-tuple-element.21), channel_id=1, source_target_pairs={{0,4},{4,8},{8,12},{12,16},{16,20},{20,24},{24,28},{28,32},{32,36}... | collective-permute-start | bytes 589832 | tf_op jit(solution)/shard_map/ppermute | solution.py:309
  6.7 14.9 %collective-permute-start.1 = (bf16[192,512]{1,0:T(8,128)(2,1)S(1)}, bf16[192,512]{1,0:T(8,128)(2,1)S(1)}, u32[]{:S(2)}, u32[]{:S(2)}) collective-permute-start(bf16[192,512]{1,0:T(8,128)(2,1)S(1)} %get-tuple-element.22), channel_id=1, source_target_pairs={{4,0},{8,4},{12,8},{16,12},{20,16},{24,20},{28,24},{32,28},{36,32}... | collective-permute-start | bytes 589832 | tf_op jit(solution)/shard_map/ppermute | solution.py:310
  25.5 3.9 %collective-permute-start.2 = (bf16[144,1536]{1,0:T(8,128)(2,1)S(1)}, bf16[144,1536]{1,0:T(8,128)(2,1)S(1)}, u32[]{:S(2)}, u32[]{:S(2)}) collective-permute-start(bf16[144,1536]{1,0:T(8,128)(2,1)S(1)} %get-tuple-element.30), channel_id=1, source_target_pairs={{0,1},{1,0},{2,3},{3,2},{4,5},{5,4},{6,7},{7,6},{8,9},{9,8},{10,11... | collective-permute-start | bytes 1327112 | tf_op jit(solution)/shard_map/ppermute | solution.py:320

commit v11 on v10

--- a/solution.py
+++ b/solution.py
@@ -48,7 +48,7 @@
     return hi, lo
 
 
-def pack(gaps, tok, cot, up, down):
+def pack(gaps, tok, cot, down, up):
     at = lax.broadcasted_iota(jnp.int32, (128, 1), 0)
     inside = (at >= gaps[0, 0]) & (at < gaps[0, 1])
     marked = jnp.where(inside, MARK, tok[...].astype(F32)).astype(BF16)
@@ -65,7 +65,7 @@
         b[...] = a[...]
 
 
-def body(own_valid, prev, nxt, tok, cot, taps, gains, proj, out, keep, send,
+def body(own_valid, nxt, prev, tok, cot, taps, gains, proj, out, keep, send,
          n0, i0, g0, h0, ab0, x1, n1, i1, g1, h1, po1, dp1, dh1, gr1, dp0, dh0, act):
     core = lax.axis_index("c")
     place_in_seq = sum(lax.axis_index(a) for a in SEQ)
@@ -305,7 +305,7 @@
     n = 128
     s = jax.ShapeDtypeStruct
     far = [pltpu.with_memory_space_constraint(a, pltpu.HBM) for a in (gaps, tok, cot)]
-    up, down = call(pack, "svv", [s((192, C), BF16), s((192, C), BF16)], mib=48)(*far)
+    down, up = call(pack, "svv", [s((192, C), BF16), s((192, C), BF16)], mib=48)(*far)
     prev = lax.ppermute(up, SEQ, [(i, i + 1) for i in range(n - 1)])
     nxt = lax.ppermute(down, SEQ, [(i + 1, i) for i in range(n - 1)])
     here = [jnp.transpose(taps, (1, 0, 2)), gains, proj]
@@ -316,7 +316,7 @@
         [s((128, 1), F32), s((128, C), BF16), s((128, C), BF16), s((3, 2, C), F32), s((2, C), F32),
          s((2, C, 2 * C), BF16)],
     )(*here)
-    tokens_grad, keep, send = main(near_args[0], prev, nxt, *near_args[1:])
+    tokens_grad, keep, send = main(near_args[0], nxt, prev, *near_args[1:])
     recv = lax.ppermute(send, "c", [(0, 1), (1, 0)])
     pick, mine = call(own_terms, "v", [s((C, C), BF16), s((C, 2 * C), F32)])(keep)
     part = call(terms, "vvvv", s((8, 528, 128), BF16))(keep, recv, pick, mine)

time: 85.4 us -> 84.7 us (level)
  waiting for transfers between devices: 12 us -> 1.79 us
  starting transfers between devices: 8.84 us -> 18.6 us
    ppermute x1, waiting for transfers between devices: 11.6 us -> 1.43 us  [shards(): nxt = lax.ppermute(down, SEQ, [(i + 1, i) for i in range(n - 1)])]
    ppermute x1, starting transfers between devices: 2.5 us -> 11.6 us  [shards(): recv = lax.ppermute(send, 'c', [(0, 1), (1, 0)])]
    all_to_all x1, blocking collectives: 20.4 us -> 15.2 us  [shards(): part = lax.all_to_all(part, ALL, 0, 0, axis_index_groups=FAR, tiled=True)]
    all_to_all x1, blocking collectives: 25.9 us -> 29.7 us  [shards(): part = lax.all_to_all(part, ALL, 0, 0, axis_index_groups=NEAR, tiled=True)]
    all_to_all x1, blocking collectives: 7.38 us -> 8.54 us  [shards(): part = lax.all_to_all(part, LAST, 0, 0, tiled=True)]
where the time goes in v11:
time: 84.7 us; the launch traced here: 84.4 us
  blocking collectives  53.4 us (63%)
  starting transfers between devices  18.6 us (22%)
  Pallas kernels  9.93 us (12%)
  waiting for transfers between devices  1.79 us (2%)
    all_to_all x1, blocking collectives, shards(): part = lax.all_to_all(part, ALL, 0, 0, axis_index_groups=NEAR, tiled=True)  29.7 us
    all_to_all x1, blocking collectives, shards(): part = lax.all_to_all(part, ALL, 0, 0, axis_index_groups=FAR, tiled=True)  15.2 us
    ppermute x1, starting transfers between devices, shards(): recv = lax.ppermute(send, 'c', [(0, 1), (1, 0)])  11.6 us
    all_to_all x1, blocking collectives, shards(): part = lax.all_to_all(part, LAST, 0, 0, tiled=True)  8.54 us
    ppermute x1, starting transfers between devices, shards(): prev = lax.ppermute(up, SEQ, [(i, i + 1) for i in range(n - 1)])  5.68 us
    pallas_call x1, Pallas kernels, main(): call(body, 'vvvvvvvv', [s((128, C), BF16), s((ACT, 3 * C), BF16), s((ACT,...  3.89 us
    pallas_call x1, Pallas kernels, shards(): call(warm, 'svvvvv', [s((128, 1), F32), s((128, C), BF16), s((128, C), BF...  1.95 us
  transfers between devices with their start and end apart: 3, of which 2 were waited for; matrix products, arithmetic and copies ran while one was open for 0% of the time, Pallas kernels for 4%

profile of v11, /device:TPU:1, one launch (start us, length us, event | category | flops | bytes accessed | tf_op | source)
XLA Modules:
  0.0 84.4 jit_solution(12750158373064393337)
XLA Ops:
  0.6 1.0 %shard_map.94 = (bf16[192,512]{1,0:T(8,128)(2,1)S(1)}, bf16[192,512]{1,0:T(8,128)(2,1)S(1)}) custom-call(s32[1,2]{1,0:T(1,128)} %gaps.3, bf16[128,512]{1,0:T(8,128)(2,1)} %bitcast.5, bf16[128,512]{1,0:T(8,128)(2,1)} %bitcast.7), custom_call_target="tpu_custom_call" | custom-call | tf_op jit(solution)/shard_map/pallas_call | solution.py:308
  1.7 1.3 %collective-permute-start = (bf16[192,512]{1,0:T(8,128)(2,1)S(1)}, bf16[192,512]{1,0:T(8,128)(2,1)S(1)}, u32[]{:S(2)}, u32[]{:S(2)}) collective-permute-start(bf16[192,512]{1,0:T(8,128)(2,1)S(1)} %get-tuple-element.21), channel_id=1, source_target_pairs={{4,0},{8,4},{12,8},{16,12},{20,16},{24,20},{28,24},{32,28},{36,32}... | collective-permute-start | bytes 589832 | tf_op jit(solution)/shard_map/ppermute | solution.py:310
  3.0 5.7 %collective-permute-start.1 = (bf16[192,512]{1,0:T(8,128)(2,1)S(1)}, bf16[192,512]{1,0:T(8,128)(2,1)S(1)}, u32[]{:S(2)}, u32[]{:S(2)}) collective-permute-start(bf16[192,512]{1,0:T(8,128)(2,1)S(1)} %get-tuple-element.22), channel_id=1, source_target_pairs={{0,4},{4,8},{8,12},{12,16},{16,20},{20,24},{24,28},{28,32},{32,36}... | collective-permute-start | bytes 589832 | tf_op jit(solution)/shard_map/ppermute | solution.py:309
  8.6 1.9 %shard_map.93 = (f32[128,1]{1,0:T(8,128)S(1)}, bf16[128,512]{1,0:T(8,128)(2,1)S(1)}, bf16[128,512]{1,0:T(8,128)(2,1)S(1)}, f32[3,2,512]{2,1,0:T(2,128)S(1)}, f32...) custom-call(s32[1,2]{1,0:T(1,128)} %gaps.3, bf16[128,512]{1,0:T(8,128)(2,1)} %bitcast.6, bf16[128,512]{1,0:T(8,128)(2,1)} %bitcast.8, ...), custom_call_target="tpu_custom_call" | custom-call | tf_op jit(solution)/shard_map/pallas_call | solution.py:313
  10.6 1.4 %collective-permute-done.nxt = bf16[192,512]{1,0:T(8,128)(2,1)S(1)} collective-permute-done((bf16[192,512]{1,0:T(8,128)(2,1)S(1)}, bf16[192,512]{1,0:T(8,128)(2,1)S(1)}, u32[]{:S(2)}, u32[]{:S(2)}) %collective-permute-start) | collective-permute-done | bytes 196640 | tf_op jit(solution)/shard_map/ppermute | solution.py:310
  12.0 0.0 collective-permute-done.1.prev
  12.0 3.9 %shard_map.95 = (bf16[128,512]{1,0:T(8,128)(2,1)}, bf16[144,1536]{1,0:T(8,128)(2,1)S(1)}, bf16[144,1536]{1,0:T(8,128)(2,1)S(1)}) custom-call(f32[128,1]{1,0:T(8,128)S(1)} %get-tuple-element.20.own_valid, bf16[192,512]{1,0:T(8,128)(2,1)S(1)} %collective-permute-done.nxt, bf16[192,512]{1,0:T(8,128)(2,1)S(1)} %collective-permute-done.1.prev, ...), custom_call_target="tpu_custom_call" | custom-call | tf_op jit(solution)/shard_map/pallas_call | solution.py:292
  15.9 11.6 %collective-permute-start.2 = (bf16[144,1536]{1,0:T(8,128)(2,1)S(1)}, bf16[144,1536]{1,0:T(8,128)(2,1)S(1)}, u32[]{:S(2)}, u32[]{:S(2)}) collective-permute-start(bf16[144,1536]{1,0:T(8,128)(2,1)S(1)} %get-tuple-element.30), channel_id=1, source_target_pairs={{0,1},{1,0},{2,3},{3,2},{4,5},{5,4},{6,7},{7,6},{8,9},{9,8},{10,11... | collective-permute-start | bytes 1327112 | tf_op jit(solution)/shard_map/ppermute | solution.py:320
  27.5 1.0 %shard_map.96 = (bf16[512,512]{1,0:T(8,128)(2,1)S(1)}, f32[512,1024]{1,0:T(8,128)S(1)}) custom-call(bf16[144,1536]{1,0:T(8,128)(2,1)S(1)} %get-tuple-element.29.keep), custom_call_target="tpu_custom_call" | custom-call | tf_op jit(solution)/shard_map/pallas_call | solution.py:321
  28.6 0.4 collective-permute-done.2.recv
  28.9 0.9 %shard_map.97 = bf16[8,528,128]{2,1,0:T(8,128)(2,1)S(1)} custom-call(bf16[144,1536]{1,0:T(8,128)(2,1)S(1)} %get-tuple-element.29.keep, bf16[144,1536]{1,0:T(8,128)(2,1)S(1)} %collective-permute-done.2.recv, bf16[512,512]{1,0:T(8,128)(2,1)S(1)} %get-tuple-element.31.pick, f32[512,1024]{1,0:T(8,128)S(1)} %get-tuple-element.32.mine), custom_call_target="tpu_custom_call" | custom-call | tf_op jit(solution)/shard_map/pallas_call | solution.py:322
  29.8 29.7 %all_to_all.15.recv = bf16[8,528,128]{2,1,0:T(8,128)(2,1)S(1)} all-to-all(bf16[8,528,128]{2,1,0:T(8,128)(2,1)S(1)} %shard_map.97), channel_id=1, replica_groups={{0,2,16,18,64,66,80,82},{4,6,20,22,68,70,84,86},{8,10,24,26,72,74,88,90..., dimensions={0} | all-to-all | bytes 2162688 | tf_op jit(solution)/shard_map/all_to_all | solution.py:323
  59.5 0.5 shard_map.98
  60.0 15.2 %all_to_all.16.recv = bf16[16,40,128]{2,1,0:T(8,128)(2,1)S(1)} all-to-all(bf16[16,40,128]{2,1,0:T(8,128)(2,1)S(1)} %shard_map.98), channel_id=1, replica_groups={{0,4,8,12,128,132,136,140,256,260,264,268,384,388,392,396},{32,36,40,44..., dimensions={0} | all-to-all | bytes 327680 | tf_op jit(solution)/shard_map/all_to_all | solution.py:325
  75.2 8.5 %all_to_all.17.recv = f32[8,24,128]{2,1,0:T(8,128)S(1)} all-to-all(f32[8,24,128]{2,1,0:T(8,128)S(1)} %shard_map.99), channel_id=1, replica_groups=mesh['z'=8,'xh'=2,'xl'=2,'yh'=4,'yl'=2,'c'=2] {'xh','yl','c'}, dimensions={0} | all-to-all | bytes 196608 | tf_op jit(solution)/shard_map/all_to_all | solution.py:327
  83.7 0.7 shard_map.100
  (1 shorter events, 0.0 us)
Async XLA Ops:
  1.7 10.4 %collective-permute-start = (bf16[192,512]{1,0:T(8,128)(2,1)S(1)}, bf16[192,512]{1,0:T(8,128)(2,1)S(1)}, u32[]{:S(2)}, u32[]{:S(2)}) collective-permute-start(bf16[192,512]{1,0:T(8,128)(2,1)S(1)} %get-tuple-element.21), channel_id=1, source_target_pairs={{4,0},{8,4},{12,8},{16,12},{20,16},{24,20},{28,24},{32,28},{36,32}... | collective-permute-start | bytes 589832 | tf_op jit(solution)/shard_map/ppermute | solution.py:310
  3.0 9.1 %collective-permute-start.1 = (bf16[192,512]{1,0:T(8,128)(2,1)S(1)}, bf16[192,512]{1,0:T(8,128)(2,1)S(1)}, u32[]{:S(2)}, u32[]{:S(2)}) collective-permute-start(bf16[192,512]{1,0:T(8,128)(2,1)S(1)} %get-tuple-element.22), channel_id=1, source_target_pairs={{0,4},{4,8},{8,12},{12,16},{16,20},{20,24},{24,28},{28,32},{32,36}... | collective-permute-start | bytes 589832 | tf_op jit(solution)/shard_map/ppermute | solution.py:309
  15.9 13.0 %collective-permute-start.2 = (bf16[144,1536]{1,0:T(8,128)(2,1)S(1)}, bf16[144,1536]{1,0:T(8,128)(2,1)S(1)}, u32[]{:S(2)}, u32[]{:S(2)}) collective-permute-start(bf16[144,1536]{1,0:T(8,128)(2,1)S(1)} %get-tuple-element.30), channel_id=1, source_target_pairs={{0,1},{1,0},{2,3},{3,2},{4,5},{5,4},{6,7},{7,6},{8,9},{9,8},{10,11... | collective-permute-start | bytes 1327112 | tf_op jit(solution)/shard_map/ppermute | solution.py:320
